TPU v7x, 32 devices: a whole 2x2x4 slice. The times are simulated.
32 devices in a mesh: fsdp: 4 (over y, x), context: 2 (over core), tensor: 4 (over z).
Axes of the slice: x: 2, y: 2, z: 4, core: 2. Of those that a mesh axis runs over, the one named last changes fastest.
Arguments:
- inputs: bfloat16 [4, 1024, 2048], P('fsdp', 'context'), may hold values from -6 to 6
- lengths: int32 [4], P('fsdp'), may hold values from 256 to 1024, as said below
- norm_attn: bfloat16 [2048], P('fsdp'), may hold values from 0.099609375 to 1.8984375
- w_query: bfloat16 [2048, 2048], P('fsdp', 'tensor'), may hold values from -0.125 to 0.125
- w_key: bfloat16 [2048, 2048], P('fsdp', 'tensor'), may hold values from -0.125 to 0.125
- w_value: bfloat16 [2048, 4096], P('fsdp', 'tensor'), may hold values from -0.125 to 0.125
- w_decay: bfloat16 [2048, 16], P('fsdp', 'tensor'), may hold values from -0.25 to 0.25
- w_strength: bfloat16 [2048, 16], P('fsdp', 'tensor'), may hold values from -0.125 to 0.125
- decay_log: bfloat16 [16], P('tensor'), may hold values from -1.5 to 1
- decay_bias: bfloat16 [16], P('tensor'), may hold values from -9 to -2
- conv_query: bfloat16 [16, 4, 128], P('tensor', None, 'fsdp'), may hold values from -3 to 3
- conv_key: bfloat16 [16, 4, 128], P('tensor', None, 'fsdp'), may hold values from -3 to 3
- conv_value: bfloat16 [16, 4, 256], P('tensor', None, 'fsdp'), may hold values from -3 to 3
- w_outgate: bfloat16 [2048, 4096], P('fsdp', 'tensor'), may hold values from -0.125 to 0.125
- norm_head: bfloat16 [256], P('fsdp'), may hold values from 0.099609375 to 1.8984375
- w_out: bfloat16 [4096, 2048], P('tensor', 'fsdp'), may hold values from -0.125 to 0.125
- norm_mlp: bfloat16 [2048], P('fsdp'), may hold values from 0.099609375 to 1.8984375
- w_gate: bfloat16 [2048, 5632], P('fsdp', 'tensor'), may hold values from -0.125 to 0.125
- w_up: bfloat16 [2048, 5632], P('fsdp', 'tensor'), may hold values from -0.125 to 0.125
- w_down: bfloat16 [5632, 2048], P('tensor', 'fsdp'), may hold values from -0.109375 to 0.109375
- cotangent: bfloat16 [4, 1024, 2048], P('fsdp', 'context'), may hold values from -6 to 6
Outputs:
- output: bfloat16 [4, 1024, 2048], P('fsdp', 'context')
- input_grad: bfloat16 [4, 1024, 2048], P('fsdp', 'context')
- grad_norm_attn: float32 [2048], P('fsdp')
- grad_w_query: float32 [2048, 2048], P('fsdp', 'tensor')
- grad_w_key: float32 [2048, 2048], P('fsdp', 'tensor')
- grad_w_value: float32 [2048, 4096], P('fsdp', 'tensor')
- grad_w_decay: float32 [2048, 16], P('fsdp', 'tensor')
- grad_w_strength: float32 [2048, 16], P('fsdp', 'tensor')
- grad_decay_log: float32 [16], P('tensor')
- grad_decay_bias: float32 [16], P('tensor')
- grad_conv_query: float32 [16, 4, 128], P('tensor', None, 'fsdp')
- grad_conv_key: float32 [16, 4, 128], P('tensor', None, 'fsdp')
- grad_conv_value: float32 [16, 4, 256], P('tensor', None, 'fsdp')
- grad_w_outgate: float32 [2048, 4096], P('fsdp', 'tensor')
- grad_norm_head: float32 [256], P('fsdp')
- grad_w_out: float32 [4096, 2048], P('tensor', 'fsdp')
- grad_norm_mlp: float32 [2048], P('fsdp')
- grad_w_gate: float32 [2048, 5632], P('fsdp', 'tensor')
- grad_w_up: float32 [2048, 5632], P('fsdp', 'tensor')
- grad_w_down: float32 [5632, 2048], P('tensor', 'fsdp')
Inputs may be any that keep to these rules, and one draw needn't show every extreme that they name: Slot s holds one sequence that fills its first lengths[s] positions; the rest of the slot is padding. In every draw at least one slot is full (1024 positions).
All inputs are finite; a program needn't handle non-finite values.
Results may differ from a plain program's by a relative error of at most 0.033.
Values may be sent and summed in bfloat16 or wider, within the bound.
No kernel may reach another device: no remote copies, remote signals or barrier semaphores. Data moves between devices by JAX's collectives and lax.ppermute only.
A program may use at most 256 MiB of HBM per device.

v0:
```python
import functools
import jax
import jax.numpy as jnp
from jax import lax
from jax.experimental import pallas as pl
from jax.experimental.pallas import tpu as pltpu
from jax.sharding import PartitionSpec as P

F32 = jnp.float32
BF16 = jnp.bfloat16
CHUNK = 128
exact = lax.Precision.HIGHEST
NN = ((1,), (0,))
NT = ((1,), (1,))
TN = ((0,), (0,))


def mm(a, b, dims=NN):
    return lax.dot_general(
        a.astype(BF16), b.astype(BF16), (dims, ((), ())), preferred_element_type=F32
    )


def mm_exact(a, b, dims=NN):
    return lax.dot_general(a, b, (dims, ((), ())), precision=exact, preferred_element_type=F32)


def grid_ids(size):
    rows = lax.broadcasted_iota(jnp.int32, (size, size), 0)
    cols = lax.broadcasted_iota(jnp.int32, (size, size), 1)
    return rows, cols


def softplus(v):
    return jnp.maximum(v, 0.0) + jnp.log1p(jnp.exp(-jnp.abs(v)))


def rates_of(rates, params, heads, triangle):
    lanes = lax.broadcasted_iota(jnp.int32, rates.shape, 1)
    shifted = rates + params[1:2, :]
    scale = jnp.exp(params[0:1, :])
    logdecay = jnp.where(lanes < heads, -scale * softplus(shifted), 0.0)
    running = mm_exact(triangle, logdecay)
    last = running[CHUNK - 1 : CHUNK, :]
    return (
        jax.nn.sigmoid(rates),
        shifted,
        scale,
        logdecay,
        running,
        jnp.transpose(running),
        jnp.exp(running),
        jnp.exp(last - running),
        jnp.exp(last),
    )


def inverse_of(system, rows, cols):
    eye = (rows == cols).astype(F32)
    size = 8
    near = jnp.where(rows // size == cols // size, system, 0.0)
    second = mm(near, near)
    third = mm(second, near)
    fourth = mm(second, second)
    partial = eye - near + second - third
    result = partial + mm(partial, fourth)
    while size < CHUNK:
        off = jnp.where(
            (rows // (2 * size) == cols // (2 * size)) & (rows // size > cols // size), system, 0.0
        )
        result = result - mm(mm(result, off), result)
        size *= 2
    return result


def refined(system, first, rows, cols):
    eye = (rows == cols).astype(F32)
    high = system.astype(BF16)
    low = system - high.astype(F32)
    first_high = first.astype(BF16)
    first_low = first - first_high.astype(F32)
    product = first + mm(high, first_high) + mm(low, first_high) + mm(high, first_low)
    return first + mm(first, eye - product)


def convolved(window, taps, rows):
    total = taps[0:1, :] * window[5 : 5 + rows, :]
    for j in range(1, 4):
        total = total + taps[j : j + 1, :] * window[5 + j : 5 + j + rows, :]
    return total


def forward_kernel(
    heads, key_dim, val_dim, order_ref, pre_ref, taps_ref, params_ref,
    mixed_ref, states_ref, inverse_ref, new_ref, state, window,
):
    step = pl.program_id(0)
    wide = heads * key_dim

    @pl.when(step == 0)
    def _():
        state[...] = jnp.zeros_like(state)
        window[0:8, :] = jnp.zeros((8, window.shape[1]), F32)

    width = window.shape[1]
    current = pre_ref[:, :width].astype(BF16).astype(F32)
    window[8 : 8 + CHUNK, :] = current
    summed = convolved(window, taps_ref, CHUNK)
    window[0:8, :] = current[CHUNK - 8 :, :]
    active = summed * jax.nn.sigmoid(summed)
    rows, cols = grid_ids(CHUNK)
    causal = rows >= cols
    strict = rows > cols
    strengths, _, _, _, running, running_t, decays, remains, whole = rates_of(
        pre_ref[:, width:], params_ref, heads, causal.astype(F32)
    )
    for h in range(heads):
        q_act = active[:, h * key_dim : (h + 1) * key_dim]
        k_act = active[:, wide + h * key_dim : wide + (h + 1) * key_dim]
        values = active[:, 2 * wide + h * val_dim : 2 * wide + (h + 1) * val_dim]
        query = q_act * (
            lax.rsqrt(jnp.sum(q_act * q_act, -1, keepdims=True) + 1e-6) * key_dim ** -0.5
        )
        keys = k_act * lax.rsqrt(jnp.sum(k_act * k_act, -1, keepdims=True) + 1e-6)
        beta = strengths[:, heads + h : heads + h + 1]
        spread = running[:, h : h + 1] - running_t[h : h + 1, :]
        ratios = jnp.where(causal, jnp.exp(jnp.where(causal, spread, 0.0)), 0.0)
        decay = decays[:, h : h + 1]
        dots = mm(jnp.concatenate([keys, query], 0), keys, NT)
        system = jnp.where(strict, beta * dots[:CHUNK] * ratios, 0.0)
        scores = dots[CHUNK:] * ratios
        inverse = refined(system, inverse_of(system, rows, cols), rows, cols)
        solved = mm(inverse, jnp.concatenate([(beta * decay) * keys, beta * values], 1))
        begin = state[h * key_dim : (h + 1) * key_dim, :]
        begin_low = begin.astype(BF16)
        through = mm(jnp.concatenate([solved[:, :key_dim], query * decay], 0), begin_low)
        new = (solved[:, key_dim:] - through[:CHUNK]).astype(BF16)
        mixed_ref[:, h * val_dim : (h + 1) * val_dim] = through[CHUNK:] + mm(scores, new)
        state[h * key_dim : (h + 1) * key_dim, :] = whole[:, h : h + 1] * begin + mm(
            keys * remains[:, h : h + 1], new, TN
        )
        states_ref[h * key_dim : (h + 1) * key_dim, :] = begin_low
        inverse_ref[h * CHUNK : (h + 1) * CHUNK, :] = inverse.astype(BF16)
        new_ref[:, h * val_dim : (h + 1) * val_dim] = new


def backward_kernel(
    heads, key_dim, val_dim, order_ref, pre_ref, before_ref, taps_ref, params_ref,
    states_ref, inverse_ref, new_ref, mixed_ref, gates_ref, d_own_ref, d_other_ref, side_ref,
    gain_ref,
    d_pre_ref, d_taps_ref, d_params_ref, d_gain_ref,
    d_state, window, after,
):
    step = pl.program_id(0)
    chunks = pl.num_programs(0)
    wide = heads * key_dim

    @pl.when(step == 0)
    def _():
        d_state[...] = jnp.zeros_like(d_state)
        after[CHUNK : CHUNK + 8, :] = jnp.zeros((8, after.shape[1]), F32)
        d_taps_ref[...] = jnp.zeros_like(d_taps_ref)
        d_params_ref[...] = jnp.zeros_like(d_params_ref)
        d_gain_ref[...] = jnp.zeros_like(d_gain_ref)

    width = window.shape[1]
    window[8 : 8 + CHUNK, :] = pre_ref[:, :width].astype(BF16).astype(F32)
    before = before_ref[:, :width].astype(BF16).astype(F32)
    window[0:8, :] = jnp.where(step == chunks - 1, 0.0, before)
    summed = convolved(window, taps_ref, CHUNK)
    sigma = jax.nn.sigmoid(summed)
    active = summed * sigma
    slope = sigma * (1.0 + summed * (1.0 - sigma))
    rows, cols = grid_ids(CHUNK)
    causal = rows >= cols
    strict = rows > cols
    strengths, shifted, scale, logdecay, running, running_t, decays, remains, whole = rates_of(
        pre_ref[:, width:], params_ref, heads, causal.astype(F32)
    )
    lanes = lax.broadcasted_iota(jnp.int32, (CHUNK, 128), 1)
    row_ids = lax.broadcasted_iota(jnp.int32, (CHUNK, 1), 0)
    d_attn = jnp.where(
        order_ref[chunks - 1 - step] < chunks // 2, d_own_ref[...], d_other_ref[...]
    )
    depth = side_ref.shape[2]
    d_heads = mm(d_attn[:, :depth], side_ref[0, 1])
    for f in range(1, side_ref.shape[0]):
        d_heads = d_heads + mm(d_attn[:, f * depth : (f + 1) * depth], side_ref[f, 1])
    d_running = jnp.zeros((CHUNK, 128), F32)
    d_strengths = jnp.zeros((CHUNK, 128), F32)
    for h in range(heads):
        q_at = slice(h * key_dim, (h + 1) * key_dim)
        k_at = slice(wide + h * key_dim, wide + (h + 1) * key_dim)
        v_at = slice(2 * wide + h * val_dim, 2 * wide + (h + 1) * val_dim)
        o_at = slice(h * val_dim, (h + 1) * val_dim)
        s_at = slice(h * key_dim, (h + 1) * key_dim)
        q_act = active[:, q_at]
        k_act = active[:, k_at]
        values = active[:, v_at]
        q_scale = lax.rsqrt(jnp.sum(q_act * q_act, -1, keepdims=True) + 1e-6)
        k_scale = lax.rsqrt(jnp.sum(k_act * k_act, -1, keepdims=True) + 1e-6)
        q_unit = q_act * q_scale
        keys = k_act * k_scale
        query = q_unit * key_dim ** -0.5
        mixed = mixed_ref[:, o_at]
        gates = gates_ref[:, o_at]
        d_out = d_heads[:, o_at]
        gain = gain_ref[...]
        m_scale = lax.rsqrt(jnp.mean(mixed * mixed, -1, keepdims=True) + 1e-5)
        unit = mixed * m_scale
        g_sigma = jax.nn.sigmoid(gates)
        gated = gates * g_sigma
        weighted = d_out * unit
        d_pre_ref[:, width + 128 + h * val_dim : width + 128 + (h + 1) * val_dim] = (
            weighted * gain * (g_sigma * (1.0 + gates * (1.0 - g_sigma)))
        ).astype(BF16)
        d_gain_ref[0:1, :] += jnp.sum(weighted * gated, 0, keepdims=True)
        d_unit = d_out * gated * gain
        d_mixed = (m_scale * (d_unit - unit * jnp.mean(d_unit * unit, -1, keepdims=True))).astype(
            BF16
        )
        beta = strengths[:, heads + h : heads + h + 1]
        spread = running[:, h : h + 1] - running_t[h : h + 1, :]
        ratios = jnp.where(causal, jnp.exp(jnp.where(causal, spread, 0.0)), 0.0)
        decay = decays[:, h : h + 1]
        remain = remains[:, h : h + 1]
        keys_low = keys.astype(BF16)
        query_low = query.astype(BF16)
        dots = mm(jnp.concatenate([keys_low, query_low], 0), keys_low, NT)
        weights = jnp.where(strict, dots[:CHUNK] * ratios, 0.0)
        scores = dots[CHUNK:] * ratios
        begin = states_ref[s_at, :]
        inverse = inverse_ref[h * CHUNK : (h + 1) * CHUNK, :]
        new = new_ref[:, o_at]
        d_end = d_state[s_at, :]
        d_end_low = d_end.astype(BF16)
        kept = (keys * remain).astype(BF16)
        d_new = mm(scores, d_mixed, TN) + mm(kept, d_end_low)
        solved = mm(inverse, d_new, TN)
        solved_low = solved.astype(BF16)
        pair = jnp.concatenate([d_mixed, solved_low], 0)
        outer = mm(pair, jnp.concatenate([begin, new], 0), NT)
        d_query_state = outer[:CHUNK, :key_dim]
        d_keys_state = outer[CHUNK:, :key_dim]
        d_scores = jnp.where(causal, outer[:CHUNK, key_dim:], 0.0)
        d_system = jnp.where(strict, -outer[CHUNK:, key_dim:], 0.0)
        d_kept = mm(new, d_end_low, NT)
        lead = beta * decay
        d_begin = whole[:, h : h + 1] * d_end + mm(
            jnp.concatenate([query * decay, -lead * keys], 0), pair, TN
        )
        d_state[s_at, :] = d_begin
        d_dots_k = d_system * (beta * ratios)
        d_dots_q = d_scores * ratios
        near = mm(
            jnp.concatenate([d_dots_q, d_dots_k + jnp.transpose(d_dots_k)], 0), keys_low
        )
        d_query = decay * d_query_state + near[:CHUNK]
        d_keys = (
            near[CHUNK:] + mm(d_dots_q, query_low, TN) - lead * d_keys_state + remain * d_kept
        )
        along = decay * jnp.sum(keys * d_keys_state, -1, keepdims=True)
        weighed = d_system * weights
        d_beta = (
            jnp.sum(solved * values, -1, keepdims=True)
            - along
            + jnp.sum(weighed, -1, keepdims=True)
        )
        joint = weighed * beta + d_scores * scores
        left = remain * jnp.sum(keys * d_kept, -1, keepdims=True)
        total = jnp.sum(left, 0, keepdims=True) + whole[:, h : h + 1] * jnp.sum(
            jnp.sum(d_end * begin.astype(F32), -1, keepdims=True), 0, keepdims=True
        )
        d_run = (
            jnp.sum(joint, -1, keepdims=True)
            - jnp.sum(jnp.transpose(joint), -1, keepdims=True)
            + decay * jnp.sum(query * d_query_state, -1, keepdims=True)
            - beta * along
            - left
            + jnp.where(row_ids == CHUNK - 1, total, 0.0)
        )
        d_running = jnp.where(lanes == h, d_run, d_running)
        d_strengths = jnp.where(lanes == heads + h, d_beta, d_strengths)
        d_q = d_query * key_dim ** -0.5
        d_q = q_scale * (d_q - q_unit * jnp.sum(q_unit * d_q, -1, keepdims=True))
        d_k = k_scale * (d_keys - keys * jnp.sum(keys * d_keys, -1, keepdims=True))
        after[0:CHUNK, q_at] = d_q * slope[:, q_at]
        after[0:CHUNK, k_at] = d_k * slope[:, k_at]
        after[0:CHUNK, v_at] = (beta * solved) * slope[:, v_at]
    d_logdecay = mm_exact((rows <= cols).astype(F32), d_running)
    d_shifted = jnp.where(lanes < heads, d_logdecay * (-scale) * jax.nn.sigmoid(shifted), 0.0)
    d_params_ref[0:1, :] += jnp.sum(d_logdecay * logdecay, 0, keepdims=True)
    d_params_ref[1:2, :] += jnp.sum(d_shifted, 0, keepdims=True)
    d_pre_ref[:, width : width + 128] = (d_shifted + d_strengths * strengths * (1.0 - strengths)).astype(BF16)
    d_summed = after[0:CHUNK, :]
    total = taps_ref[3:4, :] * d_summed
    for j in range(3):
        total = total + taps_ref[j : j + 1, :] * after[3 - j : 3 - j + CHUNK, :]
    d_pre_ref[:, :width] = total.astype(BF16)
    for j in range(4):
        d_taps_ref[j : j + 1, :] += jnp.sum(
            d_summed * window[5 + j : 5 + j + CHUNK, :], 0, keepdims=True
        )
    after[CHUNK : CHUNK + 8, :] = after[0:8, :]


def mixer_forward(order, pre, taps, params, heads, key_dim, val_dim):
    chunks = pre.shape[0] // CHUNK
    width = taps.shape[1]
    here = lambda n, order: (order[n], 0)
    plain = lambda n, order: (n, 0)
    fixed = lambda n, order: (0, 0)
    return pl.pallas_call(
        functools.partial(forward_kernel, heads, key_dim, val_dim),
        grid_spec=pltpu.PrefetchScalarGridSpec(
            num_scalar_prefetch=1,
            grid=(chunks,),
            in_specs=[
                pl.BlockSpec((CHUNK, pre.shape[1]), here),
                pl.BlockSpec(taps.shape, fixed),
                pl.BlockSpec(params.shape, fixed),
            ],
            out_specs=[
                pl.BlockSpec((CHUNK, heads * val_dim), here),
                pl.BlockSpec((heads * key_dim, val_dim), plain),
                pl.BlockSpec((heads * CHUNK, CHUNK), plain),
                pl.BlockSpec((CHUNK, heads * val_dim), plain),
            ],
            scratch_shapes=[
                pltpu.VMEM((heads * key_dim, val_dim), F32),
                pltpu.VMEM((CHUNK + 8, width), F32),
            ],
        ),
        out_shape=[
            jax.ShapeDtypeStruct((pre.shape[0], heads * val_dim), F32),
            jax.ShapeDtypeStruct((chunks * heads * key_dim, val_dim), BF16),
            jax.ShapeDtypeStruct((chunks * heads * CHUNK, CHUNK), BF16),
            jax.ShapeDtypeStruct((pre.shape[0], heads * val_dim), BF16),
        ],
        compiler_params=pltpu.CompilerParams(vmem_limit_bytes=48 * 2**20),
        cost_estimate=pl.CostEstimate(
            flops=2 * 10**9, bytes_accessed=2**20, transcendentals=0
        ),
        name="mixer_forward",
    )(order, pre, taps, params)


def mixer_backward(
    order, pre, taps, params, states, inverses, news, mixed, gates, d_own, d_other, side, gain,
    heads, key_dim, val_dim,
):
    chunks = pre.shape[0] // CHUNK
    width = taps.shape[1]
    out_width = heads * val_dim
    per = CHUNK // 8
    here = lambda n, order: (order[chunks - 1 - n], 0)
    half = chunks // 2
    first = lambda n, order: (jnp.minimum(order[chunks - 1 - n], half - 1), 0)
    second = lambda n, order: (jnp.maximum(order[chunks - 1 - n] - half, 0), 0)
    before = lambda n, order: (order[jnp.maximum(chunks - 2 - n, 0)] * per + per - 1, 0)
    plain = lambda n, order: (chunks - 1 - n, 0)
    fixed = lambda n, order: (0, 0)
    return pl.pallas_call(
        functools.partial(backward_kernel, heads, key_dim, val_dim),
        grid_spec=pltpu.PrefetchScalarGridSpec(
            num_scalar_prefetch=1,
            grid=(chunks,),
            in_specs=[
                pl.BlockSpec((CHUNK, pre.shape[1]), here),
                pl.BlockSpec((8, pre.shape[1]), before),
                pl.BlockSpec(taps.shape, fixed),
                pl.BlockSpec(params.shape, fixed),
                pl.BlockSpec((heads * key_dim, val_dim), plain),
                pl.BlockSpec((heads * CHUNK, CHUNK), plain),
                pl.BlockSpec((CHUNK, out_width), plain),
                pl.BlockSpec((CHUNK, out_width), here),
                pl.BlockSpec((CHUNK, out_width), here),
                pl.BlockSpec((CHUNK, d_own.shape[1]), first),
                pl.BlockSpec((CHUNK, d_own.shape[1]), second),
                pl.BlockSpec(side.shape, lambda n, order: (0, 0, 0, 0)),
                pl.BlockSpec((1, val_dim), fixed),
            ],
            out_specs=[
                pl.BlockSpec((CHUNK, pre.shape[1] + out_width), here),
                pl.BlockSpec((8, width), fixed),
                pl.BlockSpec((8, 128), fixed),
                pl.BlockSpec((8, val_dim), fixed),
            ],
            scratch_shapes=[
                pltpu.VMEM((heads * key_dim, val_dim), F32),
                pltpu.VMEM((CHUNK + 8, width), F32),
                pltpu.VMEM((CHUNK + 8, width), F32),
            ],
        ),
        out_shape=[
            jax.ShapeDtypeStruct((pre.shape[0], pre.shape[1] + out_width), BF16),
            jax.ShapeDtypeStruct((8, width), F32),
            jax.ShapeDtypeStruct((8, 128), F32),
            jax.ShapeDtypeStruct((8, val_dim), F32),
        ],
        compiler_params=pltpu.CompilerParams(vmem_limit_bytes=48 * 2**20),
        cost_estimate=pl.CostEstimate(
            flops=2 * 10**9, bytes_accessed=2 * 2**20, transcendentals=0
        ),
        name="mixer_backward",
    )(order, pre, pre, taps, params, states, inverses, news, mixed, gates, d_own, d_other, side, gain)


def roomy(**cost):
    return dict(
        compiler_params=pltpu.CompilerParams(vmem_limit_bytes=56 * 2**20),
        cost_estimate=pl.CostEstimate(
            flops=cost["flops"] // 8, bytes_accessed=cost["bytes"] // 8, transcendentals=0
        ),
    )


def pack_mix_kernel(heads, core_ref, q_ref, k_ref, v_ref, decay_ref, strength_ref, out_ref):
    first = core_ref[0] == 0
    wide, tall = q_ref.shape[1], v_ref.shape[1]
    out_ref[:, :wide] = q_ref[...]
    out_ref[:, wide : 2 * wide] = k_ref[...]
    out_ref[:, 2 * wide : 2 * wide + tall] = v_ref[...]

    def part(ref):
        values = ref[...].astype(F32)
        return jnp.where(first, values[:, :heads], values[:, heads:])

    rows = out_ref.shape[0]
    out_ref[:, 2 * wide + tall :] = jnp.concatenate(
        [part(decay_ref), part(strength_ref), jnp.zeros((rows, 128 - 2 * heads), F32)], 1
    ).astype(BF16)


def pack_mix(core, heads, w_query, w_key, w_value, w_decay, w_strength):
    depth = w_query.shape[0]
    wide, tall = w_query.shape[1] // 2, w_value.shape[1] // 2
    here = lambda i, core: (0, core[0])
    fixed = lambda i, core: (0, 0)
    return pl.pallas_call(
        functools.partial(pack_mix_kernel, heads),
        grid_spec=pltpu.PrefetchScalarGridSpec(
            num_scalar_prefetch=1,
            grid=(1,),
            in_specs=[
                pl.BlockSpec((depth, wide), here),
                pl.BlockSpec((depth, wide), here),
                pl.BlockSpec((depth, tall), here),
                pl.BlockSpec(w_decay.shape, fixed),
                pl.BlockSpec(w_strength.shape, fixed),
            ],
            out_specs=pl.BlockSpec((depth, 2 * wide + tall + 128), fixed),
        ),
        out_shape=jax.ShapeDtypeStruct((depth, 2 * wide + tall + 128), BF16),
        name="pack_mix",
        **roomy(flops=10**6, bytes=2**21),
    )(core, w_query, w_key, w_value, w_decay, w_strength)


def pack_rest_kernel(core_ref, outgate_ref, out_ref, gate_ref, up_ref, down_ref, side_ref, wide_ref):
    first = core_ref[0] == 0
    depth = outgate_ref.shape[0]
    units = gate_ref.shape[1] // 2
    side_ref[:depth, :] = outgate_ref[...]
    side_ref[depth:, :] = jnp.transpose(out_ref[...].astype(F32)).astype(BF16)
    for at, ref in ((0, gate_ref), (1, up_ref)):
        values = ref[...]
        wide_ref[at * depth : (at + 1) * depth, :] = jnp.where(
            first, values[:, :units], values[:, units:]
        )
    wide_ref[2 * depth :, :] = jnp.transpose(down_ref[...].astype(F32)).astype(BF16)


def pack_rest(core, w_outgate, w_out, w_gate, w_up, w_down):
    depth = w_outgate.shape[0]
    tall, units = w_outgate.shape[1] // 2, w_gate.shape[1] // 2
    fixed = lambda i, core: (0, 0)
    return pl.pallas_call(
        pack_rest_kernel,
        grid_spec=pltpu.PrefetchScalarGridSpec(
            num_scalar_prefetch=1,
            grid=(1,),
            in_specs=[
                pl.BlockSpec((depth, tall), lambda i, core: (0, core[0])),
                pl.BlockSpec((tall, depth), lambda i, core: (core[0], 0)),
                pl.BlockSpec(w_gate.shape, fixed),
                pl.BlockSpec(w_up.shape, fixed),
                pl.BlockSpec((units, depth), lambda i, core: (core[0], 0)),
            ],
            out_specs=[
                pl.BlockSpec((2 * depth, tall), fixed),
                pl.BlockSpec((3 * depth, units), fixed),
            ],
        ),
        out_shape=[
            jax.ShapeDtypeStruct((2 * depth, tall), BF16),
            jax.ShapeDtypeStruct((3 * depth, units), BF16),
        ],
        name="pack_rest",
        **roomy(flops=10**6, bytes=10 * 2**20),
    )(core, w_outgate, w_out, w_gate, w_up, w_down)


def arrange_kernel(scalars_ref, tokens_ref, cotangent_ref, gain_ref, normed_ref, branch_ref):
    step = pl.program_id(0)
    rows = tokens_ref.shape[0]
    tokens = tokens_ref[...].astype(F32)
    scale = lax.rsqrt(jnp.mean(tokens * tokens, -1, keepdims=True) + 1e-6)
    normed_ref[...] = (tokens * scale * gain_ref[...]).astype(BF16)
    place = scalars_ref[0] + scalars_ref[2 + step] * rows + lax.broadcasted_iota(
        jnp.int32, (rows, 1), 0
    )
    branch_ref[...] = jnp.where(place < scalars_ref[1], cotangent_ref[...], 0).astype(BF16)


def arrange(scalars, tokens, cotangent, gain, layers):
    rows, model = tokens.shape[0] // layers, tokens.shape[1]
    there = pl.BlockSpec((rows, model), lambda p, scalars: (scalars[2 + p], 0))
    plain = pl.BlockSpec((rows, model), lambda p, scalars: (p, 0))
    return pl.pallas_call(
        arrange_kernel,
        grid_spec=pltpu.PrefetchScalarGridSpec(
            num_scalar_prefetch=1,
            grid=(layers,),
            in_specs=[there, there, pl.BlockSpec((1, model), lambda p, scalars: (0, 0))],
            out_specs=[plain, plain],
        ),
        out_shape=[jax.ShapeDtypeStruct(tokens.shape, BF16)] * 2,
        name="arrange",
        **roomy(flops=10**7, bytes=8 * 2**20),
    )(scalars, tokens, cotangent, gain)


TILE = 256


def heads_kernel(
    heads, normed_ref, mixed_ref, side_ref, gain_ref, gates_ref, heads_ref, other_ref, own_ref
):
    step = pl.program_id(0)
    half = pl.num_programs(0) // 2
    shards, _, depth, tall = side_ref.shape
    val_dim = tall // heads
    gates = mm(normed_ref[:, :depth], side_ref[0, 0])
    for f in range(1, shards):
        gates = gates + mm(normed_ref[:, f * depth : (f + 1) * depth], side_ref[f, 0])
    gates_ref[...] = gates
    for h in range(heads):
        at = slice(h * val_dim, (h + 1) * val_dim)
        mixed = mixed_ref[:, at]
        gate = gates[:, at]
        scale = lax.rsqrt(jnp.mean(mixed * mixed, -1, keepdims=True) + 1e-5)
        heads_ref[:, at] = (
            mixed * scale * gain_ref[...] * (gate * jax.nn.sigmoid(gate))
        ).astype(BF16)
    low = heads_ref[...]

    def write(ref):
        for f in range(shards):
            ref[:, f * depth : (f + 1) * depth] = mm(low, side_ref[f, 1], NT).astype(BF16)

    @pl.when(step < half)
    def _():
        write(other_ref)

    @pl.when(step >= half)
    def _():
        write(own_ref)


def turned_specs(tiles):
    half = tiles // 2
    here = lambda i: (jnp.where(i < half, i + half, i - half), 0)
    other = lambda i: (jnp.minimum(i, half - 1), 0)
    own = lambda i: (jnp.maximum(i - half, 0), 0)
    return here, other, own


def head_outputs(normed, mixed, side, gain, heads):
    count, model = normed.shape
    tall = mixed.shape[1]
    here, other, own = turned_specs(count // TILE)
    return pl.pallas_call(
        functools.partial(heads_kernel, heads),
        grid=(count // TILE,),
        in_specs=[
            pl.BlockSpec((TILE, model), here),
            pl.BlockSpec((TILE, tall), here),
            pl.BlockSpec(side.shape, lambda i: (0, 0, 0, 0)),
            pl.BlockSpec(gain.shape, lambda i: (0, 0)),
        ],
        out_specs=[
            pl.BlockSpec((TILE, tall), here),
            pl.BlockSpec((TILE, tall), here),
            pl.BlockSpec((TILE, model), other),
            pl.BlockSpec((TILE, model), own),
        ],
        out_shape=[
            jax.ShapeDtypeStruct((count, tall), F32),
            jax.ShapeDtypeStruct((count, tall), BF16),
            jax.ShapeDtypeStruct((count // 2, model), BF16),
            jax.ShapeDtypeStruct((count // 2, model), BF16),
        ],
        name="head_outputs",
        **roomy(flops=4 * count * model * tall, bytes=16 * 2**20),
    )(normed, mixed, side, gain)


def feed_kernel(hidden_ref, branch_ref, wide_ref, stack_ref, d_hidden_ref, branch_out_ref):
    shards, _, depth, units = wide_ref.shape

    def forward(ref, at):
        total = mm(ref[:, :depth], wide_ref[0, at])
        for f in range(1, shards):
            total = total + mm(ref[:, f * depth : (f + 1) * depth], wide_ref[f, at])
        return total

    gate = forward(hidden_ref, 0)
    up = forward(hidden_ref, 1)
    d_act = forward(branch_ref, 2)
    sigma = jax.nn.sigmoid(gate)
    silu = gate * sigma
    act = (silu * up).astype(BF16)
    d_gate = (d_act * up * (sigma + silu * (1.0 - sigma))).astype(BF16)
    d_up = (d_act * silu).astype(BF16)
    stack_ref[0] = d_gate
    stack_ref[1] = d_up
    stack_ref[2] = act
    for f in range(shards):
        at = slice(f * depth, (f + 1) * depth)
        d_hidden_ref[:, at] = (
            mm(d_gate, wide_ref[f, 0], NT) + mm(d_up, wide_ref[f, 1], NT)
        ).astype(BF16)
        branch_out_ref[:, at] = mm(act, wide_ref[f, 2], NT).astype(BF16)


def feed_forward(hidden, branch, wide):
    count, model = hidden.shape
    units = wide.shape[3]
    row = pl.BlockSpec((TILE, model), lambda i: (i, 0))
    return pl.pallas_call(
        feed_kernel,
        grid=(count // TILE,),
        in_specs=[row, row, pl.BlockSpec(wide.shape, lambda i: (0, 0, 0, 0))],
        out_specs=[pl.BlockSpec((3, TILE, units), lambda i: (0, i, 0)), row, row],
        out_shape=[
            jax.ShapeDtypeStruct((3, count, units), BF16),
            jax.ShapeDtypeStruct((count, model), BF16),
            jax.ShapeDtypeStruct((count, model), BF16),
        ],
        name="feed_forward",
        **roomy(flops=12 * count * model * units, bytes=20 * 2**20),
    )(hidden, branch, wide)


def feed_grads_kernel(h_own, h_other, b_own, b_other, s_own, s_other, out_ref):
    units = s_own.shape[2]
    for at, own, other in ((0, h_own, h_other), (1, h_own, h_other), (2, b_own, b_other)):
        out_ref[:, at * units : (at + 1) * units] = (
            mm(own[...], s_own[at], TN) + mm(other[...], s_other[at], TN)
        ).astype(BF16)
    rest = out_ref.shape[1] - 3 * units
    if rest:
        out_ref[:, 3 * units :] = jnp.zeros((out_ref.shape[0], rest), BF16)


def feed_grads(hidden, branch, stacks, shards):
    count, model = hidden[0].shape
    units = stacks[0].shape[2]
    depth = model // shards
    width = -(-3 * units // 128) * 128
    part = pl.BlockSpec((count, depth), lambda f: (0, f))
    use_s = pl.BlockSpec((3, count, units), lambda f: (0, 0, 0))
    return pl.pallas_call(
        feed_grads_kernel,
        grid=(shards,),
        in_specs=[part, part, part, part, use_s, use_s],
        out_specs=pl.BlockSpec((depth, width), lambda f: (f, 0)),
        out_shape=jax.ShapeDtypeStruct((model, width), BF16),
        name="feed_grads",
        **roomy(flops=12 * count * model * units, bytes=20 * 2**20),
    )(*hidden, *branch, *stacks)


def d_normed_kernel(side_at, mix_ref, normed_ref, weights_ref, side_ref, other_ref, own_ref, sum_ref):
    step = pl.program_id(0)
    half = pl.num_programs(0) // 2
    shards, _, depth, _ = side_ref.shape

    @pl.when(step == 0)
    def _():
        sum_ref[...] = jnp.zeros_like(sum_ref)

    def write(ref):
        for f in range(shards):
            at = slice(f * depth, (f + 1) * depth)
            part = mm(mix_ref[:, :side_at], weights_ref[at, :], NT) + mm(
                mix_ref[:, side_at:], side_ref[f, 0], NT
            )
            ref[:, at] = part.astype(BF16)
            sum_ref[0:1, at] += jnp.sum(part * normed_ref[:, at].astype(F32), 0, keepdims=True)

    @pl.when(step < half)
    def _():
        write(other_ref)

    @pl.when(step >= half)
    def _():
        write(own_ref)


def d_normed_rows(d_mix, normed, weights, side):
    count, model = normed.shape
    here, other, own = turned_specs(count // TILE)
    fixed = lambda i: (0, 0)
    return pl.pallas_call(
        functools.partial(d_normed_kernel, weights.shape[1]),
        grid=(count // TILE,),
        in_specs=[
            pl.BlockSpec((TILE, d_mix.shape[1]), here),
            pl.BlockSpec((TILE, model), here),
            pl.BlockSpec(weights.shape, fixed),
            pl.BlockSpec(side.shape, lambda i: (0, 0, 0, 0)),
        ],
        out_specs=[
            pl.BlockSpec((TILE, model), other),
            pl.BlockSpec((TILE, model), own),
            pl.BlockSpec((8, model), fixed),
        ],
        out_shape=[
            jax.ShapeDtypeStruct((count // 2, model), BF16),
            jax.ShapeDtypeStruct((count // 2, model), BF16),
            jax.ShapeDtypeStruct((8, model), F32),
        ],
        name="d_normed_rows",
        **roomy(flops=2 * count * model * d_mix.shape[1], bytes=16 * 2**20),
    )(d_mix, normed, weights, side)


def mix_grads_kernel(at, normed_ref, mix_ref, d_own_ref, d_other_ref, heads_ref, extra_ref, out_ref):
    width = mix_ref.shape[1]
    half = d_own_ref.shape[0]
    out_ref[:, :width] = mm(normed_ref[...], mix_ref[...], TN).astype(BF16)
    out_ref[:, width:] = (
        mm(d_own_ref[...], heads_ref[:half, :], TN) + mm(d_other_ref[...], heads_ref[half:, :], TN)
    ).astype(BF16)
    out_ref[:, at : at + extra_ref.shape[1]] = extra_ref[...]


def mix_grads(normed, d_mix, d_own, d_other, heads_out, extra, at, shards):
    count, model = normed.shape
    depth = model // shards
    width = d_mix.shape[1] + heads_out.shape[1]
    fixed = lambda f: (0, 0)
    return pl.pallas_call(
        functools.partial(mix_grads_kernel, at),
        grid=(shards,),
        in_specs=[
            pl.BlockSpec((count, depth), lambda f: (0, f)),
            pl.BlockSpec(d_mix.shape, fixed),
            pl.BlockSpec((count // 2, depth), lambda f: (0, f)),
            pl.BlockSpec((count // 2, depth), lambda f: (0, f)),
            pl.BlockSpec(heads_out.shape, fixed),
            pl.BlockSpec((depth, extra.shape[1]), lambda f: (f, 0)),
        ],
        out_specs=pl.BlockSpec((depth, width), lambda f: (f, 0)),
        out_shape=jax.ShapeDtypeStruct((model, width), BF16),
        name="mix_grads",
        **roomy(flops=2 * count * model * width, bytes=20 * 2**20),
    )(normed, d_mix, d_own, d_other, heads_out, extra)


def finish_wide_kernel(units, core_ref, own_ref, other_ref, gate_ref, up_ref, down_ref):
    first = core_ref[0] == 0
    own, other = own_ref[...].astype(F32), other_ref[...].astype(F32)
    low, high = jnp.where(first, own, other), jnp.where(first, other, own)
    for at, ref in ((0, gate_ref), (1, up_ref)):
        ref[:, :units] = low[:, at * units : (at + 1) * units]
        ref[:, units:] = high[:, at * units : (at + 1) * units]
    down_ref[:units, :] = jnp.transpose(low[:, 2 * units : 3 * units])
    down_ref[units:, :] = jnp.transpose(high[:, 2 * units : 3 * units])


def finish_wide(core, own, other, units):
    depth, width = own.shape
    row = lambda size: pl.BlockSpec((128, size), lambda i, core: (i, 0))
    return pl.pallas_call(
        functools.partial(finish_wide_kernel, units),
        grid_spec=pltpu.PrefetchScalarGridSpec(
            num_scalar_prefetch=1,
            grid=(depth // 128,),
            in_specs=[row(width), row(width)],
            out_specs=[
                row(2 * units),
                row(2 * units),
                pl.BlockSpec((2 * units, 128), lambda i, core: (0, i)),
            ],
        ),
        out_shape=[
            jax.ShapeDtypeStruct((depth, 2 * units), F32),
            jax.ShapeDtypeStruct((depth, 2 * units), F32),
            jax.ShapeDtypeStruct((2 * units, depth), F32),
        ],
        name="finish_wide",
        **roomy(flops=10**6, bytes=14 * 2**20),
    )(core, own, other)


def finish_mix_kernel(cuts, core_ref, a_ref, b_ref, *refs):
    first = core_ref[0] == 0
    own, other = a_ref[...].astype(F32), b_ref[...].astype(F32)
    low, high = jnp.where(first, own, other), jnp.where(first, other, own)
    for (begin, size), ref in zip(cuts[:-1], refs):
        ref[:, :size] = low[:, begin : begin + size]
        ref[:, size:] = high[:, begin : begin + size]
    begin, size = cuts[-1]
    refs[-1][:size, :] = jnp.transpose(low[:, begin : begin + size])
    refs[-1][size:, :] = jnp.transpose(high[:, begin : begin + size])


def finish_mix(core, own, other, cuts):
    depth, width = own.shape
    tall = cuts[-1][1]
    row = lambda size: pl.BlockSpec((128, size), lambda i, core: (i, 0))
    return pl.pallas_call(
        functools.partial(finish_mix_kernel, cuts),
        grid_spec=pltpu.PrefetchScalarGridSpec(
            num_scalar_prefetch=1,
            grid=(depth // 128,),
            in_specs=[row(width), row(width)],
            out_specs=[row(2 * size) for _, size in cuts[:-1]]
            + [pl.BlockSpec((2 * tall, 128), lambda i, core: (0, i))],
        ),
        out_shape=[jax.ShapeDtypeStruct((depth, 2 * size), F32) for _, size in cuts[:-1]]
        + [jax.ShapeDtypeStruct((2 * tall, depth), F32)],
        name="finish_mix",
        **roomy(flops=10**6, bytes=14 * 2**20),
    )(core, own, other)


def after(value, *others):
    return lax.optimization_barrier((value,) + others)[0]


def is_square(axis):
    return lax.axis_size(axis) == 4


def across(value, flip):
    return lax.ppermute(value, "fsdp", [(i, i ^ flip) for i in range(4)])


def swapped(value):
    return lax.ppermute(value, "context", [(0, 1), (1, 0)])


def gathered_rows(own, beside):
    if not is_square("fsdp"):
        return lax.all_gather(own, "fsdp", axis=0, tiled=True), beside
    rows = own.shape[0]
    half = rows // 2
    along_x = across(own, 1)
    along_y = across(own, 2)
    along_x, along_y, beside = lax.optimization_barrier((along_x, along_y, beside))
    low = across(along_x[:half], 2)
    high = across(along_y[half:], 1)
    shard = lax.axis_index("fsdp")
    whole = jnp.zeros((4 * rows,) + own.shape[1:], own.dtype)
    for place, part in ((0, own), (1, along_x), (2, along_y)):
        whole = lax.dynamic_update_slice_in_dim(whole, part, (shard ^ place) * rows, 0)
    whole = lax.dynamic_update_slice_in_dim(whole, low, (shard ^ 3) * rows, 0)
    return lax.dynamic_update_slice_in_dim(whole, high, (shard ^ 3) * rows + half, 0), beside


def scattered(blocks):
    return lax.psum_scatter(blocks, "fsdp", scatter_dimension=0, tiled=True)


def line_sum(value, beside=(), axis="tensor"):
    size = lax.axis_size(axis)
    rows = value.shape[0] // size
    parts = [
        lax.ppermute(
            value[p * rows : (p + 1) * rows], axis, [(i, (i - p) % size) for i in range(size)]
        )
        for p in range(1, size)
    ]
    if beside:
        parts, beside = lax.optimization_barrier((parts, tuple(beside)))
    total = value[:rows].astype(F32)
    for part in parts:
        total = total + part.astype(F32)
    return (total, *beside) if beside else total


def line_sum_hops(value, axis="tensor"):
    size = lax.axis_size(axis)
    rows = value.shape[0] // size
    block = lambda p: value[p * rows : (p + 1) * rows].astype(F32)
    right = left = None
    for step in range(1, size):
        send_r, send_l = block(step), block(size - step)
        if right is not None:
            send_r = send_r + right.astype(F32)
            send_l = send_l + left.astype(F32)
        right = lax.ppermute(send_r.astype(BF16), axis, [(i, i + 1) for i in range(step)])
        left = lax.ppermute(
            send_l.astype(BF16), axis, [(i, i - 1) for i in range(size - step, size)]
        )
    return block(0) + right.astype(F32) + left.astype(F32)


def line_gather(own, beside=(), axis="tensor"):
    size = lax.axis_size(axis)
    rights, lefts = [own], [own]
    for step in range(1, size):
        rights.append(
            lax.ppermute(rights[-1], axis, [(i, i + 1) for i in range(step - 1, size - 1)])
        )
        lefts.append(lax.ppermute(lefts[-1], axis, [(i, i - 1) for i in range(1, size - step + 1)]))
    if beside:
        (rights, lefts), beside = lax.optimization_barrier(((rights, lefts), tuple(beside)))
    parts = [own] + [rights[k] + lefts[size - k] for k in range(1, size)]
    return (parts, *beside) if beside else parts


def line_gather_direct(own, axis="tensor"):
    size = lax.axis_size(axis)
    return [own] + [
        lax.ppermute(own, axis, [(i, (i + p) % size) for i in range(size)]) for p in range(1, size)
    ]


def line_total(value, axis="tensor"):
    size = lax.axis_size(axis)
    step = 1
    while step < size:
        value = value + lax.ppermute(value, axis, [(i, i ^ step) for i in range(size)])
        step *= 2
    return value


def core_sum(other_rows, own_rows):
    return (own_rows.astype(F32) + swapped(other_rows).astype(F32)).astype(BF16)


def dot(a, b, dims=NN):
    return lax.dot_general(a, b, (dims, ((), ())), preferred_element_type=F32)


def norm_parts(values, epsilon):
    return lax.rsqrt(jnp.mean(values * values, -1, keepdims=True) + epsilon)


def norm_back(d_scaled, values, scale, gain):
    raised = d_scaled * gain
    return scale * raised - values * (
        scale * scale * scale * jnp.mean(raised * values, -1, keepdims=True)
    )


def on_device(
    inputs, lengths, norm_attn, w_query, w_key, w_value, w_decay, w_strength, decay_log,
    decay_bias, conv_query, conv_key, conv_value, w_outgate, norm_head, w_out, norm_mlp, w_gate,
    w_up, w_down, cotangent,
):
    shard, core, layer = (lax.axis_index(name) for name in ("fsdp", "context", "tensor"))
    shards, layers = lax.axis_size("fsdp"), lax.axis_size("tensor")
    seg, model = inputs.shape[1:]
    rows = seg // layers
    depth = norm_attn.shape[0]
    all_heads, taps_count, key_part = conv_query.shape
    val_part = conv_value.shape[2]
    heads = all_heads // 2
    key_dim, val_dim = key_part * shards, val_part * shards
    wide, tall = heads * key_dim, heads * val_dim
    width = 2 * wide + tall
    units = w_gate.shape[1] // 2

    def mine(array, dim):
        size = array.shape[dim] // 2
        first = lax.slice_in_dim(array, 0, size, axis=dim)
        second = lax.slice_in_dim(array, size, 2 * size, axis=dim)
        return jnp.where(core == 0, first, second)

    core_id = core.reshape(1).astype(jnp.int32)
    own_mix = pack_mix(core_id, heads, w_query, w_key, w_value, w_decay, w_strength)

    pieces = (
        norm_attn, norm_mlp, norm_head,
        mine(conv_query, 0).reshape(-1), mine(conv_key, 0).reshape(-1),
        mine(conv_value, 0).reshape(-1),
    )
    small = after(jnp.concatenate(pieces), own_mix)
    if is_square("fsdp"):
        stack = jnp.stack([small, across(small, 1), across(small, 2), across(small, 3)])
        stack = jnp.stack([lax.dynamic_index_in_dim(stack, shard ^ i, 0, False) for i in range(4)])
    else:
        stack = lax.all_gather(small, "fsdp")
    cuts = [0]
    for piece in pieces:
        cuts.append(cuts[-1] + piece.shape[0])
    gain_attn = stack[:, cuts[0] : cuts[1]].reshape(1, model).astype(F32)
    gain_mlp = stack[:, cuts[1] : cuts[2]].reshape(1, model).astype(F32)
    gain_head = stack[:, cuts[2] : cuts[3]].reshape(1, val_dim).astype(F32)

    def taps_of(at, part):
        array = stack[:, cuts[at] : cuts[at + 1]].reshape(shards, heads, taps_count, part)
        return jnp.transpose(array, (2, 1, 0, 3)).reshape(taps_count, -1)

    taps = jnp.concatenate([taps_of(3, key_part), taps_of(4, key_part), taps_of(5, val_part)], 1)
    taps = jnp.pad(taps.astype(F32), ((0, 8 - taps_count), (0, 0)))
    params = jnp.pad(
        jnp.stack([mine(decay_log, 0), mine(decay_bias, 0)]).astype(F32),
        ((0, 6), (0, 128 - heads)),
    )

    turns = (layer - jnp.arange(layers, dtype=jnp.int32)) % layers
    scalars = jnp.concatenate([(core * seg).reshape(1), lengths[:1], turns]).astype(jnp.int32)
    per_core, per_block = seg // CHUNK, rows // CHUNK
    ids = jnp.arange(2 * per_core, dtype=jnp.int32)
    within = ids % per_core
    order = (
        jnp.where(ids // per_core == core, 0, per_core)
        + ((layer - within // per_block) % layers) * per_block
        + within % per_block
    ).astype(jnp.int32)
    live_own = (
        core * seg + layer * rows + jnp.arange(rows, dtype=jnp.int32) < lengths[0]
    ).astype(F32)[:, None]
    tokens_own = lax.dynamic_slice_in_dim(inputs[0], layer * rows, rows, 0).astype(F32)
    d_out_own = lax.dynamic_slice_in_dim(cotangent[0], layer * rows, rows, 0).astype(F32)
    normed_own, d_branch_own = arrange(scalars, inputs[0], cotangent[0], gain_attn, layers)
    normed_other = swapped(normed_own)
    own_side, own_feed = pack_rest(core_id, w_outgate, w_out, w_gate, w_up, w_down)
    full_mix, (normed_other, own_side, own_feed) = gathered_rows(
        own_mix, (normed_other, own_side, own_feed)
    )
    normed = jnp.concatenate([normed_own, normed_other], 0)
    d_branch = (d_branch_own, swapped(after(d_branch_own, full_mix)))
    side = lax.all_gather(after(own_side, full_mix), "fsdp", axis=0, tiled=True)

    projected = dot(normed, full_mix)
    feed = lax.all_gather(after(own_feed, projected), "fsdp", axis=0, tiled=True)
    side = side.reshape(shards, 2, depth, tall)
    feed = feed.reshape(shards, 3, depth, units)
    mixed, states, inverses, news = mixer_forward(
        order, projected, taps, params, heads, key_dim, val_dim
    )
    gates, heads_out, attn_other, attn_own = head_outputs(normed, mixed, side, gain_head, heads)
    attn = line_sum_hops(core_sum(attn_other, attn_own))
    middle = tokens_own + live_own * attn
    mlp_scale = norm_parts(middle, 1e-6)
    hidden_own = (middle * mlp_scale * gain_mlp).astype(BF16)
    hidden_mine = jnp.concatenate(line_gather(hidden_own), 0)
    hidden = (hidden_mine, swapped(hidden_mine))

    stack_own, d_hidden_mine, branch_mine = feed_forward(hidden[0], d_branch[0], feed)
    stack_other, d_hidden_other, branch_other = feed_forward(hidden[1], d_branch[1], feed)
    d_hidden_core = core_sum(d_hidden_other, d_hidden_mine)
    held = lax.optimization_barrier((stack_own, stack_other, branch_other, d_hidden_core))
    grad_feed = feed_grads(hidden, d_branch, held[:2], shards)
    branch_core = core_sum(held[2], branch_mine)
    d_hidden, grad_feed, branch_core = line_sum(d_hidden_core, (grad_feed, branch_core))
    sum_feed = scattered(grad_feed)

    grad_mlp = jnp.sum(d_hidden * middle * mlp_scale, 0)
    d_middle = d_out_own + norm_back(d_hidden, middle, mlp_scale, gain_mlp)
    d_attn_mine = jnp.concatenate(line_gather((live_own * d_middle).astype(BF16)), 0)
    d_attn = (d_attn_mine, swapped(d_attn_mine))

    branch_core, *d_attn = lax.optimization_barrier((branch_core, *d_attn))

    def placed(parts):
        whole = jnp.zeros((seg, model), BF16)
        for p, part in enumerate(parts):
            whole = lax.dynamic_update_slice(whole, part, (((layer - p) % layers) * rows, 0))
        return whole[None]

    d_mix, d_taps, d_params, d_gain = mixer_backward(
        order, projected, taps, params, states, inverses, news, mixed, gates, *d_attn, side,
        gain_head, heads, key_dim, val_dim,
    )
    branch, d_mix = line_sum(branch_core, (d_mix,))
    out_own = (middle + live_own * branch).astype(BF16)
    out_own, sum_feed, d_mix = lax.optimization_barrier((out_own, sum_feed, d_mix))
    out_parts = line_gather_direct(out_own)
    side_at = width + 128
    d_normed_other, d_normed_mine, weighted = d_normed_rows(d_mix, normed, full_mix, side)
    d_normed_core = core_sum(d_normed_other, d_normed_mine)

    grad_attn = weighted[0] / gain_attn[0]
    vector = after(jnp.concatenate([grad_mlp, grad_attn, d_gain[0]]), d_normed_core)
    vector = line_total(vector + swapped(vector))

    def tap_rows(begin, size):
        array = d_taps[:taps_count, begin : begin + heads * size]
        array = array.reshape(taps_count, heads, shards, size // shards)
        return jnp.transpose(array, (2, 0, 1, 3)).reshape(shards, -1)

    tap_list = jnp.concatenate(
        [tap_rows(0, key_dim), tap_rows(wide, key_dim), tap_rows(2 * wide, val_dim)], 1
    )
    tap_size = tap_list.shape[1]
    tap_lines = -(-tap_size // depth)
    tap_list = jnp.pad(tap_list, ((0, 0), (0, tap_lines * depth - tap_size)))
    tap_list = jnp.transpose(tap_list.reshape(shards, tap_lines, depth), (1, 0, 2))
    decays = jnp.concatenate([d_params[0, :heads], d_params[1, :heads]])
    mixed_line = jnp.concatenate(
        [
            vector[2 * model :].reshape(shards, val_part),
            jnp.broadcast_to(decays, (shards, 2 * heads)),
            jnp.zeros((shards, depth - val_part - 2 * heads), F32),
        ],
        1,
    )
    lines = jnp.concatenate(
        [
            vector[: 2 * model].reshape(2, model), mixed_line.reshape(1, model),
            tap_list.reshape(tap_lines, model),
        ],
        0,
    )
    extra = jnp.transpose(jnp.pad(lines, ((0, 64 - lines.shape[0]), (0, 0)))).astype(BF16)
    grad_mix = mix_grads(normed, d_mix, *d_attn, heads_out, extra, width + 64, shards)
    d_normed, grad_mix = line_sum(d_normed_core, (grad_mix,))
    low_mix = scattered(grad_mix)
    other_mix = swapped(low_mix)

    d_tokens = norm_back(d_normed, tokens_own, norm_parts(tokens_own, 1e-6), gain_attn)
    feed_done = finish_wide(core_id, sum_feed, swapped(sum_feed), units)
    parts, (g_gate, g_up, g_down) = line_gather((d_middle + d_tokens).astype(BF16), (feed_done,))
    input_grad = placed(parts)
    output = placed(out_parts)
    g_query, g_key, g_value, g_outgate, g_out = finish_mix(
        core_id, low_mix, other_mix,
        ((0, wide), (wide, wide), (2 * wide, tall), (side_at, tall), (side_at + tall, tall)),
    )

    def column(table, at):
        return table[:, width + 64 + at].astype(F32)

    def of_heads(table):
        flat = jnp.concatenate([column(table, 3 + i) for i in range(tap_lines)])
        q_count, v_count = taps_count * heads * key_part, taps_count * heads * val_part

        def cut_taps(begin, count):
            array = flat[begin : begin + count].reshape(taps_count, heads, -1)
            return jnp.transpose(array, (1, 0, 2))

        line = column(table, 2)
        return (
            line[val_part : val_part + heads],
            line[val_part + heads : val_part + 2 * heads],
            cut_taps(0, q_count),
            cut_taps(q_count, q_count),
            cut_taps(2 * q_count, v_count),
        )

    def ordered(own, other, dim):
        return jnp.where(
            core == 0, jnp.concatenate([own, other], dim), jnp.concatenate([other, own], dim)
        )

    d_log, d_bias, d_conv_q, d_conv_k, d_conv_v = (
        ordered(a, b, 0) for a, b in zip(of_heads(low_mix), of_heads(other_mix))
    )

    def narrow(begin):
        return ordered(
            low_mix[:, begin : begin + heads], other_mix[:, begin : begin + heads], 1
        ).astype(F32)

    return (
        output,
        input_grad,
        column(low_mix, 1),
        g_query,
        g_key,
        g_value,
        narrow(width),
        narrow(width + heads),
        d_log,
        d_bias,
        d_conv_q,
        d_conv_k,
        d_conv_v,
        g_outgate,
        column(low_mix, 2)[:val_part],
        g_out,
        column(low_mix, 0),
        g_gate,
        g_up,
        g_down,
    )


def solution(mesh):
    placed = (
        P("fsdp", "context", None),
        P("fsdp"),
        P("fsdp"),
        P("fsdp", "tensor"),
        P("fsdp", "tensor"),
        P("fsdp", "tensor"),
        P("fsdp", "tensor"),
        P("fsdp", "tensor"),
        P("tensor"),
        P("tensor"),
        P("tensor", None, "fsdp"),
        P("tensor", None, "fsdp"),
        P("tensor", None, "fsdp"),
        P("fsdp", "tensor"),
        P("fsdp"),
        P("tensor", "fsdp"),
        P("fsdp"),
        P("fsdp", "tensor"),
        P("fsdp", "tensor"),
        P("tensor", "fsdp"),
        P("fsdp", "context", None),
    )
    return jax.shard_map(
        on_device,
        mesh=mesh,
        in_specs=placed,
        out_specs=(placed[0], placed[0]) + placed[2:20],
        check_vma=False,
    )
```

profile of v0, /device:TPU:1, one launch (start us, length us, event | category | flops | bytes accessed | tf_op | source)
XLA Modules:
  0.0 645.2 jit_solution(15416293830735241748)
XLA Ops:
  25.4 5.8 arrange.1
  33.8 5.0 pack_rest.1
  38.8 22.3 %collective-permute-done.3 = bf16[512,1152]{1,0:T(8,128)(2,1)S(1)} collective-permute-done((bf16[512,1152]{1,0:T(8,128)(2,1)S(1)}, bf16[512,1152]{1,0:T(8,128)(2,1)S(1)}, u32[]{:S(2)}, u32[]{:S(2)}) %collective-permute-start.3) | collective-permute-done | bytes 1179680 | tf_op jit(solution)/shard_map/ppermute | solution.py:850
  69.3 6.7 %collective-permute-done.6 = bf16[256,1152]{1,0:T(8,128)(2,1)} collective-permute-done((bf16[256,1152]{1,0:T(8,128)(2,1)}, bf16[256,1152]{1,0:T(8,128)(2,1)}, u32[]{:S(2)}, u32[]{:S(2)}) %collective-permute-start.6) | collective-permute-done | bytes 589856 | tf_op jit(solution)/shard_map/ppermute | solution.py:850
  84.5 9.5 %fusion.38.pre_ref.before_ref = f32[1024,1152]{1,0:T(8,128)} fusion(bf16[1024,2048]{1,0:T(8,128)(2,1)S(1)} %constant_dynamic-update-slice_fusion.normed_ref, bf16[2048,1152]{1,0:T(8,128)(2,1)} %constant_dynamic-update-slice_fusion.2.weights_ref), kind=kOutput, calls=%fused_computation.153 | convolution fusion | flops 4831838208 | bytes 13631488 | tf_op jit(solution)/shard_map/dot_general | solution.py:948
  96.3 39.4 %mixer_forward.1 = (f32[1024,512]{1,0:T(8,128)S(1)}, bf16[2048,256]{1,0:T(8,128)(2,1)S(1)}, bf16[2048,128]{1,0:T(8,128)(2,1)S(1)}, bf16[1024,512]{1,0:T(8,128)(2,1)S(1)}) custom-call(s32[8]{0:T(128)S(1)} %fusion.23.order_ref, f32[1024,1152]{1,0:T(8,128)} %fusion.38.pre_ref.before_ref, f32[8,1024]{1,0:T(8,128)S(1)} %fusion.12.taps_ref, ...), custom_call_target="tpu_custom_call" | custom-call | flops 2000000000 | bytes 1048576 | tf_op jit(solution)/shard_map/mixer_forward/pallas_call | solution.py:313
  137.0 10.9 %head_outputs.1 = (f32[1024,512]{1,0:T(8,128)}, bf16[1024,512]{1,0:T(8,128)(2,1)}, bf16[512,2048]{1,0:T(8,128)(2,1)}, bf16[512,2048]{1,0:T(8,128)(2,1)}) custom-call(bf16[1024,2048]{1,0:T(8,128)(2,1)} %copy-done.3, f32[1024,512]{1,0:T(8,128)} %copy-done, bf16[4,2,512,512]{3,2,1,0:T(8,128)(2,1)} %bitcast.93, f32[1,256]{1,0:T(1,128)} %reshape.303.gain_ref), custom_call_target="tpu_custom_call" | custom-call | flops 536870912 | bytes 2097152 | tf_op jit(solution)/shard_map/head_outputs/pallas_call | solution.py:583
  150.0 4.0 collective-permute-done.8
  157.2 3.7 collective-permute-start.9
  160.9 10.4 %collective-permute-done.9 = bf16[128,2048]{1,0:T(8,128)(2,1)S(1)} collective-permute-done((bf16[128,2048]{1,0:T(8,128)(2,1)S(1)}, bf16[128,2048]{1,0:T(8,128)(2,1)S(1)}, u32[]{:S(2)}, u32[]{:S(2)}) %collective-permute-start.9) | collective-permute-done | bytes 524320 | tf_op jit(solution)/shard_map/ppermute | solution.py:906
  171.7 4.2 collective-permute-start.10
  176.6 9.4 %collective-permute-done.10 = bf16[128,2048]{1,0:T(8,128)(2,1)S(1)} collective-permute-done((bf16[128,2048]{1,0:T(8,128)(2,1)S(1)}, bf16[128,2048]{1,0:T(8,128)(2,1)S(1)}, u32[]{:S(2)}, u32[]{:S(2)}) %collective-permute-start.10) | collective-permute-done | bytes 524320 | tf_op jit(solution)/shard_map/ppermute | solution.py:906
  187.3 6.5 %collective-permute-start.11 = (bf16[128,2048]{1,0:T(8,128)(2,1)}, bf16[128,2048]{1,0:T(8,128)(2,1)S(1)}, u32[]{:S(2)}, u32[]{:S(2)}) collective-permute-start(bf16[128,2048]{1,0:T(8,128)(2,1)} %get-tuple-element.266), channel_id=1, source_target_pairs={{0,1},{1,2},{2,3},{4,5},{5,6},{6,7},{8,9},{9,10},{10,11},{12,13},{... | collective-permute-start | bytes 1572872 | tf_op jit(solution)/shard_map/ppermute | solution.py:906
  195.2 7.9 %collective-permute-done.11 = bf16[128,2048]{1,0:T(8,128)(2,1)S(1)} collective-permute-done((bf16[128,2048]{1,0:T(8,128)(2,1)}, bf16[128,2048]{1,0:T(8,128)(2,1)S(1)}, u32[]{:S(2)}, u32[]{:S(2)}) %collective-permute-start.11) | collective-permute-done | bytes 524320 | tf_op jit(solution)/shard_map/ppermute | solution.py:906
  203.1 3.9 collective-permute-done.14
  210.3 4.0 collective-permute-start.15
  214.3 6.7 %collective-permute-done.16 = bf16[128,2048]{1,0:T(8,128)(2,1)S(1)} collective-permute-done((bf16[128,2048]{1,0:T(8,128)(2,1)S(1)}, bf16[128,2048]{1,0:T(8,128)(2,1)S(1)}, u32[]{:S(2)}, u32[]{:S(2)}) %collective-permute-start.16) | collective-permute-done | bytes 524320 | tf_op jit(solution)/shard_map/ppermute | solution.py:920
  223.0 9.2 %collective-permute-done.17 = bf16[128,2048]{1,0:T(8,128)(2,1)S(1)} collective-permute-done((bf16[128,2048]{1,0:T(8,128)(2,1)S(1)}, bf16[128,2048]{1,0:T(8,128)(2,1)S(1)}, u32[]{:S(2)}, u32[]{:S(2)}) %collective-permute-start.17) | collective-permute-done | bytes 524320 | tf_op jit(solution)/shard_map/ppermute | solution.py:920
  234.2 5.1 collective-permute-start.22
  244.4 5.9 collective-permute-start.21
  250.3 4.1 collective-permute-done.21.hidden_ref.h_other
  254.4 16.9 %feed_forward.3 = (bf16[3,512,704]{2,1,0:T(8,128)(2,1)}, bf16[512,2048]{1,0:T(8,128)(2,1)}, bf16[512,2048]{1,0:T(8,128)(2,1)}) custom-call(bf16[512,2048]{1,0:T(8,128)(2,1)} %collective-permute-done.21.hidden_ref.h_other, bf16[512,2048]{1,0:T(8,128)(2,1)} %collective-permute-done.22.branch_ref.b_other, bf16[4,3,512,704]{3,2,1,0:T(8,128)(2,1)} %bitcast.91), custom_call_target="tpu_custom_call" | custom-call | flops 1107296256 | bytes 2621440 | tf_op jit(solution)/shard_map/feed_forward/pallas_call | solution.py:641
  271.7 16.9 %feed_forward.2 = (bf16[3,512,704]{2,1,0:T(8,128)(2,1)}, bf16[512,2048]{1,0:T(8,128)(2,1)}, bf16[512,2048]{1,0:T(8,128)(2,1)}) custom-call(bf16[512,2048]{1,0:T(8,128)(2,1)} %pad_maximum_fusion.hidden_ref.h_own, bf16[512,2048]{1,0:T(8,128)(2,1)} %get-tuple-element.110.branch_ref.b_own, bf16[4,3,512,704]{3,2,1,0:T(8,128)(2,1)} %bitcast.92), custom_call_target="tpu_custom_call" | custom-call | flops 1107296256 | bytes 2621440 | tf_op jit(solution)/shard_map/feed_forward/pallas_call | solution.py:641
  293.5 3.5 collective-permute-start.24
  297.4 15.3 %feed_grads.1 = bf16[2048,2176]{1,0:T(8,128)(2,1)} custom-call(bf16[512,2048]{1,0:T(8,128)(2,1)} %pad_maximum_fusion.hidden_ref.h_own, bf16[512,2048]{1,0:T(8,128)(2,1)} %collective-permute-done.21.hidden_ref.h_other, bf16[512,2048]{1,0:T(8,128)(2,1)} %get-tuple-element.110.branch_ref.b_own, bf16[512,2048]{1,0:T(8,128)(2,1)} %collective-permute-done.22.branch_ref.b_other, ...), custom_call_target="tpu_custom_call" | custom-call | flops 1107296256 | bytes 2621440 | tf_op jit(solution)/shard_map/feed_grads/pallas_call | solution.py:674
  312.8 4.4 add_convert_fusion.1
  317.2 24.0 %collective-permute-done.25 = bf16[128,2048]{1,0:T(8,128)(2,1)} collective-permute-done((bf16[128,2048]{1,0:T(8,128)(2,1)}, bf16[128,2048]{1,0:T(8,128)(2,1)}, u32[]{:S(2)}, u32[]{:S(2)}) %collective-permute-start.25) | collective-permute-done | bytes 524320 | tf_op jit(solution)/shard_map/ppermute | solution.py:883
  348.0 4.0 collective-permute-start.28
  352.1 9.4 %collective-permute-done.29 = bf16[128,2048]{1,0:T(8,128)(2,1)S(1)} collective-permute-done((bf16[128,2048]{1,0:T(8,128)(2,1)S(1)}, bf16[128,2048]{1,0:T(8,128)(2,1)S(1)}, u32[]{:S(2)}, u32[]{:S(2)}) %collective-permute-start.29) | collective-permute-done | bytes 524320 | tf_op jit(solution)/shard_map/ppermute | solution.py:920
  363.5 12.9 %collective-permute-done.30 = bf16[128,2048]{1,0:T(8,128)(2,1)S(1)} collective-permute-done((bf16[128,2048]{1,0:T(8,128)(2,1)S(1)}, bf16[128,2048]{1,0:T(8,128)(2,1)S(1)}, u32[]{:S(2)}, u32[]{:S(2)}) %collective-permute-start.30) | collective-permute-done | bytes 524320 | tf_op jit(solution)/shard_map/ppermute | solution.py:920
  378.5 11.3 %collective-permute-done.31 = bf16[128,2048]{1,0:T(8,128)(2,1)S(1)} collective-permute-done((bf16[128,2048]{1,0:T(8,128)(2,1)S(1)}, bf16[128,2048]{1,0:T(8,128)(2,1)S(1)}, u32[]{:S(2)}, u32[]{:S(2)}) %collective-permute-start.31) | collective-permute-done | bytes 524320 | tf_op jit(solution)/shard_map/ppermute | solution.py:920
  393.2 3.8 collective-permute-done.34.d_other_ref
  397.2 4.2 collective-permute-start.35
  401.9 37.5 %mixer_backward.1 = (bf16[1024,1664]{1,0:T(8,128)(2,1)}, f32[8,1024]{1,0:T(8,128)S(1)}, f32[8,128]{1,0:T(8,128)S(1)}, f32[8,256]{1,0:T(8,128)S(1)}) custom-call(s32[8]{0:T(128)S(1)} %fusion.23.order_ref, f32[1024,1152]{1,0:T(8,128)} %fusion.38.pre_ref.before_ref, f32[1024,1152]{1,0:T(8,128)} %fusion.38.pre_ref.before_ref, f32[8,1024]{1,0:T(8,128)S(1)} %fusion.12.taps_ref, ...), custom_call_target="tpu_custom_call" | custom-call | flops 2000000000 | bytes 2097152 | tf_op jit(solution)/shard_map/mixer_backward/pallas_call | solution.py:363
  439.4 5.8 collective-permute-done.36
  446.3 14.1 %d_normed_rows.1 = (bf16[512,2048]{1,0:T(8,128)(2,1)}, bf16[512,2048]{1,0:T(8,128)(2,1)}, f32[8,2048]{1,0:T(8,128)}) custom-call(bf16[1024,1664]{1,0:T(8,128)(2,1)} %get-tuple-element.137.mix_ref, bf16[1024,2048]{1,0:T(8,128)(2,1)} %copy-done.3, bf16[2048,1152]{1,0:T(8,128)(2,1)} %constant_dynamic-update-slice_fusion.2.weights_ref, ...), custom_call_target="tpu_custom_call" | custom-call | flops 872415232 | bytes 2097152 | tf_op jit(solution)/shard_map/d_normed_rows/pallas_call | solution.py:716
  473.8 3.4 collective-permute-start.47
  483.2 15.3 %mix_grads.1 = bf16[2048,2176]{1,0:T(8,128)(2,1)} custom-call(bf16[1024,2048]{1,0:T(8,128)(2,1)} %copy-done.3, bf16[1024,1664]{1,0:T(8,128)(2,1)} %get-tuple-element.137.mix_ref, bf16[512,2048]{1,0:T(8,128)(2,1)} %copy-done.6, bf16[512,2048]{1,0:T(8,128)(2,1)} %copy-done.10, bf16[1024,512]{1,0:T(8,128)(2,1)} %get-tuple-element.140.heads_ref, ...), custom_call_target="tpu_custom_call" | custom-call | flops 1140850688 | bytes 2621440 | tf_op jit(solution)/shard_map/mix_grads/pallas_call | solution.py:755
  498.5 25.4 %collective-permute-done.43 = bf16[128,2048]{1,0:T(8,128)(2,1)S(1)} collective-permute-done((bf16[128,2048]{1,0:T(8,128)(2,1)}, bf16[128,2048]{1,0:T(8,128)(2,1)S(1)}, u32[]{:S(2)}, u32[]{:S(2)}) %collective-permute-start.43) | collective-permute-done | bytes 524320 | tf_op jit(solution)/shard_map/ppermute | solution.py:883
  528.6 3.6 collective-permute-start.48
  538.7 4.7 collective-permute-done.48
  544.0 4.2 collective-permute-done.51
  553.0 7.4 %collective-permute-done.38 = bf16[128,2048]{1,0:T(8,128)(2,1)} collective-permute-done((bf16[128,2048]{1,0:T(8,128)(2,1)}, bf16[128,2048]{1,0:T(8,128)(2,1)}, u32[]{:S(2)}, u32[]{:S(2)}) %collective-permute-start.38) | collective-permute-done | bytes 524320 | tf_op jit(solution)/shard_map/ppermute | solution.py:930
  563.0 4.0 collective-permute-done.52
  568.3 14.4 %collective-permute-done.39 = bf16[128,2048]{1,0:T(8,128)(2,1)S(1)} collective-permute-done((bf16[128,2048]{1,0:T(8,128)(2,1)}, bf16[128,2048]{1,0:T(8,128)(2,1)S(1)}, u32[]{:S(2)}, u32[]{:S(2)}) %collective-permute-start.39) | collective-permute-done | bytes 524320 | tf_op jit(solution)/shard_map/ppermute | solution.py:930
  585.8 6.3 finish_wide.1
  592.1 22.5 %collective-permute-done.53 = bf16[128,2048]{1,0:T(8,128)(2,1)S(1)} collective-permute-done((bf16[128,2048]{1,0:T(8,128)(2,1)S(1)}, bf16[128,2048]{1,0:T(8,128)(2,1)S(1)}, u32[]{:S(2)}, u32[]{:S(2)}) %collective-permute-start.53) | collective-permute-done | bytes 524320 | tf_op jit(solution)/shard_map/ppermute | solution.py:920
  632.5 5.9 finish_mix.1
  (307 shorter events, 143.8 us)
Async XLA Ops:
  7.2 129.9 %all-gather.3.cloned.1.call-start = ((), (), s32[]{:S(2)}) async-start(), calls=%async_computation.2 | async-start | bytes 5242880 | tf_op jit(solution)/shard_map/all_gather | solution.py:1041
  31.2 29.9 %collective-permute-start.5 = (bf16[512,2048]{1,0:T(8,128)(2,1)}, bf16[512,2048]{1,0:T(8,128)(2,1)}, u32[]{:S(2)}, u32[]{:S(2)}) collective-permute-start(bf16[512,2048]{1,0:T(8,128)(2,1)} %get-tuple-element.95), channel_id=1, source_target_pairs={{0,4},{4,0},{1,5},{5,1},{2,6},{6,2},{3,7},{7,3},{8,12},{12,8},{9,1... | collective-permute-start | bytes 6291464 | tf_op jit(solution)/shard_map/ppermute | solution.py:854
  33.6 27.5 %collective-permute-start.3 = (bf16[512,1152]{1,0:T(8,128)(2,1)S(1)}, bf16[512,1152]{1,0:T(8,128)(2,1)S(1)}, u32[]{:S(2)}, u32[]{:S(2)}) collective-permute-start(bf16[512,1152]{1,0:T(8,128)(2,1)S(1)} %copy-done.12), channel_id=1, source_target_pairs={{0,8},{8,0},{16,24},{24,16},{1,9},{9,1},{17,25},{25,17},{2,10},{10... | collective-permute-start | bytes 3538952 | tf_op jit(solution)/shard_map/ppermute | solution.py:850
  33.8 27.3 %collective-permute-start.4 = (bf16[512,1152]{1,0:T(8,128)(2,1)S(1)}, bf16[512,1152]{1,0:T(8,128)(2,1)S(1)}, u32[]{:S(2)}, u32[]{:S(2)}) collective-permute-start(bf16[512,1152]{1,0:T(8,128)(2,1)S(1)} %copy-done.12), channel_id=1, source_target_pairs={{0,16},{8,24},{16,0},{24,8},{1,17},{9,25},{17,1},{25,9},{2,18},{10... | collective-permute-start | bytes 3538952 | tf_op jit(solution)/shard_map/ppermute | solution.py:850
  61.9 14.0 %collective-permute-start.6 = (bf16[256,1152]{1,0:T(8,128)(2,1)}, bf16[256,1152]{1,0:T(8,128)(2,1)}, u32[]{:S(2)}, u32[]{:S(2)}) collective-permute-start(bf16[256,1152]{1,0:T(8,128)(2,1)} %slice.249), channel_id=1, source_target_pairs={{0,16},{8,24},{16,0},{24,8},{1,17},{9,25},{17,1},{25,9},{2,18},{10... | collective-permute-start | bytes 1769480 | tf_op jit(solution)/shard_map/ppermute | solution.py:850
  65.8 13.7 %collective-permute-start.7 = (bf16[256,1152]{1,0:T(8,128)(2,1)S(1)}, bf16[256,1152]{1,0:T(8,128)(2,1)S(1)}, u32[]{:S(2)}, u32[]{:S(2)}) collective-permute-start(bf16[256,1152]{1,0:T(8,128)(2,1)S(1)} %slice.250), channel_id=1, source_target_pairs={{0,8},{8,0},{16,24},{24,16},{1,9},{9,1},{17,25},{25,17},{2,10},{10... | collective-permute-start | bytes 1769480 | tf_op jit(solution)/shard_map/ppermute | solution.py:850
  80.4 169.9 %all-gather.5.cloned.1.call-start = ((), (), s32[]{:S(2)}) async-start(), calls=%async_computation.3 | async-start | bytes 11796480 | tf_op jit(solution)/shard_map/all_gather | solution.py:1044
  94.0 352.3 %reduce-scatter.3.cloned.1.call-start = ((), (), s32[]{:S(2)}) async-start(), calls=%async_computation.4 | async-start | bytes 11141120 | tf_op jit(solution)/shard_map/reduce_scatter | solution.py:876
  157.2 14.1 %collective-permute-start.9 = (bf16[128,2048]{1,0:T(8,128)(2,1)S(1)}, bf16[128,2048]{1,0:T(8,128)(2,1)S(1)}, u32[]{:S(2)}, u32[]{:S(2)}) collective-permute-start(bf16[128,2048]{1,0:T(8,128)(2,1)S(1)} %get-tuple-element.270), channel_id=1, source_target_pairs={{0,1},{4,5},{8,9},{12,13},{16,17},{20,21},{24,25},{28,29}} | collective-permute-start | bytes 1572872 | tf_op jit(solution)/shard_map/ppermute | solution.py:906
  171.7 14.3 %collective-permute-start.10 = (bf16[128,2048]{1,0:T(8,128)(2,1)S(1)}, bf16[128,2048]{1,0:T(8,128)(2,1)S(1)}, u32[]{:S(2)}, u32[]{:S(2)}) collective-permute-start(bf16[128,2048]{1,0:T(8,128)(2,1)S(1)} %get-tuple-element.268), channel_id=1, source_target_pairs={{0,1},{1,2},{4,5},{5,6},{8,9},{9,10},{12,13},{13,14},{16,17},{17,1... | collective-permute-start | bytes 1572872 | tf_op jit(solution)/shard_map/ppermute | solution.py:906
  175.9 10.1 %collective-permute-start.13 = (bf16[128,2048]{1,0:T(8,128)(2,1)S(1)}, bf16[128,2048]{1,0:T(8,128)(2,1)S(1)}, u32[]{:S(2)}, u32[]{:S(2)}) collective-permute-start(bf16[128,2048]{1,0:T(8,128)(2,1)S(1)} %get-tuple-element.269), channel_id=1, source_target_pairs={{2,1},{3,2},{6,5},{7,6},{10,9},{11,10},{14,13},{15,14},{18,17},{19... | collective-permute-start | bytes 1572872 | tf_op jit(solution)/shard_map/ppermute | solution.py:907
  187.3 15.8 %collective-permute-start.11 = (bf16[128,2048]{1,0:T(8,128)(2,1)}, bf16[128,2048]{1,0:T(8,128)(2,1)S(1)}, u32[]{:S(2)}, u32[]{:S(2)}) collective-permute-start(bf16[128,2048]{1,0:T(8,128)(2,1)} %get-tuple-element.266), channel_id=1, source_target_pairs={{0,1},{1,2},{2,3},{4,5},{5,6},{6,7},{8,9},{9,10},{10,11},{12,13},{... | collective-permute-start | bytes 1572872 | tf_op jit(solution)/shard_map/ppermute | solution.py:906
  193.8 13.2 %collective-permute-start.14 = (bf16[128,2048]{1,0:T(8,128)(2,1)}, bf16[128,2048]{1,0:T(8,128)(2,1)}, u32[]{:S(2)}, u32[]{:S(2)}) collective-permute-start(bf16[128,2048]{1,0:T(8,128)(2,1)} %get-tuple-element.267), channel_id=1, source_target_pairs={{1,0},{2,1},{3,2},{5,4},{6,5},{7,6},{9,8},{10,9},{11,10},{13,12},{... | collective-permute-start | bytes 1572872 | tf_op jit(solution)/shard_map/ppermute | solution.py:907
  209.0 12.0 %collective-permute-start.16 = (bf16[128,2048]{1,0:T(8,128)(2,1)S(1)}, bf16[128,2048]{1,0:T(8,128)(2,1)S(1)}, u32[]{:S(2)}, u32[]{:S(2)}) collective-permute-start(bf16[128,2048]{1,0:T(8,128)(2,1)S(1)} %multiply_convert_fusion.1), channel_id=1, source_target_pairs={{1,0},{2,1},{3,2},{5,4},{6,5},{7,6},{9,8},{10,9},{11,10},{13,12},{... | collective-permute-start | bytes 1572872 | tf_op jit(solution)/shard_map/ppermute | solution.py:920
  210.3 12.0 %collective-permute-start.15 = (bf16[128,2048]{1,0:T(8,128)(2,1)S(1)}, bf16[128,2048]{1,0:T(8,128)(2,1)S(1)}, u32[]{:S(2)}, u32[]{:S(2)}) collective-permute-start(bf16[128,2048]{1,0:T(8,128)(2,1)S(1)} %multiply_convert_fusion.1), channel_id=1, source_target_pairs={{0,1},{1,2},{2,3},{4,5},{5,6},{6,7},{8,9},{9,10},{10,11},{12,13},{... | collective-permute-start | bytes 1572872 | tf_op jit(solution)/shard_map/ppermute | solution.py:918
  221.0 11.2 %collective-permute-start.17 = (bf16[128,2048]{1,0:T(8,128)(2,1)S(1)}, bf16[128,2048]{1,0:T(8,128)(2,1)S(1)}, u32[]{:S(2)}, u32[]{:S(2)}) collective-permute-start(bf16[128,2048]{1,0:T(8,128)(2,1)S(1)} %collective-permute-done.16), channel_id=1, source_target_pairs={{1,0},{2,1},{5,4},{6,5},{9,8},{10,9},{13,12},{14,13},{17,16},{18,1... | collective-permute-start | bytes 1572872 | tf_op jit(solution)/shard_map/ppermute | solution.py:920
  222.3 11.2 %collective-permute-start.19 = (bf16[128,2048]{1,0:T(8,128)(2,1)S(1)}, bf16[128,2048]{1,0:T(8,128)(2,1)S(1)}, u32[]{:S(2)}, u32[]{:S(2)}) collective-permute-start(bf16[128,2048]{1,0:T(8,128)(2,1)S(1)} %collective-permute-done.15), channel_id=1, source_target_pairs={{1,2},{2,3},{5,6},{6,7},{9,10},{10,11},{13,14},{14,15},{17,18},{18... | collective-permute-start | bytes 1572872 | tf_op jit(solution)/shard_map/ppermute | solution.py:918
  232.2 10.4 %collective-permute-start.18 = (bf16[128,2048]{1,0:T(8,128)(2,1)S(1)}, bf16[128,2048]{1,0:T(8,128)(2,1)S(1)}, u32[]{:S(2)}, u32[]{:S(2)}) collective-permute-start(bf16[128,2048]{1,0:T(8,128)(2,1)S(1)} %collective-permute-done.17), channel_id=1, source_target_pairs={{1,0},{5,4},{9,8},{13,12},{17,16},{21,20},{25,24},{29,28}} | collective-permute-start | bytes 1572872 | tf_op jit(solution)/shard_map/ppermute | solution.py:920
  234.2 16.1 %collective-permute-start.22 = (bf16[512,2048]{1,0:T(8,128)(2,1)S(1)}, bf16[512,2048]{1,0:T(8,128)(2,1)}, u32[]{:S(2)}, u32[]{:S(2)}) collective-permute-start(bf16[512,2048]{1,0:T(8,128)(2,1)S(1)} %copy-done.11), channel_id=1, source_target_pairs={{0,4},{4,0},{1,5},{5,1},{2,6},{6,2},{3,7},{7,3},{8,12},{12,8},{9,1... | collective-permute-start | bytes 6291464 | tf_op jit(solution)/shard_map/ppermute | solution.py:854
  271.3 17.3 %collective-permute-start.23 = (bf16[512,2048]{1,0:T(8,128)(2,1)}, bf16[512,2048]{1,0:T(8,128)(2,1)S(1)}, u32[]{:S(2)}, u32[]{:S(2)}) collective-permute-start(bf16[512,2048]{1,0:T(8,128)(2,1)} %get-tuple-element.111), channel_id=1, source_target_pairs={{0,4},{4,0},{1,5},{5,1},{2,6},{6,2},{3,7},{7,3},{8,12},{12,8},{9,1... | collective-permute-start | bytes 6291464 | tf_op jit(solution)/shard_map/ppermute | solution.py:854
  291.0 21.8 %collective-permute-start.27 = (bf16[512,2048]{1,0:T(8,128)(2,1)}, bf16[512,2048]{1,0:T(8,128)(2,1)}, u32[]{:S(2)}, u32[]{:S(2)}) collective-permute-start(bf16[512,2048]{1,0:T(8,128)(2,1)} %get-tuple-element.118), channel_id=1, source_target_pairs={{0,4},{4,0},{1,5},{5,1},{2,6},{6,2},{3,7},{7,3},{8,12},{12,8},{9,1... | collective-permute-start | bytes 6291464 | tf_op jit(solution)/shard_map/ppermute | solution.py:854
  293.5 23.7 %collective-permute-start.24 = (bf16[128,2048]{1,0:T(8,128)(2,1)}, bf16[128,2048]{1,0:T(8,128)(2,1)S(1)}, u32[]{:S(2)}, u32[]{:S(2)}) collective-permute-start(bf16[128,2048]{1,0:T(8,128)(2,1)} %get-tuple-element.265), channel_id=1, source_target_pairs={{0,3},{1,0},{2,1},{3,2},{4,7},{5,4},{6,5},{7,6},{8,11},{9,8},{10,9... | collective-permute-start | bytes 1572872 | tf_op jit(solution)/shard_map/ppermute | solution.py:883
  297.0 44.3 %collective-permute-start.25 = (bf16[128,2048]{1,0:T(8,128)(2,1)}, bf16[128,2048]{1,0:T(8,128)(2,1)}, u32[]{:S(2)}, u32[]{:S(2)}) collective-permute-start(bf16[128,2048]{1,0:T(8,128)(2,1)} %get-tuple-element.264), channel_id=1, source_target_pairs={{0,2},{1,3},{2,0},{3,1},{4,6},{5,7},{6,4},{7,5},{8,10},{9,11},{10,... | collective-permute-start | bytes 1572872 | tf_op jit(solution)/shard_map/ppermute | solution.py:883
  297.0 44.3 %collective-permute-start.26 = (bf16[128,2048]{1,0:T(8,128)(2,1)}, bf16[128,2048]{1,0:T(8,128)(2,1)}, u32[]{:S(2)}, u32[]{:S(2)}) collective-permute-start(bf16[128,2048]{1,0:T(8,128)(2,1)} %get-tuple-element.263), channel_id=1, source_target_pairs={{0,1},{1,2},{2,3},{3,0},{4,5},{5,6},{6,7},{7,4},{8,9},{9,10},{10,1... | collective-permute-start | bytes 1572872 | tf_op jit(solution)/shard_map/ppermute | solution.py:883
  341.3 274.7 %reduce-scatter.5.cloned.1.call-start = ((), (), s32[]{:S(2)}) async-start(), calls=%async_computation.5 | async-start | bytes 11141120 | tf_op jit(solution)/shard_map/reduce_scatter | solution.py:876
  346.7 14.7 %collective-permute-start.29 = (bf16[128,2048]{1,0:T(8,128)(2,1)S(1)}, bf16[128,2048]{1,0:T(8,128)(2,1)S(1)}, u32[]{:S(2)}, u32[]{:S(2)}) collective-permute-start(bf16[128,2048]{1,0:T(8,128)(2,1)S(1)} %get-tuple-element.245), channel_id=1, source_target_pairs={{1,0},{2,1},{3,2},{5,4},{6,5},{7,6},{9,8},{10,9},{11,10},{13,12},{... | collective-permute-start | bytes 1572872 | tf_op jit(solution)/shard_map/ppermute | solution.py:920
  348.0 14.7 %collective-permute-start.28 = (bf16[128,2048]{1,0:T(8,128)(2,1)S(1)}, bf16[128,2048]{1,0:T(8,128)(2,1)S(1)}, u32[]{:S(2)}, u32[]{:S(2)}) collective-permute-start(bf16[128,2048]{1,0:T(8,128)(2,1)S(1)} %get-tuple-element.245), channel_id=1, source_target_pairs={{0,1},{1,2},{2,3},{4,5},{5,6},{6,7},{8,9},{9,10},{10,11},{12,13},{... | collective-permute-start | bytes 1572872 | tf_op jit(solution)/shard_map/ppermute | solution.py:918
  361.5 14.9 %collective-permute-start.30 = (bf16[128,2048]{1,0:T(8,128)(2,1)S(1)}, bf16[128,2048]{1,0:T(8,128)(2,1)S(1)}, u32[]{:S(2)}, u32[]{:S(2)}) collective-permute-start(bf16[128,2048]{1,0:T(8,128)(2,1)S(1)} %collective-permute-done.29), channel_id=1, source_target_pairs={{1,0},{2,1},{5,4},{6,5},{9,8},{10,9},{13,12},{14,13},{17,16},{18,1... | collective-permute-start | bytes 1572872 | tf_op jit(solution)/shard_map/ppermute | solution.py:920
  362.8 14.9 %collective-permute-start.32 = (bf16[128,2048]{1,0:T(8,128)(2,1)S(1)}, bf16[128,2048]{1,0:T(8,128)(2,1)S(1)}, u32[]{:S(2)}, u32[]{:S(2)}) collective-permute-start(bf16[128,2048]{1,0:T(8,128)(2,1)S(1)} %collective-permute-done.28), channel_id=1, source_target_pairs={{1,2},{2,3},{5,6},{6,7},{9,10},{10,11},{13,14},{14,15},{17,18},{18... | collective-permute-start | bytes 1572872 | tf_op jit(solution)/shard_map/ppermute | solution.py:918
  376.3 13.4 %collective-permute-start.31 = (bf16[128,2048]{1,0:T(8,128)(2,1)S(1)}, bf16[128,2048]{1,0:T(8,128)(2,1)S(1)}, u32[]{:S(2)}, u32[]{:S(2)}) collective-permute-start(bf16[128,2048]{1,0:T(8,128)(2,1)S(1)} %collective-permute-done.30), channel_id=1, source_target_pairs={{1,0},{5,4},{9,8},{13,12},{17,16},{21,20},{25,24},{29,28}} | collective-permute-start | bytes 1572872 | tf_op jit(solution)/shard_map/ppermute | solution.py:920
  377.6 12.3 %collective-permute-start.33 = (bf16[128,2048]{1,0:T(8,128)(2,1)S(1)}, bf16[128,2048]{1,0:T(8,128)(2,1)S(1)}, u32[]{:S(2)}, u32[]{:S(2)}) collective-permute-start(bf16[128,2048]{1,0:T(8,128)(2,1)S(1)} %collective-permute-done.32), channel_id=1, source_target_pairs={{2,3},{6,7},{10,11},{14,15},{18,19},{22,23},{26,27},{30,31}} | collective-permute-start | bytes 1572872 | tf_op jit(solution)/shard_map/ppermute | solution.py:918
  397.2 42.2 %collective-permute-start.35 = (bf16[128,2048]{1,0:T(8,128)(2,1)S(1)}, bf16[128,2048]{1,0:T(8,128)(2,1)S(1)}, u32[]{:S(2)}, u32[]{:S(2)}) collective-permute-start(bf16[128,2048]{1,0:T(8,128)(2,1)S(1)} %get-tuple-element.262), channel_id=1, source_target_pairs={{0,3},{1,0},{2,1},{3,2},{4,7},{5,4},{6,5},{7,6},{8,11},{9,8},{10,9... | collective-permute-start | bytes 1572872 | tf_op jit(solution)/shard_map/ppermute | solution.py:883
  401.3 43.8 %collective-permute-start.36 = (bf16[128,2048]{1,0:T(8,128)(2,1)S(1)}, bf16[128,2048]{1,0:T(8,128)(2,1)S(1)}, u32[]{:S(2)}, u32[]{:S(2)}) collective-permute-start(bf16[128,2048]{1,0:T(8,128)(2,1)S(1)} %get-tuple-element.261), channel_id=1, source_target_pairs={{0,2},{1,3},{2,0},{3,1},{4,6},{5,7},{6,4},{7,5},{8,10},{9,11},{10,... | collective-permute-start | bytes 1572872 | tf_op jit(solution)/shard_map/ppermute | solution.py:883
  401.3 43.8 %collective-permute-start.37 = (bf16[128,2048]{1,0:T(8,128)(2,1)S(1)}, bf16[128,2048]{1,0:T(8,128)(2,1)S(1)}, u32[]{:S(2)}, u32[]{:S(2)}) collective-permute-start(bf16[128,2048]{1,0:T(8,128)(2,1)S(1)} %get-tuple-element.260), channel_id=1, source_target_pairs={{0,1},{1,2},{2,3},{3,0},{4,5},{5,6},{6,7},{7,4},{8,9},{9,10},{10,1... | collective-permute-start | bytes 1572872 | tf_op jit(solution)/shard_map/ppermute | solution.py:883
  478.3 20.2 %collective-permute-start.42 = (bf16[128,2048]{1,0:T(8,128)(2,1)}, bf16[128,2048]{1,0:T(8,128)(2,1)S(1)}, u32[]{:S(2)}, u32[]{:S(2)}) collective-permute-start(bf16[128,2048]{1,0:T(8,128)(2,1)} %get-tuple-element.259), channel_id=1, source_target_pairs={{0,3},{1,0},{2,1},{3,2},{4,7},{5,4},{6,5},{7,6},{8,11},{9,8},{10,9... | collective-permute-start | bytes 1572872 | tf_op jit(solution)/shard_map/ppermute | solution.py:883
  478.5 45.4 %collective-permute-start.43 = (bf16[128,2048]{1,0:T(8,128)(2,1)}, bf16[128,2048]{1,0:T(8,128)(2,1)S(1)}, u32[]{:S(2)}, u32[]{:S(2)}) collective-permute-start(bf16[128,2048]{1,0:T(8,128)(2,1)} %get-tuple-element.258), channel_id=1, source_target_pairs={{0,2},{1,3},{2,0},{3,1},{4,6},{5,7},{6,4},{7,5},{8,10},{9,11},{10,... | collective-permute-start | bytes 1572872 | tf_op jit(solution)/shard_map/ppermute | solution.py:883
  479.5 44.4 %collective-permute-start.44 = (bf16[128,2048]{1,0:T(8,128)(2,1)}, bf16[128,2048]{1,0:T(8,128)(2,1)}, u32[]{:S(2)}, u32[]{:S(2)}) collective-permute-start(bf16[128,2048]{1,0:T(8,128)(2,1)} %get-tuple-element.257), channel_id=1, source_target_pairs={{0,1},{1,2},{2,3},{3,0},{4,5},{5,6},{6,7},{7,4},{8,9},{9,10},{10,1... | collective-permute-start | bytes 1572872 | tf_op jit(solution)/shard_map/ppermute | solution.py:883
  528.6 14.7 %collective-permute-start.48 = (bf16[128,2048]{1,0:T(8,128)(2,1)}, bf16[128,2048]{1,0:T(8,128)(2,1)S(1)}, u32[]{:S(2)}, u32[]{:S(2)}) collective-permute-start(bf16[128,2048]{1,0:T(8,128)(2,1)} %get-tuple-element.244), channel_id=1, source_target_pairs={{0,1},{1,2},{2,3},{4,5},{5,6},{6,7},{8,9},{9,10},{10,11},{12,13},{... | collective-permute-start | bytes 1572872 | tf_op jit(solution)/shard_map/ppermute | solution.py:918
  532.3 15.9 %collective-permute-start.51 = (bf16[128,2048]{1,0:T(8,128)(2,1)}, bf16[128,2048]{1,0:T(8,128)(2,1)S(1)}, u32[]{:S(2)}, u32[]{:S(2)}) collective-permute-start(bf16[128,2048]{1,0:T(8,128)(2,1)} %get-tuple-element.244), channel_id=1, source_target_pairs={{1,0},{2,1},{3,2},{5,4},{6,5},{7,6},{9,8},{10,9},{11,10},{13,12},{... | collective-permute-start | bytes 1572872 | tf_op jit(solution)/shard_map/ppermute | solution.py:920
  533.6 50.8 %collective-permute-start.54 = (bf16[512,2176]{1,0:T(8,128)(2,1)}, bf16[512,2176]{1,0:T(8,128)(2,1)S(1)}, u32[]{:S(2)}, u32[]{:S(2)}) collective-permute-start(bf16[512,2176]{1,0:T(8,128)(2,1)} %reduce-scatter.3.cloned.1.call-done.own_ref), channel_id=1, source_target_pairs={{0,4},{4,0},{1,5},{5,1},{2,6},{6,2},{3,7},{7,3},{8,12},{12,8},{9,1... | collective-permute-start | bytes 6684680 | tf_op jit(solution)/shard_map/ppermute | solution.py:854
  534.4 26.0 %collective-permute-start.38 = (bf16[128,2048]{1,0:T(8,128)(2,1)}, bf16[128,2048]{1,0:T(8,128)(2,1)}, u32[]{:S(2)}, u32[]{:S(2)}) collective-permute-start(bf16[128,2048]{1,0:T(8,128)(2,1)} %add_convert_fusion.4), channel_id=1, source_target_pairs={{0,1},{1,2},{2,3},{3,0},{4,5},{5,6},{6,7},{7,4},{8,9},{9,10},{10,1... | collective-permute-start | bytes 1572872 | tf_op jit(solution)/shard_map/ppermute | solution.py:930
  537.2 45.5 %collective-permute-start.39 = (bf16[128,2048]{1,0:T(8,128)(2,1)}, bf16[128,2048]{1,0:T(8,128)(2,1)S(1)}, u32[]{:S(2)}, u32[]{:S(2)}) collective-permute-start(bf16[128,2048]{1,0:T(8,128)(2,1)} %add_convert_fusion.4), channel_id=1, source_target_pairs={{0,2},{1,3},{2,0},{3,1},{4,6},{5,7},{6,4},{7,5},{8,10},{9,11},{10,... | collective-permute-start | bytes 1572872 | tf_op jit(solution)/shard_map/ppermute | solution.py:930
  543.4 18.9 %collective-permute-start.49 = (bf16[128,2048]{1,0:T(8,128)(2,1)S(1)}, bf16[128,2048]{1,0:T(8,128)(2,1)S(1)}, u32[]{:S(2)}, u32[]{:S(2)}) collective-permute-start(bf16[128,2048]{1,0:T(8,128)(2,1)S(1)} %collective-permute-done.48), channel_id=1, source_target_pairs={{1,2},{2,3},{5,6},{6,7},{9,10},{10,11},{13,14},{14,15},{17,18},{18... | collective-permute-start | bytes 1572872 | tf_op jit(solution)/shard_map/ppermute | solution.py:918
  548.2 18.8 %collective-permute-start.52 = (bf16[128,2048]{1,0:T(8,128)(2,1)S(1)}, bf16[128,2048]{1,0:T(8,128)(2,1)S(1)}, u32[]{:S(2)}, u32[]{:S(2)}) collective-permute-start(bf16[128,2048]{1,0:T(8,128)(2,1)S(1)} %collective-permute-done.51), channel_id=1, source_target_pairs={{1,0},{2,1},{5,4},{6,5},{9,8},{10,9},{13,12},{14,13},{17,16},{18,1... | collective-permute-start | bytes 1572872 | tf_op jit(solution)/shard_map/ppermute | solution.py:920
  560.4 23.2 %collective-permute-start.40 = (bf16[128,2048]{1,0:T(8,128)(2,1)}, bf16[128,2048]{1,0:T(8,128)(2,1)S(1)}, u32[]{:S(2)}, u32[]{:S(2)}) collective-permute-start(bf16[128,2048]{1,0:T(8,128)(2,1)} %add_convert_fusion.4), channel_id=1, source_target_pairs={{0,3},{1,0},{2,1},{3,2},{4,7},{5,4},{6,5},{7,6},{8,11},{9,8},{10,9... | collective-permute-start | bytes 1572872 | tf_op jit(solution)/shard_map/ppermute | solution.py:930
  562.3 29.8 %collective-permute-start.50 = (bf16[128,2048]{1,0:T(8,128)(2,1)S(1)}, bf16[128,2048]{1,0:T(8,128)(2,1)S(1)}, u32[]{:S(2)}, u32[]{:S(2)}) collective-permute-start(bf16[128,2048]{1,0:T(8,128)(2,1)S(1)} %collective-permute-done.49), channel_id=1, source_target_pairs={{2,3},{6,7},{10,11},{14,15},{18,19},{22,23},{26,27},{30,31}} | collective-permute-start | bytes 1572872 | tf_op jit(solution)/shard_map/ppermute | solution.py:918
  567.0 47.6 %collective-permute-start.53 = (bf16[128,2048]{1,0:T(8,128)(2,1)S(1)}, bf16[128,2048]{1,0:T(8,128)(2,1)S(1)}, u32[]{:S(2)}, u32[]{:S(2)}) collective-permute-start(bf16[128,2048]{1,0:T(8,128)(2,1)S(1)} %collective-permute-done.52), channel_id=1, source_target_pairs={{1,0},{5,4},{9,8},{13,12},{17,16},{21,20},{25,24},{29,28}} | collective-permute-start | bytes 1572872 | tf_op jit(solution)/shard_map/ppermute | solution.py:920
  616.0 11.9 %collective-permute-start.55 = (bf16[512,2176]{1,0:T(8,128)(2,1)}, bf16[512,2176]{1,0:T(8,128)(2,1)S(1)}, u32[]{:S(2)}, u32[]{:S(2)}) collective-permute-start(bf16[512,2176]{1,0:T(8,128)(2,1)} %reduce-scatter.5.cloned.1.call-done.a_ref), channel_id=1, source_target_pairs={{0,4},{4,0},{1,5},{5,1},{2,6},{6,2},{3,7},{7,3},{8,12},{12,8},{9,1... | collective-permute-start | bytes 6684680 | tf_op jit(solution)/shard_map/ppermute | solution.py:854
  (45 other events, 356.9 us)
Sparse Core Ops, SparseCore 0:
  80.6 55.6 all-gather.2
  138.6 96.4 all-gather.4
  341.4 91.9 reduce-scatter.2
  524.0 91.9 reduce-scatter.4
where the time goes:
time: 655 us; the launch traced here: 645 us
  waiting for transfers between devices  246 us (38%)
  Pallas kernels  192 us (29%)
  starting transfers between devices  91.5 us (14%)
  local copies, waits for them, and re-layouts  47.4 us (7%)
  other arithmetic  43 us (7%)
  between operations  15.7 us (2%)
  matrix products  9.51 us (1%)
    ppermute x9, waiting for transfers between devices, line_gather(): lax.ppermute(lefts[-1], axis, [(i, i - 1) for i in range(1, size - step +...  83.3 us
    ppermute x9, waiting for transfers between devices, line_sum(): lax.ppermute(value[p * rows:(p + 1) * rows], axis, [(i, (i - p) % size) f...  55.2 us
    pallas_call x1, Pallas kernels, mixer_forward(): pl.pallas_call(functools.partial(forward_kernel, heads, key_dim, val_dim)...  39.4 us
    pallas_call x1, Pallas kernels, mixer_backward(): pl.pallas_call(functools.partial(backward_kernel, heads, key_dim, val_dim...  37.5 us
    pallas_call x2, Pallas kernels, feed_forward(): pl.pallas_call(feed_kernel, grid=(count // TILE,), in_specs=[row, row, pl...  33.8 us
    ppermute x7, waiting for transfers between devices, across(): return lax.ppermute(value, 'fsdp', [(i, i ^ flip) for i in range(4)])  32.7 us
    ppermute x3, waiting for transfers between devices, line_sum_hops(): lax.ppermute(send_r.astype(BF16), axis, [(i, i + 1) for i in range(step)])  27.7 us
    ppermute x11, starting transfers between devices, swapped(): return lax.ppermute(value, 'context', [(0, 1), (1, 0)])  22.4 us
  transfers between devices with their start and end apart: 60, of which 30 were waited for; matrix products, arithmetic and copies ran while one was open for 11% of the time, Pallas kernels for 23%

commit v1 on v0

v1 whole, which is shorter than its diff:
```python
import functools
import jax
import jax.numpy as jnp
from jax import lax
from jax.experimental import pallas as pl
from jax.experimental.pallas import tpu as pltpu
from jax.sharding import PartitionSpec as P

F32 = jnp.float32
BF16 = jnp.bfloat16
CHUNK = 128
exact = lax.Precision.HIGHEST
NN = ((1,), (0,))
NT = ((1,), (1,))
TN = ((0,), (0,))


def mm(a, b, dims=NN):
    return lax.dot_general(
        a.astype(BF16), b.astype(BF16), (dims, ((), ())), preferred_element_type=F32
    )


def mm_exact(a, b, dims=NN):
    return lax.dot_general(a, b, (dims, ((), ())), precision=exact, preferred_element_type=F32)


def small_cost():
    return pl.CostEstimate(flops=1, bytes_accessed=1, transcendentals=0)


def grid_ids(size):
    rows = lax.broadcasted_iota(jnp.int32, (size, size), 0)
    cols = lax.broadcasted_iota(jnp.int32, (size, size), 1)
    return rows, cols


def softplus(v):
    return jnp.maximum(v, 0.0) + jnp.log1p(jnp.exp(-jnp.abs(v)))


def rates_of(rates, params, heads, triangle):
    lanes = lax.broadcasted_iota(jnp.int32, rates.shape, 1)
    shifted = rates + params[1:2, :]
    scale = jnp.exp(params[0:1, :])
    logdecay = jnp.where(lanes < heads, -scale * softplus(shifted), 0.0)
    running = mm_exact(triangle, logdecay)
    last = running[CHUNK - 1 : CHUNK, :]
    return (
        jax.nn.sigmoid(rates),
        shifted,
        scale,
        logdecay,
        running,
        jnp.transpose(running),
        jnp.exp(running),
        jnp.exp(last - running),
        jnp.exp(last),
    )


def convolved(window, taps, rows):
    total = taps[0:1, :] * window[5 : 5 + rows, :]
    for j in range(1, 4):
        total = total + taps[j : j + 1, :] * window[5 + j : 5 + j + rows, :]
    return total


PER = 2


def inverses_of(systems, rows, cols):
    eye = (rows == cols).astype(F32)
    near = [jnp.where(rows // 8 == cols // 8, s, 0.0).astype(BF16) for s in systems]
    second = [mm(n, n) for n in near]
    low = [s.astype(BF16) for s in second]
    third = [mm(s, n) for s, n in zip(low, near)]
    fourth = [mm(s, s) for s in low]
    partial = [eye - n.astype(F32) + s - t for n, s, t in zip(near, second, third)]
    result = [p + mm(p, f) for p, f in zip(partial, fourth)]
    size = 8
    while size < CHUNK:
        step = min(4, CHUNK // size)
        inside = (rows // (step * size) == cols // (step * size)) & (rows // size > cols // size)
        off = [jnp.where(inside, s, 0.0).astype(BF16) for s in systems]
        low = [r.astype(BF16) for r in result]
        reach = [mm(o, r).astype(BF16) for o, r in zip(off, low)]
        twice = [mm(r, r) for r in reach]
        once = [r - mm(x, y) for r, x, y in zip(result, low, reach)]
        result = [o + mm(o, t) for o, t in zip(once, twice)]
        size *= step
    high = [s.astype(BF16) for s in systems]
    rest = [s - h.astype(F32) for s, h in zip(systems, high)]
    low = [r.astype(BF16) for r in result]
    tail = [r - x.astype(F32) for r, x in zip(result, low)]
    left = [
        eye - (r + mm(h, x) + mm(e, x) + mm(h, t))
        for r, h, x, e, t in zip(result, high, low, rest, tail)
    ]
    return [r + mm(x, d) for r, x, d in zip(result, low, left)]


def forward_kernel(heads, key_dim, val_dim, order_ref, *refs):
    pre_refs, refs = refs[:PER], refs[PER:]
    (
        taps_ref, params_ref, mixed_ref, states_ref, inverse_ref, new_ref, active_ref, sigma_ref,
        state, window,
    ) = refs
    step = pl.program_id(0)
    wide = heads * key_dim
    width = window.shape[1]
    span = PER * CHUNK

    @pl.when(step == 0)
    def _():
        state[...] = jnp.zeros_like(state)
        window[0:8, :] = jnp.zeros((8, width), F32)

    for c in range(PER):
        window[8 + c * CHUNK : 8 + (c + 1) * CHUNK, :] = (
            pre_refs[c][:, :width].astype(BF16).astype(F32)
        )
    summed = convolved(window, taps_ref, span)
    window[0:8, :] = window[span : span + 8, :]
    sigma = jax.nn.sigmoid(summed)
    active = summed * sigma
    active_ref[...] = active
    sigma_ref[...] = sigma
    rows, cols = grid_ids(CHUNK)
    causal = rows >= cols
    strict = rows > cols
    triangle = causal.astype(F32)
    rates = [rates_of(pre_refs[c][:, width:], params_ref, heads, triangle) for c in range(PER)]
    chains = [(c, h) for c in range(PER) for h in range(heads)]

    def piece(at, c, h, size):
        return active[c * CHUNK : (c + 1) * CHUNK, at + h * size : at + (h + 1) * size]

    def unit(values, factor):
        return values * (lax.rsqrt(jnp.sum(values * values, -1, keepdims=True) + 1e-6) * factor)

    query = [unit(piece(0, c, h, key_dim), key_dim ** -0.5) for c, h in chains]
    keys = [unit(piece(wide, c, h, key_dim), 1.0) for c, h in chains]
    values = [piece(2 * wide, c, h, val_dim) for c, h in chains]
    beta = [rates[c][0][:, heads + h : heads + h + 1] for c, h in chains]
    decay = [rates[c][6][:, h : h + 1] for c, h in chains]
    ratios = [
        jnp.where(
            causal,
            jnp.exp(jnp.where(causal, rates[c][4][:, h : h + 1] - rates[c][5][h : h + 1, :], 0.0)),
            0.0,
        )
        for c, h in chains
    ]
    dots = [mm(jnp.concatenate([k, q], 0), k, NT) for k, q in zip(keys, query)]
    systems = [
        jnp.where(strict, b * d[:CHUNK] * r, 0.0) for b, d, r in zip(beta, dots, ratios)
    ]
    scores = [(d[CHUNK:] * r).astype(BF16) for d, r in zip(dots, ratios)]
    inverse = [x.astype(BF16) for x in inverses_of(systems, rows, cols)]
    solved = [
        mm(x, jnp.concatenate([(b * e) * k, b * v], 1))
        for x, b, e, k, v in zip(inverse, beta, decay, keys, values)
    ]
    for i, (c, h) in enumerate(chains):
        inverse_ref[(c * heads + h) * CHUNK : (c * heads + h + 1) * CHUNK, :] = inverse[i]
    for c in range(PER):
        place = pl.multiple_of(order_ref[step * PER + c] * CHUNK, CHUNK)
        for h in range(heads):
            i = c * heads + h
            begin = state[h * key_dim : (h + 1) * key_dim, :]
            begin_low = begin.astype(BF16)
            states_ref[(c * heads + h) * key_dim : (c * heads + h + 1) * key_dim, :] = begin_low
            through = mm(
                jnp.concatenate([solved[i][:, :key_dim], query[i] * decay[i]], 0), begin_low
            )
            new = (solved[i][:, key_dim:] - through[:CHUNK]).astype(BF16)
            mixed_ref[pl.ds(place, CHUNK), h * val_dim : (h + 1) * val_dim] = through[
                CHUNK:
            ] + mm(scores[i], new)
            state[h * key_dim : (h + 1) * key_dim, :] = rates[c][8][:, h : h + 1] * begin + mm(
                keys[i] * rates[c][7][:, h : h + 1], new, TN
            )
            new_ref[c * CHUNK : (c + 1) * CHUNK, h * val_dim : (h + 1) * val_dim] = new


def backward_kernel(heads, key_dim, val_dim, order_ref, *refs):
    pre_refs, refs = refs[:PER], refs[PER:]
    active_ref, sigma_ref, taps_ref, params_ref, states_ref, inverse_ref, new_ref = refs[:7]
    mixed_refs, refs = refs[7 : 7 + PER], refs[7 + PER :]
    gates_refs, refs = refs[:PER], refs[PER:]
    own_refs, refs = refs[:PER], refs[PER:]
    other_refs, refs = refs[:PER], refs[PER:]
    (side_ref, gain_ref, d_pre_ref, d_taps_ref, d_params_ref, d_gain_ref, d_state, after) = (
        refs
    )
    step = pl.program_id(0)
    steps = pl.num_programs(0)
    wide = heads * key_dim
    width = after.shape[1]
    span = PER * CHUNK
    first = (steps - 1 - step) * PER

    @pl.when(step == 0)
    def _():
        d_state[...] = jnp.zeros_like(d_state)
        after[span : span + 8, :] = jnp.zeros((8, width), F32)
        d_taps_ref[...] = jnp.zeros_like(d_taps_ref)
        d_params_ref[...] = jnp.zeros_like(d_params_ref)
        d_gain_ref[...] = jnp.zeros_like(d_gain_ref)

    active = active_ref[...]
    sigma = sigma_ref[...]
    slope = sigma + active * (1.0 - sigma)
    rows, cols = grid_ids(CHUNK)
    causal = rows >= cols
    strict = rows > cols
    triangle = causal.astype(F32)
    rates = [rates_of(pre_refs[c][:, width:], params_ref, heads, triangle) for c in range(PER)]
    chains = [(c, h) for c in range(PER) for h in range(heads)]
    places = [pl.multiple_of(order_ref[first + c] * CHUNK, CHUNK) for c in range(PER)]
    d_attn = jnp.concatenate(
        [
            jnp.where(order_ref[first + c] < steps * PER // 2, own_refs[c][...], other_refs[c][...])
            for c in range(PER)
        ],
        0,
    )
    depth = side_ref.shape[2]
    d_heads = mm(d_attn[:, :depth], side_ref[0, 1])
    for f in range(1, side_ref.shape[0]):
        d_heads = d_heads + mm(d_attn[:, f * depth : (f + 1) * depth], side_ref[f, 1])
    gain = gain_ref[...]

    def piece(array, at, c, h, size):
        return array[c * CHUNK : (c + 1) * CHUNK, at + h * size : at + (h + 1) * size]

    def scale_of(values):
        return lax.rsqrt(jnp.sum(values * values, -1, keepdims=True) + 1e-6)

    q_act = [piece(active, 0, c, h, key_dim) for c, h in chains]
    k_act = [piece(active, wide, c, h, key_dim) for c, h in chains]
    values = [piece(active, 2 * wide, c, h, val_dim) for c, h in chains]
    q_scale = [scale_of(x) for x in q_act]
    k_scale = [scale_of(x) for x in k_act]
    q_unit = [x * s for x, s in zip(q_act, q_scale)]
    keys = [x * s for x, s in zip(k_act, k_scale)]
    query = [x * key_dim ** -0.5 for x in q_unit]
    keys_low = [x.astype(BF16) for x in keys]
    query_low = [x.astype(BF16) for x in query]
    beta = [rates[c][0][:, heads + h : heads + h + 1] for c, h in chains]
    decay = [rates[c][6][:, h : h + 1] for c, h in chains]
    remain = [rates[c][7][:, h : h + 1] for c, h in chains]
    whole = [rates[c][8][:, h : h + 1] for c, h in chains]
    lead = [b * e for b, e in zip(beta, decay)]
    ratios = [
        jnp.where(
            causal,
            jnp.exp(jnp.where(causal, rates[c][4][:, h : h + 1] - rates[c][5][h : h + 1, :], 0.0)),
            0.0,
        )
        for c, h in chains
    ]
    d_mixed = []
    for c, h in chains:
        at = slice(h * val_dim, (h + 1) * val_dim)
        mixed = mixed_refs[c][:, at]
        gates = gates_refs[c][:, at]
        d_out = piece(d_heads, 0, c, h, val_dim)
        m_scale = lax.rsqrt(jnp.mean(mixed * mixed, -1, keepdims=True) + 1e-5)
        unit = mixed * m_scale
        g_sigma = jax.nn.sigmoid(gates)
        gated = gates * g_sigma
        weighted = d_out * unit
        d_pre_ref[
            pl.ds(places[c], CHUNK), width + 128 + h * val_dim : width + 128 + (h + 1) * val_dim
        ] = (weighted * gain * (g_sigma * (1.0 + gates * (1.0 - g_sigma)))).astype(BF16)
        d_gain_ref[0:1, :] += jnp.sum(weighted * gated, 0, keepdims=True)
        d_unit = d_out * gated * gain
        d_mixed.append(
            (m_scale * (d_unit - unit * jnp.mean(d_unit * unit, -1, keepdims=True))).astype(BF16)
        )
    dots = [mm(jnp.concatenate([k, q], 0), k, NT) for k, q in zip(keys_low, query_low)]
    weights = [jnp.where(strict, d[:CHUNK] * r, 0.0) for d, r in zip(dots, ratios)]
    scores = [d[CHUNK:] * r for d, r in zip(dots, ratios)]
    begin = [
        states_ref[(c * heads + h) * key_dim : (c * heads + h + 1) * key_dim, :] for c, h in chains
    ]
    inverse = [
        inverse_ref[(c * heads + h) * CHUNK : (c * heads + h + 1) * CHUNK, :] for c, h in chains
    ]
    new = [
        new_ref[c * CHUNK : (c + 1) * CHUNK, h * val_dim : (h + 1) * val_dim] for c, h in chains
    ]
    straight = [mm(s, d, TN) for s, d in zip(scores, d_mixed)]
    kept = [(k * r).astype(BF16) for k, r in zip(keys, remain)]
    both = [mm(x, jnp.concatenate([s.astype(BF16), k], 1), TN) for x, s, k in zip(inverse, straight, kept)]
    fixed = [mm(q * e, d, TN) for q, e, d in zip(query, decay, d_mixed)]
    pull = [(l * k).astype(BF16) for l, k in zip(lead, keys)]
    d_end = [None] * len(chains)
    solved = [None] * len(chains)
    for c in reversed(range(PER)):
        for h in range(heads):
            i = c * heads + h
            at = slice(h * key_dim, (h + 1) * key_dim)
            d_end[i] = d_state[at, :]
            solved[i] = both[i][:, :val_dim] + mm(both[i][:, val_dim:], d_end[i])
            d_state[at, :] = whole[i] * d_end[i] + fixed[i] - mm(pull[i], solved[i], TN)
    end_low = [d.astype(BF16) for d in d_end]
    outer = [
        mm(jnp.concatenate([d, s.astype(BF16)], 0), jnp.concatenate([b, n], 0), NT)
        for d, s, b, n in zip(d_mixed, solved, begin, new)
    ]
    d_kept = [mm(n, d, NT) for n, d in zip(new, end_low)]
    d_scores = [jnp.where(causal, o[:CHUNK, key_dim:], 0.0) for o in outer]
    d_system = [jnp.where(strict, -o[CHUNK:, key_dim:], 0.0) for o in outer]
    d_dots_k = [d * (b * r) for d, b, r in zip(d_system, beta, ratios)]
    d_dots_q = [(d * r).astype(BF16) for d, r in zip(d_scores, ratios)]
    near = [
        mm(jnp.concatenate([q, (k + jnp.transpose(k)).astype(BF16)], 0), low)
        for q, k, low in zip(d_dots_q, d_dots_k, keys_low)
    ]
    far = [mm(q, low, TN) for q, low in zip(d_dots_q, query_low)]
    lanes = lax.broadcasted_iota(jnp.int32, (CHUNK, 128), 1)
    row_ids = lax.broadcasted_iota(jnp.int32, (CHUNK, 1), 0)
    d_running = [jnp.zeros((CHUNK, 128), F32) for _ in range(PER)]
    d_strengths = [jnp.zeros((CHUNK, 128), F32) for _ in range(PER)]
    for i, (c, h) in enumerate(chains):
        d_query_state = outer[i][:CHUNK, :key_dim]
        d_keys_state = outer[i][CHUNK:, :key_dim]
        d_query = decay[i] * d_query_state + near[i][:CHUNK]
        d_keys = near[i][CHUNK:] + far[i] - lead[i] * d_keys_state + remain[i] * d_kept[i]
        along = decay[i] * jnp.sum(keys[i] * d_keys_state, -1, keepdims=True)
        weighed = d_system[i] * weights[i]
        d_beta = (
            jnp.sum(solved[i] * values[i], -1, keepdims=True)
            - along
            + jnp.sum(weighed, -1, keepdims=True)
        )
        joint = weighed * beta[i] + d_scores[i] * scores[i]
        left = remain[i] * jnp.sum(keys[i] * d_kept[i], -1, keepdims=True)
        total = jnp.sum(left, 0, keepdims=True) + whole[i] * jnp.sum(
            jnp.sum(d_end[i] * begin[i].astype(F32), -1, keepdims=True), 0, keepdims=True
        )
        d_run = (
            jnp.sum(joint, -1, keepdims=True)
            - jnp.sum(jnp.transpose(joint), -1, keepdims=True)
            + decay[i] * jnp.sum(query[i] * d_query_state, -1, keepdims=True)
            - beta[i] * along
            - left
            + jnp.where(row_ids == CHUNK - 1, total, 0.0)
        )
        d_running[c] = jnp.where(lanes == h, d_run, d_running[c])
        d_strengths[c] = jnp.where(lanes == heads + h, d_beta, d_strengths[c])
        d_q = d_query * key_dim ** -0.5
        d_q = q_scale[i] * (d_q - q_unit[i] * jnp.sum(q_unit[i] * d_q, -1, keepdims=True))
        d_k = k_scale[i] * (d_keys - keys[i] * jnp.sum(keys[i] * d_keys, -1, keepdims=True))
        here = slice(c * CHUNK, (c + 1) * CHUNK)
        after[here, h * key_dim : (h + 1) * key_dim] = d_q * piece(slope, 0, c, h, key_dim)
        after[here, wide + h * key_dim : wide + (h + 1) * key_dim] = d_k * piece(
            slope, wide, c, h, key_dim
        )
        after[here, 2 * wide + h * val_dim : 2 * wide + (h + 1) * val_dim] = (
            beta[i] * solved[i]
        ) * piece(slope, 2 * wide, c, h, val_dim)
    upper = (rows <= cols).astype(F32)
    for c in range(PER):
        strengths, shifted, scale, logdecay = rates[c][:4]
        d_logdecay = mm_exact(upper, d_running[c])
        d_shifted = jnp.where(lanes < heads, d_logdecay * (-scale) * jax.nn.sigmoid(shifted), 0.0)
        d_params_ref[0:1, :] += jnp.sum(d_logdecay * logdecay, 0, keepdims=True)
        d_params_ref[1:2, :] += jnp.sum(d_shifted, 0, keepdims=True)
        d_pre_ref[pl.ds(places[c], CHUNK), width : width + 128] = (
            d_shifted + d_strengths[c] * strengths * (1.0 - strengths)
        ).astype(BF16)
    total = None
    pre = jnp.concatenate([ref[:, :width].astype(BF16).astype(F32) for ref in pre_refs], 0)
    for j in range(4):
        shifted = after[3 - j : 3 - j + span, :]
        term = taps_ref[j : j + 1, :] * shifted
        total = term if total is None else total + term
        d_taps_ref[j : j + 1, :] += jnp.sum(pre * shifted, 0, keepdims=True)
    for c in range(PER):
        d_pre_ref[pl.ds(places[c], CHUNK), :width] = total[c * CHUNK : (c + 1) * CHUNK].astype(BF16)
    after[span : span + 8, :] = after[0:8, :]


def mixer_forward(order, pre, taps, params, heads, key_dim, val_dim):
    chunks = pre.shape[0] // CHUNK
    width = taps.shape[1]
    here = lambda c: lambda n, order: (order[n * PER + c], 0)
    plain = lambda n, order: (n, 0)
    fixed = lambda n, order: (0, 0)
    return pl.pallas_call(
        functools.partial(forward_kernel, heads, key_dim, val_dim),
        grid_spec=pltpu.PrefetchScalarGridSpec(
            num_scalar_prefetch=1,
            grid=(chunks // PER,),
            in_specs=[pl.BlockSpec((CHUNK, pre.shape[1]), here(c)) for c in range(PER)]
            + [pl.BlockSpec(taps.shape, fixed), pl.BlockSpec(params.shape, fixed)],
            out_specs=[
                pl.BlockSpec((pre.shape[0], heads * val_dim), fixed),
                pl.BlockSpec((PER * heads * key_dim, val_dim), plain),
                pl.BlockSpec((PER * heads * CHUNK, CHUNK), plain),
                pl.BlockSpec((PER * CHUNK, heads * val_dim), plain),
                pl.BlockSpec((PER * CHUNK, width), plain),
                pl.BlockSpec((PER * CHUNK, width), plain),
            ],
            scratch_shapes=[
                pltpu.VMEM((heads * key_dim, val_dim), F32),
                pltpu.VMEM((PER * CHUNK + 8, width), F32),
            ],
        ),
        out_shape=[
            jax.ShapeDtypeStruct((pre.shape[0], heads * val_dim), F32),
            jax.ShapeDtypeStruct((chunks * heads * key_dim, val_dim), BF16),
            jax.ShapeDtypeStruct((chunks * heads * CHUNK, CHUNK), BF16),
            jax.ShapeDtypeStruct((pre.shape[0], heads * val_dim), BF16),
            jax.ShapeDtypeStruct((pre.shape[0], width), F32),
            jax.ShapeDtypeStruct((pre.shape[0], width), F32),
        ],
        compiler_params=pltpu.CompilerParams(vmem_limit_bytes=48 * 2**20),
        cost_estimate=small_cost(),
        name="mixer_forward",
    )(order, *[pre] * PER, taps, params)


def mixer_backward(
    order, pre, active, sigma, taps, params, states, inverses, news, mixed, gates, d_own, d_other,
    side, gain, heads, key_dim, val_dim,
):
    chunks = pre.shape[0] // CHUNK
    width = taps.shape[1]
    out_width = heads * val_dim
    steps = chunks // PER
    half = chunks // 2
    at = lambda n, c, order: order[(steps - 1 - n) * PER + c]
    here = lambda c: lambda n, order: (at(n, c, order), 0)
    first = lambda c: lambda n, order: (jnp.minimum(at(n, c, order), half - 1), 0)
    second = lambda c: lambda n, order: (jnp.maximum(at(n, c, order) - half, 0), 0)
    plain = lambda n, order: (steps - 1 - n, 0)
    fixed = lambda n, order: (0, 0)
    each = lambda shape, place: [pl.BlockSpec(shape, place(c)) for c in range(PER)]
    return pl.pallas_call(
        functools.partial(backward_kernel, heads, key_dim, val_dim),
        grid_spec=pltpu.PrefetchScalarGridSpec(
            num_scalar_prefetch=1,
            grid=(steps,),
            in_specs=each((CHUNK, pre.shape[1]), here)
            + [
                pl.BlockSpec((PER * CHUNK, width), plain),
                pl.BlockSpec((PER * CHUNK, width), plain),
                pl.BlockSpec(taps.shape, fixed),
                pl.BlockSpec(params.shape, fixed),
                pl.BlockSpec((PER * heads * key_dim, val_dim), plain),
                pl.BlockSpec((PER * heads * CHUNK, CHUNK), plain),
                pl.BlockSpec((PER * CHUNK, out_width), plain),
            ]
            + each((CHUNK, out_width), here)
            + each((CHUNK, out_width), here)
            + each((CHUNK, d_own.shape[1]), first)
            + each((CHUNK, d_own.shape[1]), second)
            + [
                pl.BlockSpec(side.shape, lambda n, order: (0, 0, 0, 0)),
                pl.BlockSpec((1, val_dim), fixed),
            ],
            out_specs=[
                pl.BlockSpec((pre.shape[0], pre.shape[1] + out_width), fixed),
                pl.BlockSpec((8, width), fixed),
                pl.BlockSpec((8, 128), fixed),
                pl.BlockSpec((8, val_dim), fixed),
            ],
            scratch_shapes=[
                pltpu.VMEM((heads * key_dim, val_dim), F32),
                pltpu.VMEM((PER * CHUNK + 8, width), F32),
            ],
        ),
        out_shape=[
            jax.ShapeDtypeStruct((pre.shape[0], pre.shape[1] + out_width), BF16),
            jax.ShapeDtypeStruct((8, width), F32),
            jax.ShapeDtypeStruct((8, 128), F32),
            jax.ShapeDtypeStruct((8, val_dim), F32),
        ],
        compiler_params=pltpu.CompilerParams(vmem_limit_bytes=56 * 2**20),
        cost_estimate=small_cost(),
        name="mixer_backward",
    )(
        order, *[pre] * PER, active, sigma, taps, params, states, inverses, news, *[mixed] * PER,
        *[gates] * PER, *[d_own] * PER, *[d_other] * PER, side, gain,
    )


def roomy():
    return dict(
        compiler_params=pltpu.CompilerParams(vmem_limit_bytes=56 * 2**20),
        cost_estimate=small_cost(),
    )


def pack_mix_kernel(heads, core_ref, q_ref, k_ref, v_ref, decay_ref, strength_ref, out_ref):
    first = core_ref[0] == 0
    wide, tall = q_ref.shape[1], v_ref.shape[1]
    out_ref[:, :wide] = q_ref[...]
    out_ref[:, wide : 2 * wide] = k_ref[...]
    out_ref[:, 2 * wide : 2 * wide + tall] = v_ref[...]

    rates = jnp.transpose(
        jnp.concatenate([decay_ref[...].astype(F32), strength_ref[...].astype(F32)], 0)
    )
    pick = lambda at: jnp.where(
        first, rates[:, at : at + heads], rates[:, at + heads : at + 2 * heads]
    )
    rows = out_ref.shape[0]
    out_ref[:, 2 * wide + tall :] = jnp.concatenate(
        [pick(0), pick(2 * heads), jnp.zeros((rows, 128 - 2 * heads), F32)], 1
    ).astype(BF16)


def pack_mix(core, heads, w_query, w_key, w_value, w_decay, w_strength):
    depth = w_query.shape[0]
    wide, tall = w_query.shape[1] // 2, w_value.shape[1] // 2
    here = lambda i, core: (0, core[0])
    fixed = lambda i, core: (0, 0)
    return pl.pallas_call(
        functools.partial(pack_mix_kernel, heads),
        grid_spec=pltpu.PrefetchScalarGridSpec(
            num_scalar_prefetch=1,
            grid=(1,),
            in_specs=[
                pl.BlockSpec((depth, wide), here),
                pl.BlockSpec((depth, wide), here),
                pl.BlockSpec((depth, tall), here),
                pl.BlockSpec(w_decay.shape[::-1], fixed),
                pl.BlockSpec(w_strength.shape[::-1], fixed),
            ],
            out_specs=pl.BlockSpec((depth, 2 * wide + tall + 128), fixed),
        ),
        out_shape=jax.ShapeDtypeStruct((depth, 2 * wide + tall + 128), BF16),
        name="pack_mix",
        **roomy(),
    )(core, w_query, w_key, w_value, w_decay.T, w_strength.T)


def pack_rest_kernel(core_ref, outgate_ref, out_ref, gate_ref, up_ref, down_ref, side_ref, wide_ref):
    first = core_ref[0] == 0
    depth = outgate_ref.shape[0]
    units = gate_ref.shape[1] // 2
    side_ref[:depth, :] = outgate_ref[...]
    side_ref[depth:, :] = jnp.transpose(out_ref[...].astype(F32)).astype(BF16)
    for at, ref in ((0, gate_ref), (1, up_ref)):
        values = ref[...]
        wide_ref[at * depth : (at + 1) * depth, :] = jnp.where(
            first, values[:, :units], values[:, units:]
        )
    wide_ref[2 * depth :, :] = jnp.transpose(down_ref[...].astype(F32)).astype(BF16)


def pack_rest(core, w_outgate, w_out, w_gate, w_up, w_down):
    depth = w_outgate.shape[0]
    tall, units = w_outgate.shape[1] // 2, w_gate.shape[1] // 2
    fixed = lambda i, core: (0, 0)
    return pl.pallas_call(
        pack_rest_kernel,
        grid_spec=pltpu.PrefetchScalarGridSpec(
            num_scalar_prefetch=1,
            grid=(1,),
            in_specs=[
                pl.BlockSpec((depth, tall), lambda i, core: (0, core[0])),
                pl.BlockSpec((tall, depth), lambda i, core: (core[0], 0)),
                pl.BlockSpec(w_gate.shape, fixed),
                pl.BlockSpec(w_up.shape, fixed),
                pl.BlockSpec((units, depth), lambda i, core: (core[0], 0)),
            ],
            out_specs=[
                pl.BlockSpec((2 * depth, tall), fixed),
                pl.BlockSpec((3 * depth, units), fixed),
            ],
        ),
        out_shape=[
            jax.ShapeDtypeStruct((2 * depth, tall), BF16),
            jax.ShapeDtypeStruct((3 * depth, units), BF16),
        ],
        name="pack_rest",
        **roomy(),
    )(core, w_outgate, w_out, w_gate, w_up, w_down)


def arrange_kernel(scalars_ref, tokens_ref, cotangent_ref, gain_ref, normed_ref, branch_ref):
    step = pl.program_id(0)
    rows = tokens_ref.shape[0]
    tokens = tokens_ref[...].astype(F32)
    scale = lax.rsqrt(jnp.mean(tokens * tokens, -1, keepdims=True) + 1e-6)
    normed_ref[...] = (tokens * scale * gain_ref[...]).astype(BF16)
    place = scalars_ref[0] + scalars_ref[2 + step] * rows + lax.broadcasted_iota(
        jnp.int32, (rows, 1), 0
    )
    branch_ref[...] = jnp.where(place < scalars_ref[1], cotangent_ref[...], 0).astype(BF16)


def arrange(scalars, tokens, cotangent, gain, layers):
    rows, model = tokens.shape[0] // layers, tokens.shape[1]
    there = pl.BlockSpec((rows, model), lambda p, scalars: (scalars[2 + p], 0))
    plain = pl.BlockSpec((rows, model), lambda p, scalars: (p, 0))
    return pl.pallas_call(
        arrange_kernel,
        grid_spec=pltpu.PrefetchScalarGridSpec(
            num_scalar_prefetch=1,
            grid=(layers,),
            in_specs=[there, there, pl.BlockSpec((1, model), lambda p, scalars: (0, 0))],
            out_specs=[plain, plain],
        ),
        out_shape=[jax.ShapeDtypeStruct(tokens.shape, BF16)] * 2,
        name="arrange",
        **roomy(),
    )(scalars, tokens, cotangent, gain)


TILE = 256


def heads_kernel(
    heads, normed_ref, mixed_ref, side_ref, gain_ref, gates_ref, heads_ref, other_ref, own_ref
):
    step = pl.program_id(0)
    half = pl.num_programs(0) // 2
    shards, _, depth, tall = side_ref.shape
    val_dim = tall // heads
    gates = mm(normed_ref[:, :depth], side_ref[0, 0])
    for f in range(1, shards):
        gates = gates + mm(normed_ref[:, f * depth : (f + 1) * depth], side_ref[f, 0])
    gates_ref[...] = gates
    for h in range(heads):
        at = slice(h * val_dim, (h + 1) * val_dim)
        mixed = mixed_ref[:, at]
        gate = gates[:, at]
        scale = lax.rsqrt(jnp.mean(mixed * mixed, -1, keepdims=True) + 1e-5)
        heads_ref[:, at] = (
            mixed * scale * gain_ref[...] * (gate * jax.nn.sigmoid(gate))
        ).astype(BF16)
    low = heads_ref[...]

    def write(ref):
        for f in range(shards):
            ref[:, f * depth : (f + 1) * depth] = mm(low, side_ref[f, 1], NT).astype(BF16)

    @pl.when(step < half)
    def _():
        write(other_ref)

    @pl.when(step >= half)
    def _():
        write(own_ref)


def turned_specs(tiles):
    half = tiles // 2
    here = lambda i: (jnp.where(i < half, i + half, i - half), 0)
    other = lambda i: (jnp.minimum(i, half - 1), 0)
    own = lambda i: (jnp.maximum(i - half, 0), 0)
    return here, other, own


def head_outputs(normed, mixed, side, gain, heads):
    count, model = normed.shape
    tall = mixed.shape[1]
    here, other, own = turned_specs(count // TILE)
    return pl.pallas_call(
        functools.partial(heads_kernel, heads),
        grid=(count // TILE,),
        in_specs=[
            pl.BlockSpec((TILE, model), here),
            pl.BlockSpec((TILE, tall), here),
            pl.BlockSpec(side.shape, lambda i: (0, 0, 0, 0)),
            pl.BlockSpec(gain.shape, lambda i: (0, 0)),
        ],
        out_specs=[
            pl.BlockSpec((TILE, tall), here),
            pl.BlockSpec((TILE, tall), here),
            pl.BlockSpec((TILE, model), other),
            pl.BlockSpec((TILE, model), own),
        ],
        out_shape=[
            jax.ShapeDtypeStruct((count, tall), F32),
            jax.ShapeDtypeStruct((count, tall), BF16),
            jax.ShapeDtypeStruct((count // 2, model), BF16),
            jax.ShapeDtypeStruct((count // 2, model), BF16),
        ],
        name="head_outputs",
        **roomy(),
    )(normed, mixed, side, gain)


def feed_kernel(hidden_ref, branch_ref, wide_ref, stack_ref, d_hidden_ref, branch_out_ref):
    shards, _, depth, units = wide_ref.shape

    def forward(ref, at):
        total = mm(ref[:, :depth], wide_ref[0, at])
        for f in range(1, shards):
            total = total + mm(ref[:, f * depth : (f + 1) * depth], wide_ref[f, at])
        return total

    gate = forward(hidden_ref, 0)
    up = forward(hidden_ref, 1)
    d_act = forward(branch_ref, 2)
    sigma = jax.nn.sigmoid(gate)
    silu = gate * sigma
    act = (silu * up).astype(BF16)
    d_gate = (d_act * up * (sigma + silu * (1.0 - sigma))).astype(BF16)
    d_up = (d_act * silu).astype(BF16)
    stack_ref[0] = d_gate
    stack_ref[1] = d_up
    stack_ref[2] = act
    for f in range(shards):
        at = slice(f * depth, (f + 1) * depth)
        d_hidden_ref[:, at] = (
            mm(d_gate, wide_ref[f, 0], NT) + mm(d_up, wide_ref[f, 1], NT)
        ).astype(BF16)
        branch_out_ref[:, at] = mm(act, wide_ref[f, 2], NT).astype(BF16)


def feed_forward(hidden, branch, wide):
    count, model = hidden.shape
    units = wide.shape[3]
    row = pl.BlockSpec((TILE, model), lambda i: (i, 0))
    return pl.pallas_call(
        feed_kernel,
        grid=(count // TILE,),
        in_specs=[row, row, pl.BlockSpec(wide.shape, lambda i: (0, 0, 0, 0))],
        out_specs=[pl.BlockSpec((3, TILE, units), lambda i: (0, i, 0)), row, row],
        out_shape=[
            jax.ShapeDtypeStruct((3, count, units), BF16),
            jax.ShapeDtypeStruct((count, model), BF16),
            jax.ShapeDtypeStruct((count, model), BF16),
        ],
        name="feed_forward",
        **roomy(),
    )(hidden, branch, wide)


def feed_grads_kernel(h_own, h_other, b_own, b_other, s_own, s_other, out_ref):
    units = s_own.shape[2]
    for at, own, other in ((0, h_own, h_other), (1, h_own, h_other), (2, b_own, b_other)):
        out_ref[:, at * units : (at + 1) * units] = (
            mm(own[...], s_own[at], TN) + mm(other[...], s_other[at], TN)
        ).astype(BF16)
    rest = out_ref.shape[1] - 3 * units
    if rest:
        out_ref[:, 3 * units :] = jnp.zeros((out_ref.shape[0], rest), BF16)


def feed_grads(hidden, branch, stacks, shards):
    count, model = hidden[0].shape
    units = stacks[0].shape[2]
    depth = model // shards
    width = -(-3 * units // 128) * 128
    part = pl.BlockSpec((count, depth), lambda f: (0, f))
    use_s = pl.BlockSpec((3, count, units), lambda f: (0, 0, 0))
    return pl.pallas_call(
        feed_grads_kernel,
        grid=(shards,),
        in_specs=[part, part, part, part, use_s, use_s],
        out_specs=pl.BlockSpec((depth, width), lambda f: (f, 0)),
        out_shape=jax.ShapeDtypeStruct((model, width), BF16),
        name="feed_grads",
        **roomy(),
    )(*hidden, *branch, *stacks)


def d_normed_kernel(side_at, mix_ref, normed_ref, weights_ref, side_ref, other_ref, own_ref, sum_ref):
    step = pl.program_id(0)
    half = pl.num_programs(0) // 2
    shards, _, depth, _ = side_ref.shape

    @pl.when(step == 0)
    def _():
        sum_ref[...] = jnp.zeros_like(sum_ref)

    def write(ref):
        for f in range(shards):
            at = slice(f * depth, (f + 1) * depth)
            part = mm(mix_ref[:, :side_at], weights_ref[at, :], NT) + mm(
                mix_ref[:, side_at:], side_ref[f, 0], NT
            )
            ref[:, at] = part.astype(BF16)
            sum_ref[0:1, at] += jnp.sum(part * normed_ref[:, at].astype(F32), 0, keepdims=True)

    @pl.when(step < half)
    def _():
        write(other_ref)

    @pl.when(step >= half)
    def _():
        write(own_ref)


def d_normed_rows(d_mix, normed, weights, side):
    count, model = normed.shape
    here, other, own = turned_specs(count // TILE)
    fixed = lambda i: (0, 0)
    return pl.pallas_call(
        functools.partial(d_normed_kernel, weights.shape[1]),
        grid=(count // TILE,),
        in_specs=[
            pl.BlockSpec((TILE, d_mix.shape[1]), here),
            pl.BlockSpec((TILE, model), here),
            pl.BlockSpec(weights.shape, fixed),
            pl.BlockSpec(side.shape, lambda i: (0, 0, 0, 0)),
        ],
        out_specs=[
            pl.BlockSpec((TILE, model), other),
            pl.BlockSpec((TILE, model), own),
            pl.BlockSpec((8, model), fixed),
        ],
        out_shape=[
            jax.ShapeDtypeStruct((count // 2, model), BF16),
            jax.ShapeDtypeStruct((count // 2, model), BF16),
            jax.ShapeDtypeStruct((8, model), F32),
        ],
        name="d_normed_rows",
        **roomy(),
    )(d_mix, normed, weights, side)


def mix_grads_kernel(normed_ref, mix_ref, out_ref):
    out_ref[...] = mm(normed_ref[...], mix_ref[...], TN).astype(BF16)


def mix_grads(normed, d_mix, shards):
    count, model = normed.shape
    depth, width = model // shards, d_mix.shape[1]
    return pl.pallas_call(
        mix_grads_kernel,
        grid=(shards,),
        in_specs=[
            pl.BlockSpec((count, depth), lambda f: (0, f)),
            pl.BlockSpec(d_mix.shape, lambda f: (0, 0)),
        ],
        out_specs=pl.BlockSpec((depth, width), lambda f: (f, 0)),
        out_shape=jax.ShapeDtypeStruct((model, width), BF16),
        name="mix_grads",
        **roomy(),
    )(normed, d_mix)


def out_grads_kernel(d_own_ref, d_other_ref, heads_ref, out_ref):
    half = d_own_ref.shape[0]
    out_ref[...] = (
        mm(d_own_ref[...], heads_ref[:half, :], TN) + mm(d_other_ref[...], heads_ref[half:, :], TN)
    ).astype(BF16)


def out_grads(d_own, d_other, heads_out, shards):
    count, model = d_own.shape
    depth, width = model // shards, heads_out.shape[1]
    column = pl.BlockSpec((count, depth), lambda f: (0, f))
    return pl.pallas_call(
        out_grads_kernel,
        grid=(shards,),
        in_specs=[column, column, pl.BlockSpec(heads_out.shape, lambda f: (0, 0))],
        out_specs=pl.BlockSpec((depth, width), lambda f: (f, 0)),
        out_shape=jax.ShapeDtypeStruct((model, width), BF16),
        name="out_grads",
        **roomy(),
    )(d_own, d_other, heads_out)


def place_kernel(turns_ref, *refs):
    parts, out_ref = refs[:-1], refs[-1]
    size = turns_ref.shape[0]
    rows = parts[0].shape[0]
    for p in range(size):
        at = pl.multiple_of(turns_ref[p] * rows, rows)
        if len(parts) == size:
            part = parts[p][...]
        elif p == 0:
            part = parts[0][...]
        else:
            part = parts[p][...] + parts[2 * size - 1 - p][...]
        out_ref[pl.ds(at, rows), :] = part


def place(turns, parts):
    size = turns.shape[0]
    rows, model = parts[0].shape
    whole = lambda i, turns: (0, 0)
    return pl.pallas_call(
        place_kernel,
        grid_spec=pltpu.PrefetchScalarGridSpec(
            num_scalar_prefetch=1,
            grid=(1,),
            in_specs=[pl.BlockSpec((rows, model), whole)] * len(parts),
            out_specs=pl.BlockSpec((size * rows, model), whole),
        ),
        out_shape=jax.ShapeDtypeStruct((size * rows, model), BF16),
        name="place",
        **roomy(),
    )(turns, *parts)


def finish_wide_kernel(
    units, core_ref, own_ref, other_ref, out_own_ref, out_other_ref, gate_ref, up_ref, down_ref,
    out_ref,
):
    first = core_ref[0] == 0

    def pair(a, b):
        own, other = a[...].astype(F32), b[...].astype(F32)
        return jnp.where(first, own, other), jnp.where(first, other, own)

    low, high = pair(own_ref, other_ref)
    for at, ref in ((0, gate_ref), (1, up_ref)):
        ref[:, :units] = low[:, at * units : (at + 1) * units]
        ref[:, units:] = high[:, at * units : (at + 1) * units]
    down_ref[:units, :] = jnp.transpose(low[:, 2 * units : 3 * units])
    down_ref[units:, :] = jnp.transpose(high[:, 2 * units : 3 * units])
    low, high = pair(out_own_ref, out_other_ref)
    tall = low.shape[1]
    out_ref[:tall, :] = jnp.transpose(low)
    out_ref[tall:, :] = jnp.transpose(high)


def finish_wide(core, own, other, out_own, out_other, units):
    depth, width = own.shape
    tall = out_own.shape[1]
    row = lambda size: pl.BlockSpec((128, size), lambda i, core: (i, 0))
    column = lambda size: pl.BlockSpec((size, 128), lambda i, core: (0, i))
    return pl.pallas_call(
        functools.partial(finish_wide_kernel, units),
        grid_spec=pltpu.PrefetchScalarGridSpec(
            num_scalar_prefetch=1,
            grid=(depth // 128,),
            in_specs=[row(width), row(width), row(tall), row(tall)],
            out_specs=[row(2 * units), row(2 * units), column(2 * units), column(2 * tall)],
        ),
        out_shape=[
            jax.ShapeDtypeStruct((depth, 2 * units), F32),
            jax.ShapeDtypeStruct((depth, 2 * units), F32),
            jax.ShapeDtypeStruct((2 * units, depth), F32),
            jax.ShapeDtypeStruct((2 * tall, depth), F32),
        ],
        name="finish_wide",
        **roomy(),
    )(core, own, other, out_own, out_other)


def finish_mix_kernel(cuts, core_ref, a_ref, b_ref, *refs):
    first = core_ref[0] == 0
    own, other = a_ref[...].astype(F32), b_ref[...].astype(F32)
    low, high = jnp.where(first, own, other), jnp.where(first, other, own)
    for (begin, size), ref in zip(cuts, refs):
        ref[:, :size] = low[:, begin : begin + size]
        ref[:, size:] = high[:, begin : begin + size]


def finish_mix(core, own, other, cuts):
    depth, width = own.shape
    row = lambda size: pl.BlockSpec((128, size), lambda i, core: (i, 0))
    return pl.pallas_call(
        functools.partial(finish_mix_kernel, cuts),
        grid_spec=pltpu.PrefetchScalarGridSpec(
            num_scalar_prefetch=1,
            grid=(depth // 128,),
            in_specs=[row(width), row(width)],
            out_specs=[row(2 * size) for _, size in cuts],
        ),
        out_shape=[jax.ShapeDtypeStruct((depth, 2 * size), F32) for _, size in cuts],
        name="finish_mix",
        **roomy(),
    )(core, own, other)


def after(value, *others):
    return lax.optimization_barrier((value,) + others)[0]


def is_square(axis):
    return lax.axis_size(axis) == 4


def across(value, flip):
    return lax.ppermute(value, "fsdp", [(i, i ^ flip) for i in range(4)])


def swapped(value):
    return lax.ppermute(value, "context", [(0, 1), (1, 0)])


def gathered_rows(own, beside):
    if not is_square("fsdp"):
        return lax.all_gather(own, "fsdp", axis=0, tiled=True), beside
    rows = own.shape[0]
    half = rows // 2
    along_x = across(own, 1)
    along_y = across(own, 2)
    along_x, along_y, beside = lax.optimization_barrier((along_x, along_y, beside))
    low = across(along_x[:half], 2)
    high = across(along_y[half:], 1)
    shard = lax.axis_index("fsdp")
    whole = jnp.zeros((4 * rows,) + own.shape[1:], own.dtype)
    for place, part in ((0, own), (1, along_x), (2, along_y)):
        whole = lax.dynamic_update_slice_in_dim(whole, part, (shard ^ place) * rows, 0)
    whole = lax.dynamic_update_slice_in_dim(whole, low, (shard ^ 3) * rows, 0)
    return lax.dynamic_update_slice_in_dim(whole, high, (shard ^ 3) * rows + half, 0), beside


def scattered(blocks):
    return lax.psum_scatter(blocks, "fsdp", scatter_dimension=0, tiled=True)


def line_sum(value, beside=(), axis="tensor"):
    size = lax.axis_size(axis)
    rows = value.shape[0] // size
    parts = [
        lax.ppermute(
            value[p * rows : (p + 1) * rows], axis, [(i, (i - p) % size) for i in range(size)]
        )
        for p in range(1, size)
    ]
    if beside:
        parts, beside = lax.optimization_barrier((parts, tuple(beside)))
    total = value[:rows].astype(F32)
    for part in parts:
        total = total + part.astype(F32)
    return (total, *beside) if beside else total


def line_sum_hops(value, axis="tensor"):
    size = lax.axis_size(axis)
    rows = value.shape[0] // size
    block = lambda p: value[p * rows : (p + 1) * rows].astype(F32)
    right = left = None
    for step in range(1, size):
        send_r, send_l = block(step), block(size - step)
        if right is not None:
            send_r = send_r + right.astype(F32)
            send_l = send_l + left.astype(F32)
        right = lax.ppermute(send_r.astype(BF16), axis, [(i, i + 1) for i in range(step)])
        left = lax.ppermute(
            send_l.astype(BF16), axis, [(i, i - 1) for i in range(size - step, size)]
        )
    return block(0) + right.astype(F32) + left.astype(F32)


def line_gather(own, axis="tensor"):
    size = lax.axis_size(axis)
    rights, lefts = [own], [own]
    for step in range(1, size):
        rights.append(
            lax.ppermute(rights[-1], axis, [(i, i + 1) for i in range(step - 1, size - 1)])
        )
        lefts.append(lax.ppermute(lefts[-1], axis, [(i, i - 1) for i in range(1, size - step + 1)]))
    return [own] + [rights[k] + lefts[size - k] for k in range(1, size)]


def line_hop(right, left, step, axis="tensor"):
    size = lax.axis_size(axis)
    return (
        lax.ppermute(right, axis, [(i, i + 1) for i in range(step - 1, size - 1)]),
        lax.ppermute(left, axis, [(i, i - 1) for i in range(1, size - step + 1)]),
    )


def flat(hops):
    return [hops[0][0]] + [hop[0] for hop in hops[1:]] + [hop[1] for hop in hops[1:]]


def line_total(value, axis="tensor"):
    size = lax.axis_size(axis)
    step = 1
    while step < size:
        value = value + lax.ppermute(value, axis, [(i, i ^ step) for i in range(size)])
        step *= 2
    return value


def core_sum(other_rows, own_rows):
    return (own_rows.astype(F32) + swapped(other_rows).astype(F32)).astype(BF16)


def dot(a, b, dims=NN):
    return lax.dot_general(a, b, (dims, ((), ())), preferred_element_type=F32)


def norm_parts(values, epsilon):
    return lax.rsqrt(jnp.mean(values * values, -1, keepdims=True) + epsilon)


def norm_back(d_scaled, values, scale, gain):
    raised = d_scaled * gain
    return scale * raised - values * (
        scale * scale * scale * jnp.mean(raised * values, -1, keepdims=True)
    )


def on_device(
    inputs, lengths, norm_attn, w_query, w_key, w_value, w_decay, w_strength, decay_log,
    decay_bias, conv_query, conv_key, conv_value, w_outgate, norm_head, w_out, norm_mlp, w_gate,
    w_up, w_down, cotangent,
):
    shard, core, layer = (lax.axis_index(name) for name in ("fsdp", "context", "tensor"))
    shards, layers = lax.axis_size("fsdp"), lax.axis_size("tensor")
    seg, model = inputs.shape[1:]
    rows = seg // layers
    depth = norm_attn.shape[0]
    all_heads, taps_count, key_part = conv_query.shape
    val_part = conv_value.shape[2]
    heads = all_heads // 2
    key_dim, val_dim = key_part * shards, val_part * shards
    wide, tall = heads * key_dim, heads * val_dim
    width = 2 * wide + tall
    units = w_gate.shape[1] // 2

    def mine(array, dim):
        size = array.shape[dim] // 2
        first = lax.slice_in_dim(array, 0, size, axis=dim)
        second = lax.slice_in_dim(array, size, 2 * size, axis=dim)
        return jnp.where(core == 0, first, second)

    core_id = core.reshape(1).astype(jnp.int32)
    own_mix = pack_mix(core_id, heads, w_query, w_key, w_value, w_decay, w_strength)

    pieces = (
        norm_attn, norm_mlp, norm_head,
        mine(conv_query, 0).reshape(-1), mine(conv_key, 0).reshape(-1),
        mine(conv_value, 0).reshape(-1),
    )
    small = after(jnp.concatenate(pieces), own_mix)
    if is_square("fsdp"):
        stack = jnp.stack([small, across(small, 1), across(small, 2), across(small, 3)])
        stack = jnp.stack([lax.dynamic_index_in_dim(stack, shard ^ i, 0, False) for i in range(4)])
    else:
        stack = lax.all_gather(small, "fsdp")
    cuts = [0]
    for piece in pieces:
        cuts.append(cuts[-1] + piece.shape[0])
    gain_attn = stack[:, cuts[0] : cuts[1]].reshape(1, model).astype(F32)
    gain_mlp = stack[:, cuts[1] : cuts[2]].reshape(1, model).astype(F32)
    gain_head = stack[:, cuts[2] : cuts[3]].reshape(1, val_dim).astype(F32)

    def taps_of(at, part):
        array = stack[:, cuts[at] : cuts[at + 1]].reshape(shards, heads, taps_count, part)
        return jnp.transpose(array, (2, 1, 0, 3)).reshape(taps_count, -1)

    taps = jnp.concatenate([taps_of(3, key_part), taps_of(4, key_part), taps_of(5, val_part)], 1)
    taps = jnp.pad(taps.astype(F32), ((0, 8 - taps_count), (0, 0)))
    params = jnp.pad(
        jnp.stack([mine(decay_log, 0), mine(decay_bias, 0)]).astype(F32),
        ((0, 6), (0, 128 - heads)),
    )

    turns = (layer - jnp.arange(layers, dtype=jnp.int32)) % layers
    scalars = jnp.concatenate([(core * seg).reshape(1), lengths[:1], turns]).astype(jnp.int32)
    per_core, per_block = seg // CHUNK, rows // CHUNK
    ids = jnp.arange(2 * per_core, dtype=jnp.int32)
    within = ids % per_core
    order = (
        jnp.where(ids // per_core == core, 0, per_core)
        + ((layer - within // per_block) % layers) * per_block
        + within % per_block
    ).astype(jnp.int32)
    live_own = (
        core * seg + layer * rows + jnp.arange(rows, dtype=jnp.int32) < lengths[0]
    ).astype(F32)[:, None]
    tokens_own = lax.dynamic_slice_in_dim(inputs[0], layer * rows, rows, 0).astype(F32)
    d_out_own = lax.dynamic_slice_in_dim(cotangent[0], layer * rows, rows, 0).astype(F32)
    normed_own, d_branch_own = arrange(scalars, inputs[0], cotangent[0], gain_attn, layers)
    own_side, own_feed = pack_rest(core_id, w_outgate, w_out, w_gate, w_up, w_down)
    full_mix, (normed_own, own_side, own_feed) = gathered_rows(
        own_mix, (normed_own, own_side, own_feed)
    )
    side = lax.all_gather(own_side, "fsdp", axis=0, tiled=True)
    normed = jnp.concatenate([normed_own, swapped(normed_own)], 0)
    d_branch = (d_branch_own, swapped(after(d_branch_own, full_mix)))

    projected = dot(normed, full_mix)
    feed = lax.all_gather(after(own_feed, projected), "fsdp", axis=0, tiled=True)
    side = side.reshape(shards, 2, depth, tall)
    feed = feed.reshape(shards, 3, depth, units)
    mixed, states, inverses, news, active, sigma = mixer_forward(
        order, projected, taps, params, heads, key_dim, val_dim
    )
    gates, heads_out, attn_other, attn_own = head_outputs(normed, mixed, side, gain_head, heads)
    attn = line_sum_hops(core_sum(attn_other, attn_own))
    middle = tokens_own + live_own * attn
    mlp_scale = norm_parts(middle, 1e-6)
    hidden_own = (middle * mlp_scale * gain_mlp).astype(BF16)
    hidden_mine = jnp.concatenate(line_gather(hidden_own), 0)
    hidden = (hidden_mine, swapped(hidden_mine))

    stack_own, d_hidden_mine, branch_mine = feed_forward(hidden[0], d_branch[0], feed)
    stack_other, d_hidden_other, branch_other = feed_forward(hidden[1], d_branch[1], feed)
    d_hidden_core = core_sum(d_hidden_other, d_hidden_mine)
    held = lax.optimization_barrier((stack_own, stack_other, branch_other, d_hidden_core))
    grad_feed = feed_grads(hidden, d_branch, held[:2], shards)
    branch_core = core_sum(held[2], branch_mine)
    d_hidden, grad_feed, branch_core = line_sum(d_hidden_core, (grad_feed, branch_core))
    sum_feed = scattered(grad_feed)

    grad_mlp = jnp.sum(d_hidden * middle * mlp_scale, 0)
    d_middle = d_out_own + norm_back(d_hidden, middle, mlp_scale, gain_mlp)
    d_attn_mine = jnp.concatenate(line_gather((live_own * d_middle).astype(BF16)), 0)
    branch_core, d_attn_mine = lax.optimization_barrier((branch_core, d_attn_mine))
    d_attn = (d_attn_mine, swapped(d_attn_mine))


    d_mix, d_taps, d_params, d_gain = mixer_backward(
        order, projected, active, sigma, taps, params, states, inverses, news, mixed, gates,
        *d_attn, side, gain_head, heads, key_dim, val_dim,
    )
    branch, d_mix = line_sum(branch_core, (d_mix,))
    out_own = (middle + live_own * branch).astype(BF16)
    out_own, sum_feed, d_mix = lax.optimization_barrier((out_own, sum_feed, d_mix))
    side_at = width + 128

    hops = [(out_own, out_own)]
    hops.append(line_hop(*hops[-1], 1))
    d_normed_other, d_normed_mine, weighted = d_normed_rows(d_mix, normed, full_mix, side)
    hops[1], d_normed_other, d_normed_mine = lax.optimization_barrier(
        (hops[1], d_normed_other, d_normed_mine)
    )
    hops.append(line_hop(*hops[-1], 2))
    grad_out = out_grads(*d_attn, heads_out, shards)
    d_normed_other, grad_out = lax.optimization_barrier((swapped(d_normed_other), grad_out))
    d_normed_core = (d_normed_mine.astype(F32) + d_normed_other.astype(F32)).astype(BF16)
    sum_out = scattered(grad_out)
    hops[2], d_normed_core = lax.optimization_barrier((hops[2], d_normed_core))
    for step in range(3, layers):
        hops.append(line_hop(*hops[-1], step))

    grad_mix = mix_grads(normed, after(d_mix, d_normed_core), shards)
    d_normed, grad_mix, hops = line_sum(d_normed_core, (grad_mix, hops))
    low_mix = scattered(grad_mix)

    vector = after(jnp.concatenate([weighted[0] / gain_attn[0], grad_mlp, d_gain[0]]), grad_mix)
    vector = line_total(line_total(vector, "context"), "tensor")
    vector = jnp.concatenate([vector, d_taps[:taps_count].reshape(-1), d_params[:2].reshape(-1)])
    vector = line_total(vector, "fsdp")
    g_attn = lax.dynamic_slice_in_dim(vector, shard * depth, depth, 0)
    g_mlp = lax.dynamic_slice_in_dim(vector, model + shard * depth, depth, 0)
    g_head = lax.dynamic_slice_in_dim(vector, 2 * model + shard * val_part, val_part, 0)
    mine_taps = vector[2 * model + val_dim :]
    local = jnp.stack([mine_taps, swapped(mine_taps)])
    table = jnp.where(core == 0, local, local[::-1])
    tap_table = table[:, : taps_count * width].reshape(2, taps_count, width)
    param_table = table[:, taps_count * width :].reshape(2, 2, 128)
    d_log, d_bias = param_table[:, 0, :heads].reshape(-1), param_table[:, 1, :heads].reshape(-1)

    def tap_grad(begin, size):
        array = tap_table[:, :, begin : begin + heads * size].reshape(2, taps_count, heads, size)
        part = lax.dynamic_slice_in_dim(array, shard * (size // shards), size // shards, 3)
        return jnp.transpose(part, (0, 2, 1, 3)).reshape(all_heads, taps_count, size // shards)

    d_conv_q, d_conv_k, d_conv_v = (
        tap_grad(0, key_dim), tap_grad(wide, key_dim), tap_grad(2 * wide, val_dim)
    )

    d_tokens = norm_back(d_normed, tokens_own, norm_parts(tokens_own, 1e-6), gain_attn)
    grad_own = (d_middle + d_tokens).astype(BF16)
    back = [(grad_own, grad_own)]
    for step in range(1, layers):
        back.append(line_hop(*back[-1], step))
        if step == 1:
            output = place(turns, flat(hops))
            done = finish_wide(
                core_id, sum_feed, swapped(sum_feed), sum_out, swapped(sum_out), units
            )
            back[1], output, done = lax.optimization_barrier((back[1], output, done))
    g_gate, g_up, g_down, g_out = done
    input_grad = place(turns, flat(back))[None]
    low_mix, input_grad = lax.optimization_barrier((low_mix, input_grad))
    other_mix = swapped(low_mix)
    g_query, g_key, g_value, g_outgate = finish_mix(
        core_id, low_mix, other_mix,
        ((0, wide), (wide, wide), (2 * wide, tall), (side_at, tall)),
    )

    def narrow(begin):
        own, other = low_mix[:, begin : begin + heads], other_mix[:, begin : begin + heads]
        return jnp.where(
            core == 0, jnp.concatenate([own, other], 1), jnp.concatenate([other, own], 1)
        ).astype(F32)

    return (
        output[None],
        input_grad,
        g_attn,
        g_query,
        g_key,
        g_value,
        narrow(width),
        narrow(width + heads),
        d_log,
        d_bias,
        d_conv_q,
        d_conv_k,
        d_conv_v,
        g_outgate,
        g_head,
        g_out,
        g_mlp,
        g_gate,
        g_up,
        g_down,
    )


def solution(mesh):
    placed = (
        P("fsdp", "context", None),
        P("fsdp"),
        P("fsdp"),
        P("fsdp", "tensor"),
        P("fsdp", "tensor"),
        P("fsdp", "tensor"),
        P("fsdp", "tensor"),
        P("fsdp", "tensor"),
        P("tensor"),
        P("tensor"),
        P("tensor", None, "fsdp"),
        P("tensor", None, "fsdp"),
        P("tensor", None, "fsdp"),
        P("fsdp", "tensor"),
        P("fsdp"),
        P("tensor", "fsdp"),
        P("fsdp"),
        P("fsdp", "tensor"),
        P("fsdp", "tensor"),
        P("tensor", "fsdp"),
        P("fsdp", "context", None),
    )
    return jax.shard_map(
        on_device,
        mesh=mesh,
        in_specs=placed,
        out_specs=(placed[0], placed[0]) + placed[2:20],
        check_vma=False,
    )
```

time: 655 us -> 612 us (0.934)
  waiting for transfers between devices: 246 us -> 228 us
  starting transfers between devices: 91.5 us -> 107 us
  local copies, waits for them, and re-layouts: 47.4 us -> 34.6 us
  other arithmetic: 43 us -> 31.7 us
  Pallas kernels: 192 us -> 181 us
    ppermute x9 -> x6, waiting for transfers between devices: 83.3 us -> 51.2 us  [line_gather(): lax.ppermute(lefts[-1], axis, [(i, i - 1) for i in range(1, size - step +...]
    pallas_call x1, Pallas kernels: 39.4 us -> 19.5 us  [mixer_forward(): pl.pallas_call(functools.partial(forward_kernel, heads, key_dim, val_dim)...]
    ppermute x2 -> x5, waiting for transfers between devices: 1.01 us -> 15.3 us  [line_total(): lax.ppermute(value, axis, [(i, i ^ step) for i in range(size)])]
    ppermute x3 -> x12, starting transfers between devices: 4.26 us -> 18.4 us  [the longest x6 10.4 us: line_hop(): lax.ppermute(right, axis, [(i, i + 1) for i in range(step - 1, size - 1)])]
    pallas_call x1 -> x4, Pallas kernels: 15.3 us -> 26.6 us  [the longest x1 12.1 us: mix_grads(): pl.pallas_call(mix_grads_kernel, grid=(shards,), in_specs=[pl.BlockSpec((...]
    ppermute x11 -> x12, waiting for transfers between devices: 15.2 us -> 6.62 us  [swapped(): return lax.ppermute(value, 'context', [(0, 1), (1, 0)])]
    ppermute x11 -> x12, starting transfers between devices: 22.4 us -> 30.1 us  [swapped(): return lax.ppermute(value, 'context', [(0, 1), (1, 0)])]
    dynamic_update_slice x4 -> x0, other arithmetic: 7.61 us -> none  [placed(): lax.dynamic_update_slice(whole, part, ((layer - p) % layers * rows, 0))]
  transfers between devices with their start and end apart: 60 -> 68, of which waited for: 30 -> 26; matrix products, arithmetic and copies ran while one was open for 11% -> 9% of each run, Pallas kernels for 23% -> 26%
where the time goes in v1:
time: 612 us; the launch traced here: 605 us
  waiting for transfers between devices  228 us (37%)
  Pallas kernels  181 us (30%)
  starting transfers between devices  107 us (17%)
  local copies, waits for them, and re-layouts  34.6 us (6%)
  other arithmetic  31.7 us (5%)
  between operations  15.8 us (3%)
  matrix products  7.11 us (1%)
    ppermute x9, waiting for transfers between devices, line_sum(): lax.ppermute(value[p * rows:(p + 1) * rows], axis, [(i, (i - p) % size) f...  59.2 us
    ppermute x6, waiting for transfers between devices, line_gather(): lax.ppermute(lefts[-1], axis, [(i, i - 1) for i in range(1, size - step +...  51.2 us
    pallas_call x1, Pallas kernels, mixer_backward(): pl.pallas_call(functools.partial(backward_kernel, heads, key_dim, val_dim...  35.2 us
    pallas_call x2, Pallas kernels, feed_forward(): pl.pallas_call(feed_kernel, grid=(count // TILE,), in_specs=[row, row, pl...  34 us
    ppermute x7, waiting for transfers between devices, across(): return lax.ppermute(value, 'fsdp', [(i, i ^ flip) for i in range(4)])  33.4 us
    ppermute x12, starting transfers between devices, swapped(): return lax.ppermute(value, 'context', [(0, 1), (1, 0)])  30.1 us
    ppermute x6, waiting for transfers between devices, line_hop(): lax.ppermute(left, axis, [(i, i - 1) for i in range(1, size - step + 1)])  29.2 us
    ppermute x3, waiting for transfers between devices, line_sum_hops(): lax.ppermute(send_r.astype(BF16), axis, [(i, i + 1) for i in range(step)])  28.2 us
  transfers between devices with their start and end apart: 68, of which 26 were waited for; matrix products, arithmetic and copies ran while one was open for 9% of the time, Pallas kernels for 26%

profile of v1, /device:TPU:1, one launch (start us, length us, event | category | flops | bytes accessed | tf_op | source)
XLA Modules:
  0.0 605.5 jit_solution(14516441064305493902)
XLA Ops:
  21.5 5.0 pack_rest.1
  27.4 5.6 arrange.1
  33.0 11.1 %collective-permute-done = bf16[512,1152]{1,0:T(8,128)(2,1)S(1)} collective-permute-done((bf16[512,1152]{1,0:T(8,128)(2,1)}, bf16[512,1152]{1,0:T(8,128)(2,1)S(1)}, u32[]{:S(2)}, u32[]{:S(2)}) %collective-permute-start) | collective-permute-done | bytes 1179680 | tf_op jit(solution)/shard_map/ppermute | solution.py:981
  51.4 18.5 %collective-permute-done.6 = bf16[256,1152]{1,0:T(8,128)(2,1)S(1)} collective-permute-done((bf16[256,1152]{1,0:T(8,128)(2,1)S(1)}, bf16[256,1152]{1,0:T(8,128)(2,1)S(1)}, u32[]{:S(2)}, u32[]{:S(2)}) %collective-permute-start.6) | collective-permute-done | bytes 589856 | tf_op jit(solution)/shard_map/ppermute | solution.py:981
  73.0 3.4 constant_dynamic-update-slice_fusion.normed_ref
  78.4 7.1 %fusion.38.refs_0_.refs_1_ = f32[1024,1152]{1,0:T(8,128)} fusion(bf16[1024,2048]{1,0:T(8,128)(2,1)S(1)} %constant_dynamic-update-slice_fusion.normed_ref, bf16[2048,1152]{1,0:T(8,128)(2,1)S(1)} %constant_dynamic-update-slice_fusion.2.weights_ref), kind=kOutput, calls=%fused_computation.125 | convolution fusion | flops 4831838208 | bytes 13631488 | tf_op jit(solution)/shard_map/dot_general | solution.py:1081
  87.8 19.5 %mixer_forward.1 = (f32[1024,512]{1,0:T(8,128)S(1)}, bf16[2048,256]{1,0:T(8,128)(2,1)S(1)}, bf16[2048,128]{1,0:T(8,128)(2,1)S(1)}, bf16[1024,512]{1,0:T(8,128)(2...) custom-call(s32[8]{0:T(128)S(1)} %fusion.23.order_ref, f32[1024,1152]{1,0:T(8,128)} %fusion.38.refs_0_.refs_1_, ...), custom_call_target="tpu_custom_call" | custom-call | flops 1 | bytes 1 | tf_op jit(solution)/shard_map/mixer_forward/pallas_call | solution.py:394
  111.4 11.0 %head_outputs.1 = (f32[1024,512]{1,0:T(8,128)}, bf16[1024,512]{1,0:T(8,128)(2,1)}, bf16[512,2048]{1,0:T(8,128)(2,1)}, bf16[512,2048]{1,0:T(8,128)(2,1)}) custom-call(bf16[1024,2048]{1,0:T(8,128)(2,1)} %copy-done.7, f32[1024,512]{1,0:T(8,128)} %copy-done, bf16[4,2,512,512]{3,2,1,0:T(8,128)(2,1)} %bitcast.77, f32[1,256]{1,0:T(1,128)} %reshape.231.gain_ref.refs_18_), custom_call_target="tpu_custom_call" | custom-call | flops 1 | bytes 1 | tf_op jit(solution)/shard_map/head_outputs/pallas_call | solution.py:667
  125.0 4.0 collective-permute-done.8
  132.1 3.4 collective-permute-start.9
  135.5 10.9 %collective-permute-done.9 = bf16[128,2048]{1,0:T(8,128)(2,1)S(1)} collective-permute-done((bf16[128,2048]{1,0:T(8,128)(2,1)S(1)}, bf16[128,2048]{1,0:T(8,128)(2,1)S(1)}, u32[]{:S(2)}, u32[]{:S(2)}) %collective-permute-start.9) | collective-permute-done | bytes 524320 | tf_op jit(solution)/shard_map/ppermute | solution.py:1037
  146.7 4.2 collective-permute-start.10
  151.7 9.4 %collective-permute-done.10 = bf16[128,2048]{1,0:T(8,128)(2,1)S(1)} collective-permute-done((bf16[128,2048]{1,0:T(8,128)(2,1)S(1)}, bf16[128,2048]{1,0:T(8,128)(2,1)S(1)}, u32[]{:S(2)}, u32[]{:S(2)}) %collective-permute-start.10) | collective-permute-done | bytes 524320 | tf_op jit(solution)/shard_map/ppermute | solution.py:1037
  162.2 6.5 %collective-permute-start.11 = (bf16[128,2048]{1,0:T(8,128)(2,1)}, bf16[128,2048]{1,0:T(8,128)(2,1)S(1)}, u32[]{:S(2)}, u32[]{:S(2)}) collective-permute-start(bf16[128,2048]{1,0:T(8,128)(2,1)} %get-tuple-element.239), channel_id=1, source_target_pairs={{0,1},{1,2},{2,3},{4,5},{5,6},{6,7},{8,9},{9,10},{10,11},{12,13},{... | collective-permute-start | bytes 1572872 | tf_op jit(solution)/shard_map/ppermute | solution.py:1037
  170.1 7.9 %collective-permute-done.11 = bf16[128,2048]{1,0:T(8,128)(2,1)S(1)} collective-permute-done((bf16[128,2048]{1,0:T(8,128)(2,1)}, bf16[128,2048]{1,0:T(8,128)(2,1)S(1)}, u32[]{:S(2)}, u32[]{:S(2)}) %collective-permute-start.11) | collective-permute-done | bytes 524320 | tf_op jit(solution)/shard_map/ppermute | solution.py:1037
  185.0 4.0 collective-permute-start.15
  189.0 6.7 %collective-permute-done.16 = bf16[128,2048]{1,0:T(8,128)(2,1)S(1)} collective-permute-done((bf16[128,2048]{1,0:T(8,128)(2,1)S(1)}, bf16[128,2048]{1,0:T(8,128)(2,1)S(1)}, u32[]{:S(2)}, u32[]{:S(2)}) %collective-permute-start.16) | collective-permute-done | bytes 524320 | tf_op jit(solution)/shard_map/ppermute | solution.py:1051
  197.7 9.2 %collective-permute-done.17 = bf16[128,2048]{1,0:T(8,128)(2,1)S(1)} collective-permute-done((bf16[128,2048]{1,0:T(8,128)(2,1)S(1)}, bf16[128,2048]{1,0:T(8,128)(2,1)S(1)}, u32[]{:S(2)}, u32[]{:S(2)}) %collective-permute-start.17) | collective-permute-done | bytes 524320 | tf_op jit(solution)/shard_map/ppermute | solution.py:1051
  209.3 5.1 collective-permute-start.22
  217.7 6.0 collective-permute-start.21
  227.6 17.0 %feed_forward.3 = (bf16[3,512,704]{2,1,0:T(8,128)(2,1)}, bf16[512,2048]{1,0:T(8,128)(2,1)}, bf16[512,2048]{1,0:T(8,128)(2,1)}) custom-call(bf16[512,2048]{1,0:T(8,128)(2,1)} %collective-permute-done.21.hidden_ref.h_other, bf16[512,2048]{1,0:T(8,128)(2,1)} %copy-done.14, bf16[4,3,512,704]{3,2,1,0:T(8,128)(2,1)} %bitcast.80), custom_call_target="tpu_custom_call" | custom-call | flops 1 | bytes 1 | tf_op jit(solution)/shard_map/feed_forward/pallas_call | solution.py:725
  245.0 17.0 %feed_forward.2 = (bf16[3,512,704]{2,1,0:T(8,128)(2,1)}, bf16[512,2048]{1,0:T(8,128)(2,1)}, bf16[512,2048]{1,0:T(8,128)(2,1)}) custom-call(bf16[512,2048]{1,0:T(8,128)(2,1)} %copy-done.11, bf16[512,2048]{1,0:T(8,128)(2,1)} %get-tuple-element.126.branch_ref.b_own, bf16[4,3,512,704]{3,2,1,0:T(8,128)(2,1)} %bitcast.81), custom_call_target="tpu_custom_call" | custom-call | flops 1 | bytes 1 | tf_op jit(solution)/shard_map/feed_forward/pallas_call | solution.py:725
  265.8 3.4 collective-permute-start.24
  269.6 15.3 %feed_grads.1 = bf16[2048,2176]{1,0:T(8,128)(2,1)} custom-call(bf16[512,2048]{1,0:T(8,128)(2,1)} %copy-done.11, bf16[512,2048]{1,0:T(8,128)(2,1)} %collective-permute-done.21.hidden_ref.h_other, bf16[512,2048]{1,0:T(8,128)(2,1)} %get-tuple-element.126.branch_ref.b_own, bf16[512,2048]{1,0:T(8,128)(2,1)} %copy-done.14, ...), custom_call_target="tpu_custom_call" | custom-call | flops 1 | bytes 1 | tf_op jit(solution)/shard_map/feed_grads/pallas_call | solution.py:758
  284.9 4.4 add_convert_fusion.1
  289.4 23.9 %collective-permute-done.25 = bf16[128,2048]{1,0:T(8,128)(2,1)} collective-permute-done((bf16[128,2048]{1,0:T(8,128)(2,1)}, bf16[128,2048]{1,0:T(8,128)(2,1)}, u32[]{:S(2)}, u32[]{:S(2)}) %collective-permute-start.25) | collective-permute-done | bytes 524320 | tf_op jit(solution)/shard_map/ppermute | solution.py:1014
  319.6 4.0 collective-permute-start.28
  323.6 9.2 %collective-permute-done.29 = bf16[128,2048]{1,0:T(8,128)(2,1)S(1)} collective-permute-done((bf16[128,2048]{1,0:T(8,128)(2,1)S(1)}, bf16[128,2048]{1,0:T(8,128)(2,1)S(1)}, u32[]{:S(2)}, u32[]{:S(2)}) %collective-permute-start.29) | collective-permute-done | bytes 524320 | tf_op jit(solution)/shard_map/ppermute | solution.py:1051
  334.8 12.4 %collective-permute-done.30 = bf16[128,2048]{1,0:T(8,128)(2,1)S(1)} collective-permute-done((bf16[128,2048]{1,0:T(8,128)(2,1)S(1)}, bf16[128,2048]{1,0:T(8,128)(2,1)S(1)}, u32[]{:S(2)}, u32[]{:S(2)}) %collective-permute-start.30) | collective-permute-done | bytes 524320 | tf_op jit(solution)/shard_map/ppermute | solution.py:1051
  349.4 11.0 %collective-permute-done.31 = bf16[128,2048]{1,0:T(8,128)(2,1)S(1)} collective-permute-done((bf16[128,2048]{1,0:T(8,128)(2,1)S(1)}, bf16[128,2048]{1,0:T(8,128)(2,1)S(1)}, u32[]{:S(2)}, u32[]{:S(2)}) %collective-permute-start.31) | collective-permute-done | bytes 524320 | tf_op jit(solution)/shard_map/ppermute | solution.py:1051
  360.9 3.1 collective-permute-start.37
  365.2 4.2 collective-permute-start.34
  371.0 35.2 %mixer_backward.1 = (bf16[1024,1664]{1,0:T(8,128)(2,1)}, f32[8,1024]{1,0:T(8,128)}, f32[8,128]{1,0:T(8,128)}, f32[8,256]{1,0:T(8,128)}) custom-call(s32[8]{0:T(128)} %copy-done.6, f32[1024,1152]{1,0:T(8,128)} %fusion.38.refs_0_.refs_1_, f32[1024,1152]{1,0:T(8,128)} %fusion.38.refs_0_.refs_1_, f32[1024,1024]{1,0:T(8,128)} %get-tuple-element.140.refs_2_, ...), custom_call_target="tpu_custom_call" | custom-call | flops 1 | bytes 1 | tf_op jit(solution)/shard_map/mixer_backward/pallas_call | solution.py:444
  406.2 5.5 collective-permute-done.35
  413.4 4.6 collective-permute-start.38
  419.3 14.1 %d_normed_rows.1 = (bf16[512,2048]{1,0:T(8,128)(2,1)}, bf16[512,2048]{1,0:T(8,128)(2,1)}, f32[8,2048]{1,0:T(8,128)}) custom-call(bf16[1024,1664]{1,0:T(8,128)(2,1)} %get-tuple-element.164.mix_ref, bf16[1024,2048]{1,0:T(8,128)(2,1)} %copy-done.7, bf16[2048,1152]{1,0:T(8,128)(2,1)} %copy-done.10, bf16[4,2,512,512]{3,2,1,0:T(8,128)(2,1)} %bitcast.79), custom_call_target="tpu_custom_call" | custom-call | flops 1 | bytes 1 | tf_op jit(solution)/shard_map/d_normed_rows/pallas_call | solution.py:800
  436.1 6.1 %out_grads.1 = bf16[2048,512]{1,0:T(8,128)(2,1)} custom-call(bf16[512,2048]{1,0:T(8,128)(2,1)} %copy-done.8, bf16[512,2048]{1,0:T(8,128)(2,1)} %copy-done.9, bf16[1024,512]{1,0:T(8,128)(2,1)} %get-tuple-element.161.heads_ref), custom_call_target="tpu_custom_call" | custom-call | flops 1 | bytes 1 | tf_op jit(solution)/shard_map/out_grads/pallas_call | solution.py:856
  448.2 15.6 %collective-permute-done.41.refs_5_ = bf16[128,2048]{1,0:T(8,128)(2,1)} collective-permute-done((bf16[128,2048]{1,0:T(8,128)(2,1)S(1)}, bf16[128,2048]{1,0:T(8,128)(2,1)}, u32[]{:S(2)}, u32[]{:S(2)}) %collective-permute-start.41) | collective-permute-done | bytes 524320 | tf_op jit(solution)/shard_map/ppermute | solution.py:1059
  470.2 12.1 %mix_grads.1 = bf16[2048,1664]{1,0:T(8,128)(2,1)} custom-call(bf16[1024,2048]{1,0:T(8,128)(2,1)} %copy-done.7, bf16[1024,1664]{1,0:T(8,128)(2,1)} %get-tuple-element.164.mix_ref), custom_call_target="tpu_custom_call" | custom-call | flops 1 | bytes 1 | tf_op jit(solution)/shard_map/mix_grads/pallas_call | solution.py:831
  482.3 29.8 %collective-permute-done.44 = bf16[128,2048]{1,0:T(8,128)(2,1)S(1)} collective-permute-done((bf16[128,2048]{1,0:T(8,128)(2,1)}, bf16[128,2048]{1,0:T(8,128)(2,1)S(1)}, u32[]{:S(2)}, u32[]{:S(2)}) %collective-permute-start.44) | collective-permute-done | bytes 524320 | tf_op jit(solution)/shard_map/ppermute | solution.py:1014
  525.9 11.4 %collective-permute-done.57 = f32[4352]{0:T(1024)S(1)} collective-permute-done((f32[4352]{0:T(1024)S(1)}, f32[4352]{0:T(1024)S(1)}, u32[]{:S(2)}, u32[]{:S(2)}) %collective-permute-start.57) | collective-permute-done | bytes 17440 | tf_op jit(solution)/shard_map/ppermute | solution.py:1071
  541.0 4.2 place.2
  545.9 6.9 %finish_wide.1 = (f32[512,1408]{1,0:T(8,128)}, f32[512,1408]{1,0:T(8,128)}, f32[1408,512]{1,0:T(8,128)}, f32[1024,512]{1,0:T(8,128)}) custom-call(s32[1]{0:T(128)} %bitcast.3.core_ref, bf16[512,2176]{1,0:T(8,128)(2,1)} %reduce-scatter.4.cloned.1.call-done.own_ref, bf16[512,2176]{1,0:T(8,128)(2,1)} %collective-permute-done.50.other_ref, ...), custom_call_target="tpu_custom_call" | custom-call | flops 1 | bytes 1 | tf_op jit(solution)/shard_map/finish_wide/pallas_call | solution.py:927
  557.8 3.5 collective-permute-start.62
  563.3 4.1 collective-permute-done.54.refs_5_
  569.6 9.6 %collective-permute-done.55.refs_6_ = bf16[128,2048]{1,0:T(8,128)(2,1)S(1)} collective-permute-done((bf16[128,2048]{1,0:T(8,128)(2,1)S(1)}, bf16[128,2048]{1,0:T(8,128)(2,1)S(1)}, u32[]{:S(2)}, u32[]{:S(2)}) %collective-permute-start.55) | collective-permute-done | bytes 524320 | tf_op jit(solution)/shard_map/ppermute | solution.py:1059
  580.0 4.3 place.3
  593.8 5.0 finish_mix.1
  (301 shorter events, 134.3 us)
Async XLA Ops:
  7.2 104.2 %all-gather.3.cloned.1.call-start = ((), (), s32[]{:S(2)}) async-start(), calls=%async_computation.3 | async-start | bytes 5242880 | tf_op jit(solution)/shard_map/all_gather | solution.py:1171
  14.3 12.2 %collective-permute-start.2 = (bf16[2112]{0:T(1024)(128)(2,1)S(1)}, bf16[2112]{0:T(1024)(128)(2,1)S(1)}, u32[]{:S(2)}, u32[]{:S(2)}) collective-permute-start(bf16[2112]{0:T(1024)(128)(2,1)S(1)} %concatenate.37), channel_id=1, source_target_pairs={{0,8},{8,0},{16,24},{24,16},{1,9},{9,1},{17,25},{25,17},{2,10},{10... | collective-permute-start | bytes 12680 | tf_op jit(solution)/shard_map/ppermute | solution.py:981
  17.6 26.6 %collective-permute-start = (bf16[512,1152]{1,0:T(8,128)(2,1)}, bf16[512,1152]{1,0:T(8,128)(2,1)S(1)}, u32[]{:S(2)}, u32[]{:S(2)}) collective-permute-start(bf16[512,1152]{1,0:T(8,128)(2,1)} %pack_mix.1), channel_id=1, source_target_pairs={{0,8},{8,0},{16,24},{24,16},{1,9},{9,1},{17,25},{25,17},{2,10},{10... | collective-permute-start | bytes 3538952 | tf_op jit(solution)/shard_map/ppermute | solution.py:981
  19.0 26.0 %collective-permute-start.1 = (bf16[512,1152]{1,0:T(8,128)(2,1)}, bf16[512,1152]{1,0:T(8,128)(2,1)S(1)}, u32[]{:S(2)}, u32[]{:S(2)}) collective-permute-start(bf16[512,1152]{1,0:T(8,128)(2,1)} %pack_mix.1), channel_id=1, source_target_pairs={{0,16},{8,24},{16,0},{24,8},{1,17},{9,25},{17,1},{25,9},{2,18},{10... | collective-permute-start | bytes 3538952 | tf_op jit(solution)/shard_map/ppermute | solution.py:981
  45.0 182.5 %all-gather.5.cloned.1.call-start = ((), (), s32[]{:S(2)}) async-start(), calls=%async_computation.4 | async-start | bytes 11796480 | tf_op jit(solution)/shard_map/all_gather | solution.py:1176
  45.1 27.9 %collective-permute-start.5 = (bf16[512,2048]{1,0:T(8,128)(2,1)}, bf16[512,2048]{1,0:T(8,128)(2,1)}, u32[]{:S(2)}, u32[]{:S(2)}) collective-permute-start(bf16[512,2048]{1,0:T(8,128)(2,1)} %get-tuple-element.115), channel_id=1, source_target_pairs={{0,4},{4,0},{1,5},{5,1},{2,6},{6,2},{3,7},{7,3},{8,12},{12,8},{9,1... | collective-permute-start | bytes 6291464 | tf_op jit(solution)/shard_map/ppermute | solution.py:985
  49.3 20.6 %collective-permute-start.6 = (bf16[256,1152]{1,0:T(8,128)(2,1)S(1)}, bf16[256,1152]{1,0:T(8,128)(2,1)S(1)}, u32[]{:S(2)}, u32[]{:S(2)}) collective-permute-start(bf16[256,1152]{1,0:T(8,128)(2,1)S(1)} %slice.160), channel_id=1, source_target_pairs={{0,16},{8,24},{16,0},{24,8},{1,17},{9,25},{17,1},{25,9},{2,18},{10... | collective-permute-start | bytes 1769480 | tf_op jit(solution)/shard_map/ppermute | solution.py:981
  50.9 22.0 %collective-permute-start.7 = (bf16[256,1152]{1,0:T(8,128)(2,1)S(1)}, bf16[256,1152]{1,0:T(8,128)(2,1)S(1)}, u32[]{:S(2)}, u32[]{:S(2)}) collective-permute-start(bf16[256,1152]{1,0:T(8,128)(2,1)S(1)} %slice.161), channel_id=1, source_target_pairs={{0,8},{8,0},{16,24},{24,16},{1,9},{9,1},{17,25},{25,17},{2,10},{10... | collective-permute-start | bytes 1769480 | tf_op jit(solution)/shard_map/ppermute | solution.py:981
  85.5 327.9 %reduce-scatter.4.cloned.1.call-start = ((), (), s32[]{:S(2)}) async-start(), calls=%async_computation.5 | async-start | bytes 11141120 | tf_op jit(solution)/shard_map/reduce_scatter | solution.py:1007
  132.1 14.2 %collective-permute-start.9 = (bf16[128,2048]{1,0:T(8,128)(2,1)S(1)}, bf16[128,2048]{1,0:T(8,128)(2,1)S(1)}, u32[]{:S(2)}, u32[]{:S(2)}) collective-permute-start(bf16[128,2048]{1,0:T(8,128)(2,1)S(1)} %get-tuple-element.243), channel_id=1, source_target_pairs={{0,1},{4,5},{8,9},{12,13},{16,17},{20,21},{24,25},{28,29}} | collective-permute-start | bytes 1572872 | tf_op jit(solution)/shard_map/ppermute | solution.py:1037
  146.7 14.3 %collective-permute-start.10 = (bf16[128,2048]{1,0:T(8,128)(2,1)S(1)}, bf16[128,2048]{1,0:T(8,128)(2,1)S(1)}, u32[]{:S(2)}, u32[]{:S(2)}) collective-permute-start(bf16[128,2048]{1,0:T(8,128)(2,1)S(1)} %get-tuple-element.241), channel_id=1, source_target_pairs={{0,1},{1,2},{4,5},{5,6},{8,9},{9,10},{12,13},{13,14},{16,17},{17,1... | collective-permute-start | bytes 1572872 | tf_op jit(solution)/shard_map/ppermute | solution.py:1037
  162.2 15.8 %collective-permute-start.11 = (bf16[128,2048]{1,0:T(8,128)(2,1)}, bf16[128,2048]{1,0:T(8,128)(2,1)S(1)}, u32[]{:S(2)}, u32[]{:S(2)}) collective-permute-start(bf16[128,2048]{1,0:T(8,128)(2,1)} %get-tuple-element.239), channel_id=1, source_target_pairs={{0,1},{1,2},{2,3},{4,5},{5,6},{6,7},{8,9},{9,10},{10,11},{12,13},{... | collective-permute-start | bytes 1572872 | tf_op jit(solution)/shard_map/ppermute | solution.py:1037
  168.8 12.9 %collective-permute-start.14 = (bf16[128,2048]{1,0:T(8,128)(2,1)S(1)}, bf16[128,2048]{1,0:T(8,128)(2,1)}, u32[]{:S(2)}, u32[]{:S(2)}) collective-permute-start(bf16[128,2048]{1,0:T(8,128)(2,1)S(1)} %get-tuple-element.240), channel_id=1, source_target_pairs={{1,0},{2,1},{3,2},{5,4},{6,5},{7,6},{9,8},{10,9},{11,10},{13,12},{... | collective-permute-start | bytes 1572872 | tf_op jit(solution)/shard_map/ppermute | solution.py:1038
  183.7 12.0 %collective-permute-start.16 = (bf16[128,2048]{1,0:T(8,128)(2,1)S(1)}, bf16[128,2048]{1,0:T(8,128)(2,1)S(1)}, u32[]{:S(2)}, u32[]{:S(2)}) collective-permute-start(bf16[128,2048]{1,0:T(8,128)(2,1)S(1)} %multiply_convert_fusion.1), channel_id=1, source_target_pairs={{1,0},{2,1},{3,2},{5,4},{6,5},{7,6},{9,8},{10,9},{11,10},{13,12},{... | collective-permute-start | bytes 1572872 | tf_op jit(solution)/shard_map/ppermute | solution.py:1051
  185.0 12.0 %collective-permute-start.15 = (bf16[128,2048]{1,0:T(8,128)(2,1)S(1)}, bf16[128,2048]{1,0:T(8,128)(2,1)S(1)}, u32[]{:S(2)}, u32[]{:S(2)}) collective-permute-start(bf16[128,2048]{1,0:T(8,128)(2,1)S(1)} %multiply_convert_fusion.1), channel_id=1, source_target_pairs={{0,1},{1,2},{2,3},{4,5},{5,6},{6,7},{8,9},{9,10},{10,11},{12,13},{... | collective-permute-start | bytes 1572872 | tf_op jit(solution)/shard_map/ppermute | solution.py:1049
  209.3 14.4 %collective-permute-start.22 = (bf16[512,2048]{1,0:T(8,128)(2,1)S(1)}, bf16[512,2048]{1,0:T(8,128)(2,1)S(1)}, u32[]{:S(2)}, u32[]{:S(2)}) collective-permute-start(bf16[512,2048]{1,0:T(8,128)(2,1)S(1)} %copy-done.13), channel_id=1, source_target_pairs={{0,4},{4,0},{1,5},{5,1},{2,6},{6,2},{3,7},{7,3},{8,12},{12,8},{9,1... | collective-permute-start | bytes 6291464 | tf_op jit(solution)/shard_map/ppermute | solution.py:985
  244.6 17.4 %collective-permute-start.23 = (bf16[512,2048]{1,0:T(8,128)(2,1)}, bf16[512,2048]{1,0:T(8,128)(2,1)S(1)}, u32[]{:S(2)}, u32[]{:S(2)}) collective-permute-start(bf16[512,2048]{1,0:T(8,128)(2,1)} %get-tuple-element.127), channel_id=1, source_target_pairs={{0,4},{4,0},{1,5},{5,1},{2,6},{6,2},{3,7},{7,3},{8,12},{12,8},{9,1... | collective-permute-start | bytes 6291464 | tf_op jit(solution)/shard_map/ppermute | solution.py:985
  264.4 20.6 %collective-permute-start.27 = (bf16[512,2048]{1,0:T(8,128)(2,1)}, bf16[512,2048]{1,0:T(8,128)(2,1)}, u32[]{:S(2)}, u32[]{:S(2)}) collective-permute-start(bf16[512,2048]{1,0:T(8,128)(2,1)} %get-tuple-element.134), channel_id=1, source_target_pairs={{0,4},{4,0},{1,5},{5,1},{2,6},{6,2},{3,7},{7,3},{8,12},{12,8},{9,1... | collective-permute-start | bytes 6291464 | tf_op jit(solution)/shard_map/ppermute | solution.py:985
  265.8 23.6 %collective-permute-start.24 = (bf16[128,2048]{1,0:T(8,128)(2,1)}, bf16[128,2048]{1,0:T(8,128)(2,1)}, u32[]{:S(2)}, u32[]{:S(2)}) collective-permute-start(bf16[128,2048]{1,0:T(8,128)(2,1)} %get-tuple-element.238), channel_id=1, source_target_pairs={{0,3},{1,0},{2,1},{3,2},{4,7},{5,4},{6,5},{7,6},{8,11},{9,8},{10,9... | collective-permute-start | bytes 1572872 | tf_op jit(solution)/shard_map/ppermute | solution.py:1014
  269.2 44.1 %collective-permute-start.25 = (bf16[128,2048]{1,0:T(8,128)(2,1)}, bf16[128,2048]{1,0:T(8,128)(2,1)}, u32[]{:S(2)}, u32[]{:S(2)}) collective-permute-start(bf16[128,2048]{1,0:T(8,128)(2,1)} %get-tuple-element.237), channel_id=1, source_target_pairs={{0,2},{1,3},{2,0},{3,1},{4,6},{5,7},{6,4},{7,5},{8,10},{9,11},{10,... | collective-permute-start | bytes 1572872 | tf_op jit(solution)/shard_map/ppermute | solution.py:1014
  269.2 44.1 %collective-permute-start.26 = (bf16[128,2048]{1,0:T(8,128)(2,1)}, bf16[128,2048]{1,0:T(8,128)(2,1)}, u32[]{:S(2)}, u32[]{:S(2)}) collective-permute-start(bf16[128,2048]{1,0:T(8,128)(2,1)} %get-tuple-element.236), channel_id=1, source_target_pairs={{0,1},{1,2},{2,3},{3,0},{4,5},{5,6},{6,7},{7,4},{8,9},{9,10},{10,1... | collective-permute-start | bytes 1572872 | tf_op jit(solution)/shard_map/ppermute | solution.py:1014
  313.3 211.8 %reduce-scatter.6.cloned.1.call-start = ((), (), s32[]{:S(2)}) async-start(), calls=%async_computation.6 | async-start | bytes 2621440 | tf_op jit(solution)/shard_map/reduce_scatter | solution.py:1007
  318.3 14.5 %collective-permute-start.29 = (bf16[128,2048]{1,0:T(8,128)(2,1)S(1)}, bf16[128,2048]{1,0:T(8,128)(2,1)S(1)}, u32[]{:S(2)}, u32[]{:S(2)}) collective-permute-start(bf16[128,2048]{1,0:T(8,128)(2,1)S(1)} %get-tuple-element.226), channel_id=1, source_target_pairs={{1,0},{2,1},{3,2},{5,4},{6,5},{7,6},{9,8},{10,9},{11,10},{13,12},{... | collective-permute-start | bytes 1572872 | tf_op jit(solution)/shard_map/ppermute | solution.py:1051
  319.6 14.5 %collective-permute-start.28 = (bf16[128,2048]{1,0:T(8,128)(2,1)S(1)}, bf16[128,2048]{1,0:T(8,128)(2,1)S(1)}, u32[]{:S(2)}, u32[]{:S(2)}) collective-permute-start(bf16[128,2048]{1,0:T(8,128)(2,1)S(1)} %get-tuple-element.226), channel_id=1, source_target_pairs={{0,1},{1,2},{2,3},{4,5},{5,6},{6,7},{8,9},{9,10},{10,11},{12,13},{... | collective-permute-start | bytes 1572872 | tf_op jit(solution)/shard_map/ppermute | solution.py:1049
  332.8 14.4 %collective-permute-start.30 = (bf16[128,2048]{1,0:T(8,128)(2,1)S(1)}, bf16[128,2048]{1,0:T(8,128)(2,1)S(1)}, u32[]{:S(2)}, u32[]{:S(2)}) collective-permute-start(bf16[128,2048]{1,0:T(8,128)(2,1)S(1)} %collective-permute-done.29), channel_id=1, source_target_pairs={{1,0},{2,1},{5,4},{6,5},{9,8},{10,9},{13,12},{14,13},{17,16},{18,1... | collective-permute-start | bytes 1572872 | tf_op jit(solution)/shard_map/ppermute | solution.py:1051
  334.1 14.4 %collective-permute-start.32 = (bf16[128,2048]{1,0:T(8,128)(2,1)S(1)}, bf16[128,2048]{1,0:T(8,128)(2,1)S(1)}, u32[]{:S(2)}, u32[]{:S(2)}) collective-permute-start(bf16[128,2048]{1,0:T(8,128)(2,1)S(1)} %collective-permute-done.28), channel_id=1, source_target_pairs={{1,2},{2,3},{5,6},{6,7},{9,10},{10,11},{13,14},{14,15},{17,18},{18... | collective-permute-start | bytes 1572872 | tf_op jit(solution)/shard_map/ppermute | solution.py:1049
  347.2 13.1 %collective-permute-start.31 = (bf16[128,2048]{1,0:T(8,128)(2,1)S(1)}, bf16[128,2048]{1,0:T(8,128)(2,1)S(1)}, u32[]{:S(2)}, u32[]{:S(2)}) collective-permute-start(bf16[128,2048]{1,0:T(8,128)(2,1)S(1)} %collective-permute-done.30), channel_id=1, source_target_pairs={{1,0},{5,4},{9,8},{13,12},{17,16},{21,20},{25,24},{29,28}} | collective-permute-start | bytes 1572872 | tf_op jit(solution)/shard_map/ppermute | solution.py:1051
  348.5 12.0 %collective-permute-start.33 = (bf16[128,2048]{1,0:T(8,128)(2,1)S(1)}, bf16[128,2048]{1,0:T(8,128)(2,1)S(1)}, u32[]{:S(2)}, u32[]{:S(2)}) collective-permute-start(bf16[128,2048]{1,0:T(8,128)(2,1)S(1)} %collective-permute-done.32), channel_id=1, source_target_pairs={{2,3},{6,7},{10,11},{14,15},{18,19},{22,23},{26,27},{30,31}} | collective-permute-start | bytes 1572872 | tf_op jit(solution)/shard_map/ppermute | solution.py:1049
  365.2 41.0 %collective-permute-start.34 = (bf16[128,2048]{1,0:T(8,128)(2,1)}, bf16[128,2048]{1,0:T(8,128)(2,1)S(1)}, u32[]{:S(2)}, u32[]{:S(2)}) collective-permute-start(bf16[128,2048]{1,0:T(8,128)(2,1)} %get-tuple-element.235), channel_id=1, source_target_pairs={{0,3},{1,0},{2,1},{3,2},{4,7},{5,4},{6,5},{7,6},{8,11},{9,8},{10,9... | collective-permute-start | bytes 1572872 | tf_op jit(solution)/shard_map/ppermute | solution.py:1014
  369.4 42.3 %collective-permute-start.35 = (bf16[128,2048]{1,0:T(8,128)(2,1)}, bf16[128,2048]{1,0:T(8,128)(2,1)}, u32[]{:S(2)}, u32[]{:S(2)}) collective-permute-start(bf16[128,2048]{1,0:T(8,128)(2,1)} %get-tuple-element.234), channel_id=1, source_target_pairs={{0,2},{1,3},{2,0},{3,1},{4,6},{5,7},{6,4},{7,5},{8,10},{9,11},{10,... | collective-permute-start | bytes 1572872 | tf_op jit(solution)/shard_map/ppermute | solution.py:1014
  369.4 42.3 %collective-permute-start.36 = (bf16[128,2048]{1,0:T(8,128)(2,1)}, bf16[128,2048]{1,0:T(8,128)(2,1)}, u32[]{:S(2)}, u32[]{:S(2)}) collective-permute-start(bf16[128,2048]{1,0:T(8,128)(2,1)} %get-tuple-element.233), channel_id=1, source_target_pairs={{0,1},{1,2},{2,3},{3,0},{4,5},{5,6},{6,7},{7,4},{8,9},{9,10},{10,1... | collective-permute-start | bytes 1572872 | tf_op jit(solution)/shard_map/ppermute | solution.py:1014
  413.4 20.1 %collective-permute-start.38 = (bf16[128,2048]{1,0:T(8,128)(2,1)S(1)}, bf16[128,2048]{1,0:T(8,128)(2,1)S(1)}, u32[]{:S(2)}, u32[]{:S(2)}) collective-permute-start(bf16[128,2048]{1,0:T(8,128)(2,1)S(1)} %add_convert_fusion.4.refs_0_), channel_id=1, source_target_pairs={{0,1},{1,2},{2,3},{4,5},{5,6},{6,7},{8,9},{9,10},{10,11},{12,13},{... | collective-permute-start | bytes 1572872 | tf_op jit(solution)/shard_map/ppermute | solution.py:1058
  418.0 15.5 %collective-permute-start.39 = (bf16[128,2048]{1,0:T(8,128)(2,1)S(1)}, bf16[128,2048]{1,0:T(8,128)(2,1)S(1)}, u32[]{:S(2)}, u32[]{:S(2)}) collective-permute-start(bf16[128,2048]{1,0:T(8,128)(2,1)S(1)} %add_convert_fusion.4.refs_0_), channel_id=1, source_target_pairs={{1,0},{2,1},{3,2},{5,4},{6,5},{7,6},{9,8},{10,9},{11,10},{13,12},{... | collective-permute-start | bytes 1572872 | tf_op jit(solution)/shard_map/ppermute | solution.py:1059
  442.2 144.4 %reduce-scatter.8.cloned.1.call-start = ((), (), s32[]{:S(2)}) async-start(), calls=%async_computation.7 | async-start | bytes 8519680 | tf_op jit(solution)/shard_map/reduce_scatter | solution.py:1007
  443.9 19.9 %collective-permute-start.41 = (bf16[128,2048]{1,0:T(8,128)(2,1)S(1)}, bf16[128,2048]{1,0:T(8,128)(2,1)}, u32[]{:S(2)}, u32[]{:S(2)}) collective-permute-start(bf16[128,2048]{1,0:T(8,128)(2,1)S(1)} %copy-done.25), channel_id=1, source_target_pairs={{1,0},{2,1},{5,4},{6,5},{9,8},{10,9},{13,12},{14,13},{17,16},{18,1... | collective-permute-start | bytes 1572872 | tf_op jit(solution)/shard_map/ppermute | solution.py:1059
  464.9 17.3 %collective-permute-start.43 = (bf16[128,2048]{1,0:T(8,128)(2,1)}, bf16[128,2048]{1,0:T(8,128)(2,1)S(1)}, u32[]{:S(2)}, u32[]{:S(2)}) collective-permute-start(bf16[128,2048]{1,0:T(8,128)(2,1)} %get-tuple-element.232), channel_id=1, source_target_pairs={{0,3},{1,0},{2,1},{3,2},{4,7},{5,4},{6,5},{7,6},{8,11},{9,8},{10,9... | collective-permute-start | bytes 1572872 | tf_op jit(solution)/shard_map/ppermute | solution.py:1014
  464.9 47.1 %collective-permute-start.44 = (bf16[128,2048]{1,0:T(8,128)(2,1)}, bf16[128,2048]{1,0:T(8,128)(2,1)S(1)}, u32[]{:S(2)}, u32[]{:S(2)}) collective-permute-start(bf16[128,2048]{1,0:T(8,128)(2,1)} %get-tuple-element.231), channel_id=1, source_target_pairs={{0,2},{1,3},{2,0},{3,1},{4,6},{5,7},{6,4},{7,5},{8,10},{9,11},{10,... | collective-permute-start | bytes 1572872 | tf_op jit(solution)/shard_map/ppermute | solution.py:1014
  467.3 44.8 %collective-permute-start.45 = (bf16[128,2048]{1,0:T(8,128)(2,1)}, bf16[128,2048]{1,0:T(8,128)(2,1)}, u32[]{:S(2)}, u32[]{:S(2)}) collective-permute-start(bf16[128,2048]{1,0:T(8,128)(2,1)} %get-tuple-element.230), channel_id=1, source_target_pairs={{0,1},{1,2},{2,3},{3,0},{4,5},{5,6},{6,7},{7,4},{8,9},{9,10},{10,1... | collective-permute-start | bytes 1572872 | tf_op jit(solution)/shard_map/ppermute | solution.py:1014
  467.3 44.8 %collective-permute-start.46 = (bf16[128,2048]{1,0:T(8,128)(2,1)}, bf16[128,2048]{1,0:T(8,128)(2,1)}, u32[]{:S(2)}, u32[]{:S(2)}) collective-permute-start(bf16[128,2048]{1,0:T(8,128)(2,1)} %collective-permute-done.40.refs_2_), channel_id=1, source_target_pairs={{2,3},{6,7},{10,11},{14,15},{18,19},{22,23},{26,27},{30,31}} | collective-permute-start | bytes 1572872 | tf_op jit(solution)/shard_map/ppermute | solution.py:1058
  468.7 43.4 %collective-permute-start.47 = (bf16[128,2048]{1,0:T(8,128)(2,1)}, bf16[128,2048]{1,0:T(8,128)(2,1)}, u32[]{:S(2)}, u32[]{:S(2)}) collective-permute-start(bf16[128,2048]{1,0:T(8,128)(2,1)} %collective-permute-done.41.refs_5_), channel_id=1, source_target_pairs={{1,0},{5,4},{9,8},{13,12},{17,16},{21,20},{25,24},{29,28}} | collective-permute-start | bytes 1572872 | tf_op jit(solution)/shard_map/ppermute | solution.py:1059
  512.1 33.0 %collective-permute-start.50 = (bf16[512,2176]{1,0:T(8,128)(2,1)}, bf16[512,2176]{1,0:T(8,128)(2,1)}, u32[]{:S(2)}, u32[]{:S(2)}) collective-permute-start(bf16[512,2176]{1,0:T(8,128)(2,1)} %reduce-scatter.4.cloned.1.call-done.own_ref), channel_id=1, source_target_pairs={{0,4},{4,0},{1,5},{5,1},{2,6},{6,2},{3,7},{7,3},{8,12},{12,8},{9,1... | collective-permute-start | bytes 6684680 | tf_op jit(solution)/shard_map/ppermute | solution.py:985
  520.3 32.6 %collective-permute-start.48 = (bf16[128,2048]{1,0:T(8,128)(2,1)S(1)}, bf16[128,2048]{1,0:T(8,128)(2,1)S(1)}, u32[]{:S(2)}, u32[]{:S(2)}) collective-permute-start(bf16[128,2048]{1,0:T(8,128)(2,1)S(1)} %fusion.6.refs_0_), channel_id=1, source_target_pairs={{0,1},{1,2},{2,3},{4,5},{5,6},{6,7},{8,9},{9,10},{10,11},{12,13},{... | collective-permute-start | bytes 1572872 | tf_op jit(solution)/shard_map/ppermute | solution.py:1058
  521.6 31.3 %collective-permute-start.49 = (bf16[128,2048]{1,0:T(8,128)(2,1)S(1)}, bf16[128,2048]{1,0:T(8,128)(2,1)S(1)}, u32[]{:S(2)}, u32[]{:S(2)}) collective-permute-start(bf16[128,2048]{1,0:T(8,128)(2,1)S(1)} %fusion.6.refs_0_), channel_id=1, source_target_pairs={{1,0},{2,1},{3,2},{5,4},{6,5},{7,6},{9,8},{10,9},{11,10},{13,12},{... | collective-permute-start | bytes 1572872 | tf_op jit(solution)/shard_map/ppermute | solution.py:1059
  522.9 14.3 %collective-permute-start.57 = (f32[4352]{0:T(1024)S(1)}, f32[4352]{0:T(1024)S(1)}, u32[]{:S(2)}, u32[]{:S(2)}) collective-permute-start(f32[4352]{0:T(1024)S(1)} %add.278), channel_id=1, source_target_pairs={{0,1},{1,0},{2,3},{3,2},{4,5},{5,4},{6,7},{7,6},{8,9},{9,8},{10,11... | collective-permute-start | bytes 52232 | tf_op jit(solution)/shard_map/ppermute | solution.py:1071
  525.1 20.1 %collective-permute-start.51 = (bf16[512,512]{1,0:T(8,128)(2,1)}, bf16[512,512]{1,0:T(8,128)(2,1)S(1)}, u32[]{:S(2)}, u32[]{:S(2)}) collective-permute-start(bf16[512,512]{1,0:T(8,128)(2,1)} %reduce-scatter.6.cloned.1.call-done.out_own_ref), channel_id=1, source_target_pairs={{0,4},{4,0},{1,5},{5,1},{2,6},{6,2},{3,7},{7,3},{8,12},{12,8},{9,1... | collective-permute-start | bytes 1572872 | tf_op jit(solution)/shard_map/ppermute | solution.py:985
  540.9 14.0 %collective-permute-start.59 = (f32[8704]{0:T(1024)S(1)}, f32[8704]{0:T(1024)S(1)}, u32[]{:S(2)}, u32[]{:S(2)}) collective-permute-start(f32[8704]{0:T(1024)S(1)} %pad_maximum_fusion.2), channel_id=1, source_target_pairs={{0,8},{8,0},{16,24},{24,16},{1,9},{9,1},{17,25},{25,17},{2,10},{10... | collective-permute-start | bytes 104456 | tf_op jit(solution)/shard_map/ppermute | solution.py:1071
  553.6 13.7 %collective-permute-start.54 = (bf16[128,2048]{1,0:T(8,128)(2,1)S(1)}, bf16[128,2048]{1,0:T(8,128)(2,1)S(1)}, u32[]{:S(2)}, u32[]{:S(2)}) collective-permute-start(bf16[128,2048]{1,0:T(8,128)(2,1)S(1)} %collective-permute-done.49.refs_4_), channel_id=1, source_target_pairs={{1,0},{2,1},{5,4},{6,5},{9,8},{10,9},{13,12},{14,13},{17,16},{18,1... | collective-permute-start | bytes 1572872 | tf_op jit(solution)/shard_map/ppermute | solution.py:1059
  567.4 11.8 %collective-permute-start.55 = (bf16[128,2048]{1,0:T(8,128)(2,1)S(1)}, bf16[128,2048]{1,0:T(8,128)(2,1)S(1)}, u32[]{:S(2)}, u32[]{:S(2)}) collective-permute-start(bf16[128,2048]{1,0:T(8,128)(2,1)S(1)} %collective-permute-done.54.refs_5_), channel_id=1, source_target_pairs={{1,0},{5,4},{9,8},{13,12},{17,16},{21,20},{25,24},{29,28}} | collective-permute-start | bytes 1572872 | tf_op jit(solution)/shard_map/ppermute | solution.py:1059
  (58 other events, 488.3 us)
Sparse Core Ops, SparseCore 0:
  45.2 62.8 all-gather.2
  110.4 96.4 all-gather.4
  313.4 91.1 reduce-scatter.3
  442.3 35.7 reduce-scatter.5
  512.2 74.3 reduce-scatter.7

commit v2 on v1

--- a/solution.py
+++ b/solution.py
@@ -227,9 +227,9 @@
         0,
     )
     depth = side_ref.shape[2]
-    d_heads = mm(d_attn[:, :depth], side_ref[0, 1])
+    d_heads = mm(d_attn[:, :depth], side_ref[0, 0])
     for f in range(1, side_ref.shape[0]):
-        d_heads = d_heads + mm(d_attn[:, f * depth : (f + 1) * depth], side_ref[f, 1])
+        d_heads = d_heads + mm(d_attn[:, f * depth : (f + 1) * depth], side_ref[f, 0])
     gain = gain_ref[...]
 
     def piece(array, at, c, h, size):
@@ -314,17 +314,19 @@
     d_kept = [mm(n, d, NT) for n, d in zip(new, end_low)]
     d_scores = [jnp.where(causal, o[:CHUNK, key_dim:], 0.0) for o in outer]
     d_system = [jnp.where(strict, -o[CHUNK:, key_dim:], 0.0) for o in outer]
-    d_dots_k = [d * (b * r) for d, b, r in zip(d_system, beta, ratios)]
-    d_dots_q = [(d * r).astype(BF16) for d, r in zip(d_scores, ratios)]
-    near = [
-        mm(jnp.concatenate([q, (k + jnp.transpose(k)).astype(BF16)], 0), low)
-        for q, k, low in zip(d_dots_q, d_dots_k, keys_low)
+    d_dots = [
+        jnp.concatenate([(d * r).astype(BF16), (e * (b * r)).astype(BF16)], 0)
+        for d, e, b, r in zip(d_scores, d_system, beta, ratios)
     ]
-    far = [mm(q, low, TN) for q, low in zip(d_dots_q, query_low)]
+    near = [mm(d, low) for d, low in zip(d_dots, keys_low)]
+    far = [
+        mm(d, jnp.concatenate([q, k], 0), TN) for d, q, k in zip(d_dots, query_low, keys_low)
+    ]
     lanes = lax.broadcasted_iota(jnp.int32, (CHUNK, 128), 1)
     row_ids = lax.broadcasted_iota(jnp.int32, (CHUNK, 1), 0)
     d_running = [jnp.zeros((CHUNK, 128), F32) for _ in range(PER)]
     d_strengths = [jnp.zeros((CHUNK, 128), F32) for _ in range(PER)]
+    columns = [[] for _ in range(PER)]
     for i, (c, h) in enumerate(chains):
         d_query_state = outer[i][:CHUNK, :key_dim]
         d_keys_state = outer[i][CHUNK:, :key_dim]
@@ -344,13 +346,13 @@
         )
         d_run = (
             jnp.sum(joint, -1, keepdims=True)
-            - jnp.sum(jnp.transpose(joint), -1, keepdims=True)
             + decay[i] * jnp.sum(query[i] * d_query_state, -1, keepdims=True)
             - beta[i] * along
             - left
             + jnp.where(row_ids == CHUNK - 1, total, 0.0)
         )
         d_running[c] = jnp.where(lanes == h, d_run, d_running[c])
+        columns[c].append(jnp.sum(joint, 0, keepdims=True))
         d_strengths[c] = jnp.where(lanes == heads + h, d_beta, d_strengths[c])
         d_q = d_query * key_dim ** -0.5
         d_q = q_scale[i] * (d_q - q_unit[i] * jnp.sum(q_unit[i] * d_q, -1, keepdims=True))
@@ -366,7 +368,10 @@
     upper = (rows <= cols).astype(F32)
     for c in range(PER):
         strengths, shifted, scale, logdecay = rates[c][:4]
-        d_logdecay = mm_exact(upper, d_running[c])
+        turned = jnp.transpose(
+            jnp.concatenate(columns[c] + [jnp.zeros((CHUNK - heads, CHUNK), F32)], 0)
+        )
+        d_logdecay = mm_exact(upper, d_running[c] - turned)
         d_shifted = jnp.where(lanes < heads, d_logdecay * (-scale) * jax.nn.sigmoid(shifted), 0.0)
         d_params_ref[0:1, :] += jnp.sum(d_logdecay * logdecay, 0, keepdims=True)
         d_params_ref[1:2, :] += jnp.sum(d_shifted, 0, keepdims=True)
@@ -461,7 +466,9 @@
             + each((CHUNK, d_own.shape[1]), first)
             + each((CHUNK, d_own.shape[1]), second)
             + [
-                pl.BlockSpec(side.shape, lambda n, order: (0, 0, 0, 0)),
+                pl.BlockSpec(
+                    (side.shape[0], 1) + side.shape[2:], lambda n, order: (0, 1, 0, 0)
+                ),
                 pl.BlockSpec((1, val_dim), fixed),
             ],
             out_specs=[
@@ -690,8 +697,11 @@
     )(normed, mixed, side, gain)
 
 
-def feed_kernel(hidden_ref, branch_ref, wide_ref, stack_ref, d_hidden_ref, branch_out_ref):
+def feed_kernel(turns_ref, hidden_ref, branch_ref, wide_ref, stack_ref, d_hidden_ref, branch_out_ref):
     shards, _, depth, units = wide_ref.shape
+    step = pl.program_id(0)
+    rows = d_hidden_ref.shape[0] // turns_ref.shape[0]
+    blocks = hidden_ref.shape[0] // rows
 
     def forward(ref, at):
         total = mm(ref[:, :depth], wide_ref[0, at])
@@ -712,21 +722,30 @@
     stack_ref[2] = act
     for f in range(shards):
         at = slice(f * depth, (f + 1) * depth)
-        d_hidden_ref[:, at] = (
-            mm(d_gate, wide_ref[f, 0], NT) + mm(d_up, wide_ref[f, 1], NT)
-        ).astype(BF16)
+        d_hidden = (mm(d_gate, wide_ref[f, 0], NT) + mm(d_up, wide_ref[f, 1], NT)).astype(BF16)
+        for k in range(blocks):
+            place = pl.multiple_of(turns_ref[step * blocks + k] * rows, rows)
+            d_hidden_ref[pl.ds(place, rows), at] = d_hidden[k * rows : (k + 1) * rows]
         branch_out_ref[:, at] = mm(act, wide_ref[f, 2], NT).astype(BF16)
 
 
-def feed_forward(hidden, branch, wide):
+def feed_forward(turns, hidden, branch, wide):
     count, model = hidden.shape
     units = wide.shape[3]
-    row = pl.BlockSpec((TILE, model), lambda i: (i, 0))
+    tile = max(TILE, count // turns.shape[0])
+    row = pl.BlockSpec((tile, model), lambda i, turns: (i, 0))
     return pl.pallas_call(
         feed_kernel,
-        grid=(count // TILE,),
-        in_specs=[row, row, pl.BlockSpec(wide.shape, lambda i: (0, 0, 0, 0))],
-        out_specs=[pl.BlockSpec((3, TILE, units), lambda i: (0, i, 0)), row, row],
+        grid_spec=pltpu.PrefetchScalarGridSpec(
+            num_scalar_prefetch=1,
+            grid=(count // tile,),
+            in_specs=[row, row, pl.BlockSpec(wide.shape, lambda i, turns: (0, 0, 0, 0))],
+            out_specs=[
+                pl.BlockSpec((3, tile, units), lambda i, turns: (0, i, 0)),
+                pl.BlockSpec((count, model), lambda i, turns: (0, 0)),
+                row,
+            ],
+        ),
         out_shape=[
             jax.ShapeDtypeStruct((3, count, units), BF16),
             jax.ShapeDtypeStruct((count, model), BF16),
@@ -734,7 +753,7 @@
         ],
         name="feed_forward",
         **roomy(),
-    )(hidden, branch, wide)
+    )(turns, hidden, branch, wide)
 
 
 def feed_grads_kernel(h_own, h_other, b_own, b_other, s_own, s_other, out_ref):
@@ -804,7 +823,7 @@
             pl.BlockSpec((TILE, d_mix.shape[1]), here),
             pl.BlockSpec((TILE, model), here),
             pl.BlockSpec(weights.shape, fixed),
-            pl.BlockSpec(side.shape, lambda i: (0, 0, 0, 0)),
+            pl.BlockSpec((side.shape[0], 1) + side.shape[2:], lambda i: (0, 0, 0, 0)),
         ],
         out_specs=[
             pl.BlockSpec((TILE, model), other),
@@ -897,74 +916,38 @@
     )(turns, *parts)
 
 
-def finish_wide_kernel(
-    units, core_ref, own_ref, other_ref, out_own_ref, out_other_ref, gate_ref, up_ref, down_ref,
-    out_ref,
-):
+def finish_kernel(cuts, turned, core_ref, own_ref, other_ref, *refs):
     first = core_ref[0] == 0
-
-    def pair(a, b):
-        own, other = a[...].astype(F32), b[...].astype(F32)
-        return jnp.where(first, own, other), jnp.where(first, other, own)
-
-    low, high = pair(own_ref, other_ref)
-    for at, ref in ((0, gate_ref), (1, up_ref)):
-        ref[:, :units] = low[:, at * units : (at + 1) * units]
-        ref[:, units:] = high[:, at * units : (at + 1) * units]
-    down_ref[:units, :] = jnp.transpose(low[:, 2 * units : 3 * units])
-    down_ref[units:, :] = jnp.transpose(high[:, 2 * units : 3 * units])
-    low, high = pair(out_own_ref, out_other_ref)
-    tall = low.shape[1]
-    out_ref[:tall, :] = jnp.transpose(low)
-    out_ref[tall:, :] = jnp.transpose(high)
-
-
-def finish_wide(core, own, other, out_own, out_other, units):
-    depth, width = own.shape
-    tall = out_own.shape[1]
-    row = lambda size: pl.BlockSpec((128, size), lambda i, core: (i, 0))
-    column = lambda size: pl.BlockSpec((size, 128), lambda i, core: (0, i))
-    return pl.pallas_call(
-        functools.partial(finish_wide_kernel, units),
-        grid_spec=pltpu.PrefetchScalarGridSpec(
-            num_scalar_prefetch=1,
-            grid=(depth // 128,),
-            in_specs=[row(width), row(width), row(tall), row(tall)],
-            out_specs=[row(2 * units), row(2 * units), column(2 * units), column(2 * tall)],
-        ),
-        out_shape=[
-            jax.ShapeDtypeStruct((depth, 2 * units), F32),
-            jax.ShapeDtypeStruct((depth, 2 * units), F32),
-            jax.ShapeDtypeStruct((2 * units, depth), F32),
-            jax.ShapeDtypeStruct((2 * tall, depth), F32),
-        ],
-        name="finish_wide",
-        **roomy(),
-    )(core, own, other, out_own, out_other)
-
-
-def finish_mix_kernel(cuts, core_ref, a_ref, b_ref, *refs):
-    first = core_ref[0] == 0
-    own, other = a_ref[...].astype(F32), b_ref[...].astype(F32)
+    own, other = own_ref[...].astype(F32), other_ref[...].astype(F32)
     low, high = jnp.where(first, own, other), jnp.where(first, other, own)
     for (begin, size), ref in zip(cuts, refs):
         ref[:, :size] = low[:, begin : begin + size]
         ref[:, size:] = high[:, begin : begin + size]
-
-
-def finish_mix(core, own, other, cuts):
+    if turned is None:
+        return
+    begin, size = turned
+    refs[-1][:size, :] = jnp.transpose(low[:, begin : begin + size])
+    refs[-1][size:, :] = jnp.transpose(high[:, begin : begin + size])
+
+
+def finish(core, own, other, cuts, turned):
     depth, width = own.shape
     row = lambda size: pl.BlockSpec((128, size), lambda i, core: (i, 0))
+    shapes = [(depth, 2 * size) for _, size in cuts]
+    specs = [row(2 * size) for _, size in cuts]
+    if turned is not None:
+        shapes.append((2 * turned[1], depth))
+        specs.append(pl.BlockSpec((2 * turned[1], 128), lambda i, core: (0, i)))
     return pl.pallas_call(
-        functools.partial(finish_mix_kernel, cuts),
+        functools.partial(finish_kernel, cuts, turned),
         grid_spec=pltpu.PrefetchScalarGridSpec(
             num_scalar_prefetch=1,
             grid=(depth // 128,),
             in_specs=[row(width), row(width)],
-            out_specs=[row(2 * size) for _, size in cuts],
+            out_specs=specs,
         ),
-        out_shape=[jax.ShapeDtypeStruct((depth, 2 * size), F32) for _, size in cuts],
-        name="finish_mix",
+        out_shape=[jax.ShapeDtypeStruct(shape, F32) for shape in shapes],
+        name="finish",
         **roomy(),
     )(core, own, other)
 
@@ -985,9 +968,9 @@
     return lax.ppermute(value, "context", [(0, 1), (1, 0)])
 
 
-def gathered_rows(own, beside):
+def gathered_rows(own, beside, later):
     if not is_square("fsdp"):
-        return lax.all_gather(own, "fsdp", axis=0, tiled=True), beside
+        return lax.all_gather(own, "fsdp", axis=0, tiled=True), beside, later(beside)
     rows = own.shape[0]
     half = rows // 2
     along_x = across(own, 1)
@@ -995,12 +978,13 @@
     along_x, along_y, beside = lax.optimization_barrier((along_x, along_y, beside))
     low = across(along_x[:half], 2)
     high = across(along_y[half:], 1)
+    low, high, extra = lax.optimization_barrier((low, high, later(beside)))
     shard = lax.axis_index("fsdp")
     whole = jnp.zeros((4 * rows,) + own.shape[1:], own.dtype)
     for place, part in ((0, own), (1, along_x), (2, along_y)):
         whole = lax.dynamic_update_slice_in_dim(whole, part, (shard ^ place) * rows, 0)
     whole = lax.dynamic_update_slice_in_dim(whole, low, (shard ^ 3) * rows, 0)
-    return lax.dynamic_update_slice_in_dim(whole, high, (shard ^ 3) * rows + half, 0), beside
+    return lax.dynamic_update_slice_in_dim(whole, high, (shard ^ 3) * rows + half, 0), beside, extra
 
 
 def scattered(blocks):
@@ -1024,7 +1008,7 @@
     return (total, *beside) if beside else total
 
 
-def line_sum_hops(value, axis="tensor"):
+def line_sum_hops(value, beside=None, axis="tensor"):
     size = lax.axis_size(axis)
     rows = value.shape[0] // size
     block = lambda p: value[p * rows : (p + 1) * rows].astype(F32)
@@ -1038,6 +1022,8 @@
         left = lax.ppermute(
             send_l.astype(BF16), axis, [(i, i - 1) for i in range(size - step, size)]
         )
+        if beside:
+            right, left = beside(step, (right, left))
     return block(0) + right.astype(F32) + left.astype(F32)
 
 
@@ -1062,15 +1048,6 @@
 
 def flat(hops):
     return [hops[0][0]] + [hop[0] for hop in hops[1:]] + [hop[1] for hop in hops[1:]]
-
-
-def line_total(value, axis="tensor"):
-    size = lax.axis_size(axis)
-    step = 1
-    while step < size:
-        value = value + lax.ppermute(value, axis, [(i, i ^ step) for i in range(size)])
-        step *= 2
-    return value
 
 
 def core_sum(other_rows, own_rows):
@@ -1148,7 +1125,7 @@
         ((0, 6), (0, 128 - heads)),
     )
 
-    turns = (layer - jnp.arange(layers, dtype=jnp.int32)) % layers
+    turns = ((layer - jnp.arange(layers, dtype=jnp.int32)) % layers).astype(jnp.int32)
     scalars = jnp.concatenate([(core * seg).reshape(1), lengths[:1], turns]).astype(jnp.int32)
     per_core, per_block = seg // CHUNK, rows // CHUNK
     ids = jnp.arange(2 * per_core, dtype=jnp.int32)
@@ -1165,12 +1142,16 @@
     d_out_own = lax.dynamic_slice_in_dim(cotangent[0], layer * rows, rows, 0).astype(F32)
     normed_own, d_branch_own = arrange(scalars, inputs[0], cotangent[0], gain_attn, layers)
     own_side, own_feed = pack_rest(core_id, w_outgate, w_out, w_gate, w_up, w_down)
-    full_mix, (normed_own, own_side, own_feed) = gathered_rows(
-        own_mix, (normed_own, own_side, own_feed)
+    full_mix, (_, own_side, own_feed), (normed, d_branch_other) = gathered_rows(
+        own_mix,
+        (normed_own, own_side, own_feed),
+        lambda held: (
+            jnp.concatenate([held[0], swapped(held[0])], 0),
+            swapped(after(d_branch_own, held[0])),
+        ),
     )
     side = lax.all_gather(own_side, "fsdp", axis=0, tiled=True)
-    normed = jnp.concatenate([normed_own, swapped(normed_own)], 0)
-    d_branch = (d_branch_own, swapped(after(d_branch_own, full_mix)))
+    d_branch = (d_branch_own, d_branch_other)
 
     projected = dot(normed, full_mix)
     feed = lax.all_gather(after(own_feed, projected), "fsdp", axis=0, tiled=True)
@@ -1187,14 +1168,16 @@
     hidden_mine = jnp.concatenate(line_gather(hidden_own), 0)
     hidden = (hidden_mine, swapped(hidden_mine))
 
-    stack_own, d_hidden_mine, branch_mine = feed_forward(hidden[0], d_branch[0], feed)
-    stack_other, d_hidden_other, branch_other = feed_forward(hidden[1], d_branch[1], feed)
+    stack_own, d_hidden_mine, branch_mine = feed_forward(turns, hidden[0], d_branch[0], feed)
+    stack_other, d_hidden_other, branch_other = feed_forward(turns, hidden[1], d_branch[1], feed)
     d_hidden_core = core_sum(d_hidden_other, d_hidden_mine)
+    d_hidden = lax.psum_scatter(d_hidden_core, "tensor", scatter_dimension=0, tiled=True)
     held = lax.optimization_barrier((stack_own, stack_other, branch_other, d_hidden_core))
     grad_feed = feed_grads(hidden, d_branch, held[:2], shards)
     branch_core = core_sum(held[2], branch_mine)
-    d_hidden, grad_feed, branch_core = line_sum(d_hidden_core, (grad_feed, branch_core))
+    d_hidden, grad_feed, branch_core = lax.optimization_barrier((d_hidden, grad_feed, branch_core))
     sum_feed = scattered(grad_feed)
+    d_hidden = d_hidden.astype(F32)
 
     grad_mlp = jnp.sum(d_hidden * middle * mlp_scale, 0)
     d_middle = d_out_own + norm_back(d_hidden, middle, mlp_scale, gain_mlp)
@@ -1221,20 +1204,63 @@
     hops.append(line_hop(*hops[-1], 2))
     grad_out = out_grads(*d_attn, heads_out, shards)
     d_normed_other, grad_out = lax.optimization_barrier((swapped(d_normed_other), grad_out))
+    sum_out = scattered(grad_out)
     d_normed_core = (d_normed_mine.astype(F32) + d_normed_other.astype(F32)).astype(BF16)
-    sum_out = scattered(grad_out)
-    hops[2], d_normed_core = lax.optimization_barrier((hops[2], d_normed_core))
-    for step in range(3, layers):
-        hops.append(line_hop(*hops[-1], step))
-
-    grad_mix = mix_grads(normed, after(d_mix, d_normed_core), shards)
-    d_normed, grad_mix, hops = line_sum(d_normed_core, (grad_mix, hops))
-    low_mix = scattered(grad_mix)
-
-    vector = after(jnp.concatenate([weighted[0] / gain_attn[0], grad_mlp, d_gain[0]]), grad_mix)
-    vector = line_total(line_total(vector, "context"), "tensor")
-    vector = jnp.concatenate([vector, d_taps[:taps_count].reshape(-1), d_params[:2].reshape(-1)])
-    vector = line_total(vector, "fsdp")
+
+    small_sum = {"value": jnp.concatenate([weighted[0] / gain_attn[0], grad_mlp, d_gain[0]])}
+    axes = ("context", "tensor", "fsdp")
+    pairs = [
+        (axis, 1 << k) for axis in axes for k in range((lax.axis_size(axis) - 1).bit_length())
+    ]
+    taps_line = jnp.concatenate([d_taps[:taps_count].reshape(-1), d_params[:2].reshape(-1)])
+
+    def advance(hop):
+        if not pairs:
+            return hop
+        axis, flip = pairs.pop(0)
+        value = small_sum["value"]
+        if axis == "fsdp" and flip == 1:
+            value = jnp.concatenate([value, taps_line])
+        value = after(value, d_normed_core)
+        other = lax.ppermute(value, axis, [(i, i ^ flip) for i in range(lax.axis_size(axis))])
+        hop, other = lax.optimization_barrier((hop, other))
+        small_sum["value"] = value + other
+        return hop
+
+    work = {}
+
+    def with_rest(step, hop):
+        if step == 1:
+            grad_mix = mix_grads(normed, after(d_mix, d_normed_core), shards)
+            hop, hops[:], grad_mix = lax.optimization_barrier((hop, hops, grad_mix))
+            work["mix"] = scattered(grad_mix)
+        else:
+            while len(hops) < (layers if step == layers - 1 else step + 2):
+                hops.append(line_hop(*hops[-1], len(hops)))
+        if step == 2:
+            done = finish(
+                core_id, sum_feed, swapped(sum_feed), ((0, units), (units, units)),
+                (2 * units, units),
+            )
+            hop, work["feed"], hops[:] = lax.optimization_barrier((hop, done, hops))
+        if step == 3:
+            hop, work["output"] = lax.optimization_barrier((hop, place(turns, flat(hops))))
+        return advance(hop)
+
+    d_normed = line_sum_hops(d_normed_core, with_rest)
+    output = work["output"] if "output" in work else place(turns, flat(hops))
+    d_tokens = norm_back(d_normed, tokens_own, norm_parts(tokens_own, 1e-6), gain_attn)
+    grad_own = (d_middle + d_tokens).astype(BF16)
+    back = [(grad_own, grad_own)]
+    for step in range(1, layers):
+        hop = line_hop(*back[-1], step)
+        if step == 1:
+            out_done = finish(core_id, sum_out, swapped(sum_out), (), (0, tall))
+            hop, (g_out,) = lax.optimization_barrier((hop, out_done))
+        back.append(advance(hop))
+    while pairs:
+        advance(())
+    vector = small_sum["value"]
     g_attn = lax.dynamic_slice_in_dim(vector, shard * depth, depth, 0)
     g_mlp = lax.dynamic_slice_in_dim(vector, model + shard * depth, depth, 0)
     g_head = lax.dynamic_slice_in_dim(vector, 2 * model + shard * val_part, val_part, 0)
@@ -1254,24 +1280,13 @@
         tap_grad(0, key_dim), tap_grad(wide, key_dim), tap_grad(2 * wide, val_dim)
     )
 
-    d_tokens = norm_back(d_normed, tokens_own, norm_parts(tokens_own, 1e-6), gain_attn)
-    grad_own = (d_middle + d_tokens).astype(BF16)
-    back = [(grad_own, grad_own)]
-    for step in range(1, layers):
-        back.append(line_hop(*back[-1], step))
-        if step == 1:
-            output = place(turns, flat(hops))
-            done = finish_wide(
-                core_id, sum_feed, swapped(sum_feed), sum_out, swapped(sum_out), units
-            )
-            back[1], output, done = lax.optimization_barrier((back[1], output, done))
-    g_gate, g_up, g_down, g_out = done
+    g_gate, g_up, g_down = work["feed"]
     input_grad = place(turns, flat(back))[None]
-    low_mix, input_grad = lax.optimization_barrier((low_mix, input_grad))
+    low_mix, input_grad = lax.optimization_barrier((work["mix"], input_grad))
     other_mix = swapped(low_mix)
-    g_query, g_key, g_value, g_outgate = finish_mix(
+    g_query, g_key, g_value, g_outgate = finish(
         core_id, low_mix, other_mix,
-        ((0, wide), (wide, wide), (2 * wide, tall), (side_at, tall)),
+        ((0, wide), (wide, wide), (2 * wide, tall), (side_at, tall)), None,
     )
 
     def narrow(begin):

time: 612 us -> 596 us (0.974)
  waiting for transfers between devices: 228 us -> 195 us
  starting transfers between devices: 107 us -> 122 us
    ppermute x9 -> x3, waiting for transfers between devices: 59.2 us -> 8.47 us  [line_sum(): lax.ppermute(value[p * rows:(p + 1) * rows], axis, [(i, (i - p) % size) f...]
    reduce_scatter x0 -> x1, waiting for transfers between devices: none -> 23.3 us  [on_device(): lax.psum_scatter(d_hidden_core, 'tensor', scatter_dimension=0, tiled=True)]
    ppermute x3 -> x6, starting transfers between devices: 14.1 us -> 28.8 us  [line_sum_hops(): lax.ppermute(send_r.astype(BF16), axis, [(i, i + 1) for i in range(step)])]
    ppermute x5, waiting for transfers between devices: 15.3 us -> 7.84 us  [advance(): lax.ppermute(value, axis, [(i, i ^ flip) for i in range(lax.axis_size(axi...]
    pallas_call x4 -> x5, Pallas kernels: 45.9 us -> 51.4 us  [the longest x2 36.1 us: feed_forward(): pl.pallas_call(feed_kernel, grid_spec=pltpu.PrefetchScalarGridSpec(num_sc...]
    ppermute x3 -> x6, waiting for transfers between devices: 28.2 us -> 27.5 us  [line_sum_hops(): lax.ppermute(send_r.astype(BF16), axis, [(i, i + 1) for i in range(step)])]
    unnamed x82 -> x89, local copies, waits for them, and re-layouts: 14.2 us -> 14.7 us
  transfers between devices with their start and end apart: 68 -> 69, of which waited for: 26 -> 27; matrix products, arithmetic and copies ran while one was open for 9% -> 8% of each run, Pallas kernels for 26% -> 27%
where the time goes in v2:
time: 596 us; the launch traced here: 589 us
  waiting for transfers between devices  195 us (33%)
  Pallas kernels  183 us (31%)
  starting transfers between devices  122 us (20%)
  other arithmetic  34.3 us (6%)
  local copies, waits for them, and re-layouts  30.3 us (5%)
  between operations  16.4 us (3%)
  matrix products  7.12 us (1%)
    ppermute x6, waiting for transfers between devices, line_gather(): lax.ppermute(lefts[-1], axis, [(i, i - 1) for i in range(1, size - step +...  55.8 us
    pallas_call x2, Pallas kernels, feed_forward(): pl.pallas_call(feed_kernel, grid_spec=pltpu.PrefetchScalarGridSpec(num_sc...  36.1 us
    pallas_call x1, Pallas kernels, mixer_backward(): pl.pallas_call(functools.partial(backward_kernel, heads, key_dim, val_dim...  32.1 us
    ppermute x7, waiting for transfers between devices, across(): return lax.ppermute(value, 'fsdp', [(i, i ^ flip) for i in range(4)])  30.8 us
    ppermute x6, starting transfers between devices, line_sum_hops(): lax.ppermute(send_r.astype(BF16), axis, [(i, i + 1) for i in range(step)])  28.8 us
    ppermute x6, waiting for transfers between devices, line_sum_hops(): lax.ppermute(send_r.astype(BF16), axis, [(i, i + 1) for i in range(step)])  27.5 us
    ppermute x6, waiting for transfers between devices, line_hop(): lax.ppermute(left, axis, [(i, i - 1) for i in range(1, size - step + 1)])  26.8 us
    ppermute x12, starting transfers between devices, swapped(): return lax.ppermute(value, 'context', [(0, 1), (1, 0)])  26.3 us
  transfers between devices with their start and end apart: 69, of which 27 were waited for; matrix products, arithmetic and copies ran while one was open for 8% of the time, Pallas kernels for 27%

profile of v2, /device:TPU:1, one launch (start us, length us, event | category | flops | bytes accessed | tf_op | source)
XLA Modules:
  0.0 588.9 jit_solution(1556604914802276203)
XLA Ops:
  21.5 5.0 pack_rest.1
  27.4 5.6 arrange.1
  33.0 11.1 %collective-permute-done = bf16[512,1152]{1,0:T(8,128)(2,1)S(1)} collective-permute-done((bf16[512,1152]{1,0:T(8,128)(2,1)}, bf16[512,1152]{1,0:T(8,128)(2,1)S(1)}, u32[]{:S(2)}, u32[]{:S(2)}) %collective-permute-start) | collective-permute-done | bytes 1179680 | tf_op jit(solution)/shard_map/ppermute | solution.py:964
  55.5 16.3 %collective-permute-done.5 = bf16[256,1152]{1,0:T(8,128)(2,1)S(1)} collective-permute-done((bf16[256,1152]{1,0:T(8,128)(2,1)S(1)}, bf16[256,1152]{1,0:T(8,128)(2,1)S(1)}, u32[]{:S(2)}, u32[]{:S(2)}) %collective-permute-start.5) | collective-permute-done | bytes 589856 | tf_op jit(solution)/shard_map/ppermute | solution.py:964
  76.7 7.1 %fusion.46.refs_0_.refs_1_ = f32[1024,1152]{1,0:T(8,128)} fusion(bf16[1024,2048]{1,0:T(8,128)(2,1)S(1)} %pad_maximum_fusion.normed_ref, bf16[2048,1152]{1,0:T(8,128)(2,1)S(1)} %constant_dynamic-update-slice_fusion.weights_ref), kind=kOutput, calls=%fused_computation.134 | convolution fusion | flops 4831838208 | bytes 13631488 | tf_op jit(solution)/shard_map/dot_general | solution.py:1058
  86.1 19.5 %mixer_forward.1 = (f32[1024,512]{1,0:T(8,128)S(1)}, bf16[2048,256]{1,0:T(8,128)(2,1)S(1)}, bf16[2048,128]{1,0:T(8,128)(2,1)S(1)}, bf16[1024,512]{1,0:T(8,128)(2...) custom-call(s32[8]{0:T(128)S(1)} %fusion.32.order_ref, f32[1024,1152]{1,0:T(8,128)} %fusion.46.refs_0_.refs_1_, ...), custom_call_target="tpu_custom_call" | custom-call | flops 1 | bytes 1 | tf_op jit(solution)/shard_map/mixer_forward/pallas_call | solution.py:399
  109.7 10.9 %head_outputs.1 = (f32[1024,512]{1,0:T(8,128)}, bf16[1024,512]{1,0:T(8,128)(2,1)}, bf16[512,2048]{1,0:T(8,128)(2,1)}, bf16[512,2048]{1,0:T(8,128)(2,1)}) custom-call(bf16[1024,2048]{1,0:T(8,128)(2,1)} %copy-done.7, f32[1024,512]{1,0:T(8,128)} %copy-done, bf16[4,2,512,512]{3,2,1,0:T(8,128)(2,1)} %bitcast.82, f32[1,256]{1,0:T(1,128)} %reshape.230.gain_ref.refs_18_), custom_call_target="tpu_custom_call" | custom-call | flops 1 | bytes 1 | tf_op jit(solution)/shard_map/head_outputs/pallas_call | solution.py:674
  123.1 4.0 collective-permute-done.9
  133.6 10.2 %collective-permute-done.10 = bf16[128,2048]{1,0:T(8,128)(2,1)S(1)} collective-permute-done((bf16[128,2048]{1,0:T(8,128)(2,1)S(1)}, bf16[128,2048]{1,0:T(8,128)(2,1)S(1)}, u32[]{:S(2)}, u32[]{:S(2)}) %collective-permute-start.10) | collective-permute-done | bytes 524320 | tf_op jit(solution)/shard_map/ppermute | solution.py:1021
  144.1 4.2 collective-permute-start.11
  149.1 9.4 %collective-permute-done.11 = bf16[128,2048]{1,0:T(8,128)(2,1)S(1)} collective-permute-done((bf16[128,2048]{1,0:T(8,128)(2,1)S(1)}, bf16[128,2048]{1,0:T(8,128)(2,1)S(1)}, u32[]{:S(2)}, u32[]{:S(2)}) %collective-permute-start.11) | collective-permute-done | bytes 524320 | tf_op jit(solution)/shard_map/ppermute | solution.py:1021
  159.6 7.9 %collective-permute-start.12 = (bf16[128,2048]{1,0:T(8,128)(2,1)}, bf16[128,2048]{1,0:T(8,128)(2,1)S(1)}, u32[]{:S(2)}, u32[]{:S(2)}) collective-permute-start(bf16[128,2048]{1,0:T(8,128)(2,1)} %get-tuple-element.287), channel_id=1, source_target_pairs={{0,1},{1,2},{2,3},{4,5},{5,6},{6,7},{8,9},{9,10},{10,11},{12,13},{... | collective-permute-start | bytes 1572872 | tf_op jit(solution)/shard_map/ppermute | solution.py:1021
  168.9 8.0 %collective-permute-done.12 = bf16[128,2048]{1,0:T(8,128)(2,1)S(1)} collective-permute-done((bf16[128,2048]{1,0:T(8,128)(2,1)}, bf16[128,2048]{1,0:T(8,128)(2,1)S(1)}, u32[]{:S(2)}, u32[]{:S(2)}) %collective-permute-start.12) | collective-permute-done | bytes 524320 | tf_op jit(solution)/shard_map/ppermute | solution.py:1021
  183.8 4.0 collective-permute-start.16
  187.8 6.7 %collective-permute-done.17 = bf16[128,2048]{1,0:T(8,128)(2,1)S(1)} collective-permute-done((bf16[128,2048]{1,0:T(8,128)(2,1)S(1)}, bf16[128,2048]{1,0:T(8,128)(2,1)S(1)}, u32[]{:S(2)}, u32[]{:S(2)}) %collective-permute-start.17) | collective-permute-done | bytes 524320 | tf_op jit(solution)/shard_map/ppermute | solution.py:1037
  196.5 9.2 %collective-permute-done.18 = bf16[128,2048]{1,0:T(8,128)(2,1)S(1)} collective-permute-done((bf16[128,2048]{1,0:T(8,128)(2,1)S(1)}, bf16[128,2048]{1,0:T(8,128)(2,1)S(1)}, u32[]{:S(2)}, u32[]{:S(2)}) %collective-permute-start.18) | collective-permute-done | bytes 524320 | tf_op jit(solution)/shard_map/ppermute | solution.py:1037
  208.0 8.0 %collective-permute-done.19 = bf16[128,2048]{1,0:T(8,128)(2,1)S(1)} collective-permute-done((bf16[128,2048]{1,0:T(8,128)(2,1)S(1)}, bf16[128,2048]{1,0:T(8,128)(2,1)S(1)}, u32[]{:S(2)}, u32[]{:S(2)}) %collective-permute-start.19) | collective-permute-done | bytes 524320 | tf_op jit(solution)/shard_map/ppermute | solution.py:1037
  216.5 6.0 %collective-permute-start.22 = (bf16[512,2048]{1,0:T(8,128)(2,1)S(1)}, bf16[512,2048]{1,0:T(8,128)(2,1)}, u32[]{:S(2)}, u32[]{:S(2)}) collective-permute-start(bf16[512,2048]{1,0:T(8,128)(2,1)S(1)} %pad_maximum_fusion.1.hidden_ref.h_own), channel_id=1, source_target_pairs={{0,4},{4,0},{1,5},{5,1},{2,6},{6,2},{3,7},{7,3},{8,12},{12,8},{9,1... | collective-permute-start | bytes 6291464 | tf_op jit(solution)/shard_map/ppermute | solution.py:968
  222.5 3.9 collective-permute-done.22.hidden_ref.h_other
  226.4 18.0 %feed_forward.3 = (bf16[3,512,704]{2,1,0:T(8,128)(2,1)}, bf16[512,2048]{1,0:T(8,128)(2,1)}, bf16[512,2048]{1,0:T(8,128)(2,1)}) custom-call(s32[4]{0:T(128)} %copy-done.38, bf16[512,2048]{1,0:T(8,128)(2,1)} %collective-permute-done.22.hidden_ref.h_other, bf16[512,2048]{1,0:T(8,128)(2,1)} %copy-done.13, bf16[4,3,512,704]{3,2,1,0:T(8,128)(2,1)} %bitcast.80), custom_call_target="tpu_custom_call" | custom-call | flops 1 | bytes 1 | tf_op jit(solution)/shard_map/feed_forward/pallas_call | solution.py:737
  244.8 18.0 %feed_forward.2 = (bf16[3,512,704]{2,1,0:T(8,128)(2,1)}, bf16[512,2048]{1,0:T(8,128)(2,1)}, bf16[512,2048]{1,0:T(8,128)(2,1)}) custom-call(s32[4]{0:T(128)} %copy-done.38, bf16[512,2048]{1,0:T(8,128)(2,1)} %copy-done.11, bf16[512,2048]{1,0:T(8,128)(2,1)} %get-tuple-element.144.branch_ref.b_own, bf16[4,3,512,704]{3,2,1,0:T(8,128)(2,1)} %bitcast.81), custom_call_target="tpu_custom_call" | custom-call | flops 1 | bytes 1 | tf_op jit(solution)/shard_map/feed_forward/pallas_call | solution.py:737
  262.8 3.8 add_convert_fusion.2
  267.1 15.4 %feed_grads.1 = bf16[2048,2176]{1,0:T(8,128)(2,1)} custom-call(bf16[512,2048]{1,0:T(8,128)(2,1)} %copy-done.11, bf16[512,2048]{1,0:T(8,128)(2,1)} %collective-permute-done.22.hidden_ref.h_other, bf16[512,2048]{1,0:T(8,128)(2,1)} %get-tuple-element.144.branch_ref.b_own, bf16[512,2048]{1,0:T(8,128)(2,1)} %copy-done.13, ...), custom_call_target="tpu_custom_call" | custom-call | flops 1 | bytes 1 | tf_op jit(solution)/shard_map/feed_grads/pallas_call | solution.py:777
  282.6 3.7 add_convert_fusion.1
  286.2 23.3 %reduce-scatter.5.cloned.1.call-done = bf16[128,2048]{1,0:T(8,128)(2,1)} async-done(((bf16[512,2048]{1,0:T(8,128)(2,1)}), bf16[128,2048]{1,0:T(8,128)(2,1)}) %reduce-scatter.5.cloned.1.call-update) | async-done | bytes 524304 | tf_op jit(solution)/shard_map/reduce_scatter | solution.py:1174
  313.6 4.0 collective-permute-start.25
  317.7 9.3 %collective-permute-done.26 = bf16[128,2048]{1,0:T(8,128)(2,1)S(1)} collective-permute-done((bf16[128,2048]{1,0:T(8,128)(2,1)S(1)}, bf16[128,2048]{1,0:T(8,128)(2,1)S(1)}, u32[]{:S(2)}, u32[]{:S(2)}) %collective-permute-start.26) | collective-permute-done | bytes 524320 | tf_op jit(solution)/shard_map/ppermute | solution.py:1037
  328.9 11.8 %collective-permute-done.27 = bf16[128,2048]{1,0:T(8,128)(2,1)S(1)} collective-permute-done((bf16[128,2048]{1,0:T(8,128)(2,1)S(1)}, bf16[128,2048]{1,0:T(8,128)(2,1)S(1)}, u32[]{:S(2)}, u32[]{:S(2)}) %collective-permute-start.27) | collective-permute-done | bytes 524320 | tf_op jit(solution)/shard_map/ppermute | solution.py:1037
  342.9 10.8 %collective-permute-done.28 = bf16[128,2048]{1,0:T(8,128)(2,1)S(1)} collective-permute-done((bf16[128,2048]{1,0:T(8,128)(2,1)S(1)}, bf16[128,2048]{1,0:T(8,128)(2,1)S(1)}, u32[]{:S(2)}, u32[]{:S(2)}) %collective-permute-start.28) | collective-permute-done | bytes 524320 | tf_op jit(solution)/shard_map/ppermute | solution.py:1037
  358.7 4.5 collective-permute-start.31
  364.9 32.1 %mixer_backward.1 = (bf16[1024,1664]{1,0:T(8,128)(2,1)}, f32[8,1024]{1,0:T(8,128)}, f32[8,128]{1,0:T(8,128)}, f32[8,256]{1,0:T(8,128)}) custom-call(s32[8]{0:T(128)} %copy-done.6, f32[1024,1152]{1,0:T(8,128)} %fusion.46.refs_0_.refs_1_, f32[1024,1152]{1,0:T(8,128)} %fusion.46.refs_0_.refs_1_, f32[1024,1024]{1,0:T(8,128)} %get-tuple-element.167.refs_2_, ...), custom_call_target="tpu_custom_call" | custom-call | flops 1 | bytes 1 | tf_op jit(solution)/shard_map/mixer_backward/pallas_call | solution.py:449
  397.1 8.5 %collective-permute-done.32 = bf16[128,2048]{1,0:T(8,128)(2,1)} collective-permute-done((bf16[128,2048]{1,0:T(8,128)(2,1)}, bf16[128,2048]{1,0:T(8,128)(2,1)}, u32[]{:S(2)}, u32[]{:S(2)}) %collective-permute-start.32) | collective-permute-done | bytes 524320 | tf_op jit(solution)/shard_map/ppermute | solution.py:998
  407.2 4.7 collective-permute-start.35
  413.5 13.6 %d_normed_rows.1 = (bf16[512,2048]{1,0:T(8,128)(2,1)}, bf16[512,2048]{1,0:T(8,128)(2,1)}, f32[8,2048]{1,0:T(8,128)}) custom-call(bf16[1024,1664]{1,0:T(8,128)(2,1)} %get-tuple-element.190.mix_ref, bf16[1024,2048]{1,0:T(8,128)(2,1)} %copy-done.7, bf16[2048,1152]{1,0:T(8,128)(2,1)} %copy-done.10, bf16[4,2,512,512]{3,2,1,0:T(8,128)(2,1)} %bitcast.84), custom_call_target="tpu_custom_call" | custom-call | flops 1 | bytes 1 | tf_op jit(solution)/shard_map/d_normed_rows/pallas_call | solution.py:819
  429.8 6.1 %out_grads.1 = bf16[2048,512]{1,0:T(8,128)(2,1)} custom-call(bf16[512,2048]{1,0:T(8,128)(2,1)} %copy-done.8, bf16[512,2048]{1,0:T(8,128)(2,1)} %copy-done.9, bf16[1024,512]{1,0:T(8,128)(2,1)} %get-tuple-element.186.heads_ref), custom_call_target="tpu_custom_call" | custom-call | flops 1 | bytes 1 | tf_op jit(solution)/shard_map/out_grads/pallas_call | solution.py:875
  442.8 9.4 %collective-permute-start.38 = (bf16[128,2048]{1,0:T(8,128)(2,1)}, bf16[128,2048]{1,0:T(8,128)(2,1)}, u32[]{:S(2)}, u32[]{:S(2)}) collective-permute-start(bf16[128,2048]{1,0:T(8,128)(2,1)} %get-tuple-element.283), channel_id=1, source_target_pairs={{0,1},{4,5},{8,9},{12,13},{16,17},{20,21},{24,25},{28,29}} | collective-permute-start | bytes 1572872 | tf_op jit(solution)/shard_map/ppermute | solution.py:1021
  453.7 12.1 %mix_grads.1 = bf16[2048,1664]{1,0:T(8,128)(2,1)} custom-call(bf16[1024,2048]{1,0:T(8,128)(2,1)} %copy-done.7, bf16[1024,1664]{1,0:T(8,128)(2,1)} %get-tuple-element.190.mix_ref), custom_call_target="tpu_custom_call" | custom-call | flops 1 | bytes 1 | tf_op jit(solution)/shard_map/mix_grads/pallas_call | solution.py:850
  480.4 6.4 %finish.3 = (f32[512,1408]{1,0:T(8,128)}, f32[512,1408]{1,0:T(8,128)}, f32[1408,512]{1,0:T(8,128)}) custom-call(s32[1]{0:T(128)} %bitcast.2.core_ref, bf16[512,2176]{1,0:T(8,128)(2,1)} %reduce-scatter.7.cloned.1.call-done.own_ref, bf16[512,2176]{1,0:T(8,128)(2,1)} %copy-done.21), custom_call_target="tpu_custom_call" | custom-call | flops 1 | bytes 1 | tf_op jit(solution)/shard_map/finish/pallas_call | solution.py:941
  486.8 5.4 collective-permute-done.47.refs_6_
  498.0 4.2 collective-permute-start.51
  502.2 4.5 place.2
  506.7 3.9 collective-permute-done.50
  526.3 4.0 finish.4
  537.3 8.6 %collective-permute-done.57.refs_5_ = bf16[128,2048]{1,0:T(8,128)(2,1)S(1)} collective-permute-done((bf16[128,2048]{1,0:T(8,128)(2,1)S(1)}, bf16[128,2048]{1,0:T(8,128)(2,1)S(1)}, u32[]{:S(2)}, u32[]{:S(2)}) %collective-permute-start.57) | collective-permute-done | bytes 524320 | tf_op jit(solution)/shard_map/ppermute | solution.py:1045
  545.9 3.7 collective-permute-start.62
  553.8 11.9 %collective-permute-done.60.refs_6_ = bf16[128,2048]{1,0:T(8,128)(2,1)S(1)} collective-permute-done((bf16[128,2048]{1,0:T(8,128)(2,1)S(1)}, bf16[128,2048]{1,0:T(8,128)(2,1)S(1)}, u32[]{:S(2)}, u32[]{:S(2)}) %collective-permute-start.60) | collective-permute-done | bytes 524320 | tf_op jit(solution)/shard_map/ppermute | solution.py:1045
  566.5 4.2 place.3
  576.7 5.0 finish.5
  (313 shorter events, 144.6 us)
Async XLA Ops:
  7.2 102.5 %all-gather.3.cloned.1.call-start = ((), (), s32[]{:S(2)}) async-start(), calls=%async_computation.4 | async-start | bytes 5242880 | tf_op jit(solution)/shard_map/all_gather | solution.py:1153
  14.3 12.2 %collective-permute-start.2 = (bf16[2112]{0:T(1024)(128)(2,1)S(1)}, bf16[2112]{0:T(1024)(128)(2,1)S(1)}, u32[]{:S(2)}, u32[]{:S(2)}) collective-permute-start(bf16[2112]{0:T(1024)(128)(2,1)S(1)} %concatenate.37), channel_id=1, source_target_pairs={{0,8},{8,0},{16,24},{24,16},{1,9},{9,1},{17,25},{25,17},{2,10},{10... | collective-permute-start | bytes 12680 | tf_op jit(solution)/shard_map/ppermute | solution.py:964
  17.6 26.6 %collective-permute-start = (bf16[512,1152]{1,0:T(8,128)(2,1)}, bf16[512,1152]{1,0:T(8,128)(2,1)S(1)}, u32[]{:S(2)}, u32[]{:S(2)}) collective-permute-start(bf16[512,1152]{1,0:T(8,128)(2,1)} %pack_mix.1), channel_id=1, source_target_pairs={{0,8},{8,0},{16,24},{24,16},{1,9},{9,1},{17,25},{25,17},{2,10},{10... | collective-permute-start | bytes 3538952 | tf_op jit(solution)/shard_map/ppermute | solution.py:964
  19.0 26.0 %collective-permute-start.1 = (bf16[512,1152]{1,0:T(8,128)(2,1)}, bf16[512,1152]{1,0:T(8,128)(2,1)S(1)}, u32[]{:S(2)}, u32[]{:S(2)}) collective-permute-start(bf16[512,1152]{1,0:T(8,128)(2,1)} %pack_mix.1), channel_id=1, source_target_pairs={{0,16},{8,24},{16,0},{24,8},{1,17},{9,25},{17,1},{25,9},{2,18},{10... | collective-permute-start | bytes 3538952 | tf_op jit(solution)/shard_map/ppermute | solution.py:964
  45.0 181.3 %all-gather.5.cloned.1.call-start = ((), (), s32[]{:S(2)}) async-start(), calls=%async_computation.5 | async-start | bytes 11796480 | tf_op jit(solution)/shard_map/all_gather | solution.py:1157
  47.8 26.4 %collective-permute-start.8 = (bf16[512,2048]{1,0:T(8,128)(2,1)}, bf16[512,2048]{1,0:T(8,128)(2,1)S(1)}, u32[]{:S(2)}, u32[]{:S(2)}) collective-permute-start(bf16[512,2048]{1,0:T(8,128)(2,1)} %get-tuple-element.144.branch_ref.b_own), channel_id=1, source_target_pairs={{0,4},{4,0},{1,5},{5,1},{2,6},{6,2},{3,7},{7,3},{8,12},{12,8},{9,1... | collective-permute-start | bytes 6291464 | tf_op jit(solution)/shard_map/ppermute | solution.py:968
  50.2 21.6 %collective-permute-start.5 = (bf16[256,1152]{1,0:T(8,128)(2,1)S(1)}, bf16[256,1152]{1,0:T(8,128)(2,1)S(1)}, u32[]{:S(2)}, u32[]{:S(2)}) collective-permute-start(bf16[256,1152]{1,0:T(8,128)(2,1)S(1)} %slice.151), channel_id=1, source_target_pairs={{0,16},{8,24},{16,0},{24,8},{1,17},{9,25},{17,1},{25,9},{2,18},{10... | collective-permute-start | bytes 1769480 | tf_op jit(solution)/shard_map/ppermute | solution.py:964
  51.6 22.7 %collective-permute-start.6 = (bf16[256,1152]{1,0:T(8,128)(2,1)S(1)}, bf16[256,1152]{1,0:T(8,128)(2,1)S(1)}, u32[]{:S(2)}, u32[]{:S(2)}) collective-permute-start(bf16[256,1152]{1,0:T(8,128)(2,1)S(1)} %slice.152), channel_id=1, source_target_pairs={{0,8},{8,0},{16,24},{24,16},{1,9},{9,1},{17,25},{25,17},{2,10},{10... | collective-permute-start | bytes 1769480 | tf_op jit(solution)/shard_map/ppermute | solution.py:964
  83.8 225.7 %reduce-scatter.5.cloned.1.call-start = ((), (), s32[]{:S(2)}) async-start(), calls=%async_computation.6 | async-start | bytes 2621440 | tf_op jit(solution)/shard_map/reduce_scatter | solution.py:1174
  129.6 14.2 %collective-permute-start.10 = (bf16[128,2048]{1,0:T(8,128)(2,1)S(1)}, bf16[128,2048]{1,0:T(8,128)(2,1)S(1)}, u32[]{:S(2)}, u32[]{:S(2)}) collective-permute-start(bf16[128,2048]{1,0:T(8,128)(2,1)S(1)} %get-tuple-element.291), channel_id=1, source_target_pairs={{0,1},{4,5},{8,9},{12,13},{16,17},{20,21},{24,25},{28,29}} | collective-permute-start | bytes 1572872 | tf_op jit(solution)/shard_map/ppermute | solution.py:1021
  144.1 14.3 %collective-permute-start.11 = (bf16[128,2048]{1,0:T(8,128)(2,1)S(1)}, bf16[128,2048]{1,0:T(8,128)(2,1)S(1)}, u32[]{:S(2)}, u32[]{:S(2)}) collective-permute-start(bf16[128,2048]{1,0:T(8,128)(2,1)S(1)} %get-tuple-element.289), channel_id=1, source_target_pairs={{0,1},{1,2},{4,5},{5,6},{8,9},{9,10},{12,13},{13,14},{16,17},{17,1... | collective-permute-start | bytes 1572872 | tf_op jit(solution)/shard_map/ppermute | solution.py:1021
  159.6 17.2 %collective-permute-start.12 = (bf16[128,2048]{1,0:T(8,128)(2,1)}, bf16[128,2048]{1,0:T(8,128)(2,1)S(1)}, u32[]{:S(2)}, u32[]{:S(2)}) collective-permute-start(bf16[128,2048]{1,0:T(8,128)(2,1)} %get-tuple-element.287), channel_id=1, source_target_pairs={{0,1},{1,2},{2,3},{4,5},{5,6},{6,7},{8,9},{9,10},{10,11},{12,13},{... | collective-permute-start | bytes 1572872 | tf_op jit(solution)/shard_map/ppermute | solution.py:1021
  167.6 12.9 %collective-permute-start.15 = (bf16[128,2048]{1,0:T(8,128)(2,1)S(1)}, bf16[128,2048]{1,0:T(8,128)(2,1)}, u32[]{:S(2)}, u32[]{:S(2)}) collective-permute-start(bf16[128,2048]{1,0:T(8,128)(2,1)S(1)} %get-tuple-element.288), channel_id=1, source_target_pairs={{1,0},{2,1},{3,2},{5,4},{6,5},{7,6},{9,8},{10,9},{11,10},{13,12},{... | collective-permute-start | bytes 1572872 | tf_op jit(solution)/shard_map/ppermute | solution.py:1022
  182.5 12.0 %collective-permute-start.17 = (bf16[128,2048]{1,0:T(8,128)(2,1)S(1)}, bf16[128,2048]{1,0:T(8,128)(2,1)S(1)}, u32[]{:S(2)}, u32[]{:S(2)}) collective-permute-start(bf16[128,2048]{1,0:T(8,128)(2,1)S(1)} %multiply_convert_fusion.1), channel_id=1, source_target_pairs={{1,0},{2,1},{3,2},{5,4},{6,5},{7,6},{9,8},{10,9},{11,10},{13,12},{... | collective-permute-start | bytes 1572872 | tf_op jit(solution)/shard_map/ppermute | solution.py:1037
  183.8 12.0 %collective-permute-start.16 = (bf16[128,2048]{1,0:T(8,128)(2,1)S(1)}, bf16[128,2048]{1,0:T(8,128)(2,1)S(1)}, u32[]{:S(2)}, u32[]{:S(2)}) collective-permute-start(bf16[128,2048]{1,0:T(8,128)(2,1)S(1)} %multiply_convert_fusion.1), channel_id=1, source_target_pairs={{0,1},{1,2},{2,3},{4,5},{5,6},{6,7},{8,9},{9,10},{10,11},{12,13},{... | collective-permute-start | bytes 1572872 | tf_op jit(solution)/shard_map/ppermute | solution.py:1035
  194.5 11.2 %collective-permute-start.18 = (bf16[128,2048]{1,0:T(8,128)(2,1)S(1)}, bf16[128,2048]{1,0:T(8,128)(2,1)S(1)}, u32[]{:S(2)}, u32[]{:S(2)}) collective-permute-start(bf16[128,2048]{1,0:T(8,128)(2,1)S(1)} %collective-permute-done.17), channel_id=1, source_target_pairs={{1,0},{2,1},{5,4},{6,5},{9,8},{10,9},{13,12},{14,13},{17,16},{18,1... | collective-permute-start | bytes 1572872 | tf_op jit(solution)/shard_map/ppermute | solution.py:1037
  244.4 18.4 %collective-permute-start.23 = (bf16[512,2048]{1,0:T(8,128)(2,1)}, bf16[512,2048]{1,0:T(8,128)(2,1)S(1)}, u32[]{:S(2)}, u32[]{:S(2)}) collective-permute-start(bf16[512,2048]{1,0:T(8,128)(2,1)} %get-tuple-element.156), channel_id=1, source_target_pairs={{0,4},{4,0},{1,5},{5,1},{2,6},{6,2},{3,7},{7,3},{8,12},{12,8},{9,1... | collective-permute-start | bytes 6291464 | tf_op jit(solution)/shard_map/ppermute | solution.py:968
  266.7 140.5 %reduce-scatter.7.cloned.1.call-start = ((), (), s32[]{:S(2)}) async-start(), calls=%async_computation.7 | async-start | bytes 11141120 | tf_op jit(solution)/shard_map/reduce_scatter | solution.py:991
  266.9 15.6 %collective-permute-start.24 = (bf16[512,2048]{1,0:T(8,128)(2,1)}, bf16[512,2048]{1,0:T(8,128)(2,1)}, u32[]{:S(2)}, u32[]{:S(2)}) collective-permute-start(bf16[512,2048]{1,0:T(8,128)(2,1)} %get-tuple-element.163), channel_id=1, source_target_pairs={{0,4},{4,0},{1,5},{5,1},{2,6},{6,2},{3,7},{7,3},{8,12},{12,8},{9,1... | collective-permute-start | bytes 6291464 | tf_op jit(solution)/shard_map/ppermute | solution.py:968
  309.6 210.7 %reduce-scatter.11.cloned.1.call-start = ((), (), s32[]{:S(2)}) async-start(), calls=%async_computation.9 | async-start | bytes 2621440 | tf_op jit(solution)/shard_map/reduce_scatter | solution.py:991
  312.3 14.6 %collective-permute-start.26 = (bf16[128,2048]{1,0:T(8,128)(2,1)S(1)}, bf16[128,2048]{1,0:T(8,128)(2,1)S(1)}, u32[]{:S(2)}, u32[]{:S(2)}) collective-permute-start(bf16[128,2048]{1,0:T(8,128)(2,1)S(1)} %multiply_convert_fusion), channel_id=1, source_target_pairs={{1,0},{2,1},{3,2},{5,4},{6,5},{7,6},{9,8},{10,9},{11,10},{13,12},{... | collective-permute-start | bytes 1572872 | tf_op jit(solution)/shard_map/ppermute | solution.py:1037
  313.6 14.6 %collective-permute-start.25 = (bf16[128,2048]{1,0:T(8,128)(2,1)S(1)}, bf16[128,2048]{1,0:T(8,128)(2,1)S(1)}, u32[]{:S(2)}, u32[]{:S(2)}) collective-permute-start(bf16[128,2048]{1,0:T(8,128)(2,1)S(1)} %multiply_convert_fusion), channel_id=1, source_target_pairs={{0,1},{1,2},{2,3},{4,5},{5,6},{6,7},{8,9},{9,10},{10,11},{12,13},{... | collective-permute-start | bytes 1572872 | tf_op jit(solution)/shard_map/ppermute | solution.py:1035
  326.9 13.8 %collective-permute-start.27 = (bf16[128,2048]{1,0:T(8,128)(2,1)S(1)}, bf16[128,2048]{1,0:T(8,128)(2,1)S(1)}, u32[]{:S(2)}, u32[]{:S(2)}) collective-permute-start(bf16[128,2048]{1,0:T(8,128)(2,1)S(1)} %collective-permute-done.26), channel_id=1, source_target_pairs={{1,0},{2,1},{5,4},{6,5},{9,8},{10,9},{13,12},{14,13},{17,16},{18,1... | collective-permute-start | bytes 1572872 | tf_op jit(solution)/shard_map/ppermute | solution.py:1037
  328.2 13.8 %collective-permute-start.29 = (bf16[128,2048]{1,0:T(8,128)(2,1)S(1)}, bf16[128,2048]{1,0:T(8,128)(2,1)S(1)}, u32[]{:S(2)}, u32[]{:S(2)}) collective-permute-start(bf16[128,2048]{1,0:T(8,128)(2,1)S(1)} %collective-permute-done.25), channel_id=1, source_target_pairs={{1,2},{2,3},{5,6},{6,7},{9,10},{10,11},{13,14},{14,15},{17,18},{18... | collective-permute-start | bytes 1572872 | tf_op jit(solution)/shard_map/ppermute | solution.py:1035
  340.7 13.0 %collective-permute-start.28 = (bf16[128,2048]{1,0:T(8,128)(2,1)S(1)}, bf16[128,2048]{1,0:T(8,128)(2,1)S(1)}, u32[]{:S(2)}, u32[]{:S(2)}) collective-permute-start(bf16[128,2048]{1,0:T(8,128)(2,1)S(1)} %collective-permute-done.27), channel_id=1, source_target_pairs={{1,0},{5,4},{9,8},{13,12},{17,16},{21,20},{25,24},{29,28}} | collective-permute-start | bytes 1572872 | tf_op jit(solution)/shard_map/ppermute | solution.py:1037
  342.0 11.8 %collective-permute-start.30 = (bf16[128,2048]{1,0:T(8,128)(2,1)S(1)}, bf16[128,2048]{1,0:T(8,128)(2,1)S(1)}, u32[]{:S(2)}, u32[]{:S(2)}) collective-permute-start(bf16[128,2048]{1,0:T(8,128)(2,1)S(1)} %collective-permute-done.29), channel_id=1, source_target_pairs={{2,3},{6,7},{10,11},{14,15},{18,19},{22,23},{26,27},{30,31}} | collective-permute-start | bytes 1572872 | tf_op jit(solution)/shard_map/ppermute | solution.py:1035
  358.7 38.3 %collective-permute-start.31 = (bf16[128,2048]{1,0:T(8,128)(2,1)}, bf16[128,2048]{1,0:T(8,128)(2,1)S(1)}, u32[]{:S(2)}, u32[]{:S(2)}) collective-permute-start(bf16[128,2048]{1,0:T(8,128)(2,1)} %get-tuple-element.286), channel_id=1, source_target_pairs={{0,3},{1,0},{2,1},{3,2},{4,7},{5,4},{6,5},{7,6},{8,11},{9,8},{10,9... | collective-permute-start | bytes 1572872 | tf_op jit(solution)/shard_map/ppermute | solution.py:998
  363.3 42.2 %collective-permute-start.32 = (bf16[128,2048]{1,0:T(8,128)(2,1)}, bf16[128,2048]{1,0:T(8,128)(2,1)}, u32[]{:S(2)}, u32[]{:S(2)}) collective-permute-start(bf16[128,2048]{1,0:T(8,128)(2,1)} %get-tuple-element.285), channel_id=1, source_target_pairs={{0,2},{1,3},{2,0},{3,1},{4,6},{5,7},{6,4},{7,5},{8,10},{9,11},{10,... | collective-permute-start | bytes 1572872 | tf_op jit(solution)/shard_map/ppermute | solution.py:998
  363.3 42.2 %collective-permute-start.33 = (bf16[128,2048]{1,0:T(8,128)(2,1)}, bf16[128,2048]{1,0:T(8,128)(2,1)}, u32[]{:S(2)}, u32[]{:S(2)}) collective-permute-start(bf16[128,2048]{1,0:T(8,128)(2,1)} %get-tuple-element.284), channel_id=1, source_target_pairs={{0,1},{1,2},{2,3},{3,0},{4,5},{5,6},{6,7},{7,4},{8,9},{9,10},{10,1... | collective-permute-start | bytes 1572872 | tf_op jit(solution)/shard_map/ppermute | solution.py:998
  407.2 19.9 %collective-permute-start.35 = (bf16[128,2048]{1,0:T(8,128)(2,1)S(1)}, bf16[128,2048]{1,0:T(8,128)(2,1)S(1)}, u32[]{:S(2)}, u32[]{:S(2)}) collective-permute-start(bf16[128,2048]{1,0:T(8,128)(2,1)S(1)} %add_convert_fusion.6.refs_0_), channel_id=1, source_target_pairs={{0,1},{1,2},{2,3},{4,5},{5,6},{6,7},{8,9},{9,10},{10,11},{12,13},{... | collective-permute-start | bytes 1572872 | tf_op jit(solution)/shard_map/ppermute | solution.py:1044
  411.9 15.2 %collective-permute-start.36 = (bf16[128,2048]{1,0:T(8,128)(2,1)S(1)}, bf16[128,2048]{1,0:T(8,128)(2,1)S(1)}, u32[]{:S(2)}, u32[]{:S(2)}) collective-permute-start(bf16[128,2048]{1,0:T(8,128)(2,1)S(1)} %add_convert_fusion.6.refs_0_), channel_id=1, source_target_pairs={{1,0},{2,1},{3,2},{5,4},{6,5},{7,6},{9,8},{10,9},{11,10},{13,12},{... | collective-permute-start | bytes 1572872 | tf_op jit(solution)/shard_map/ppermute | solution.py:1045
  435.9 134.8 %reduce-scatter.9.cloned.1.call-start = ((), (), s32[]{:S(2)}) async-start(), calls=%async_computation.8 | async-start | bytes 8519680 | tf_op jit(solution)/shard_map/reduce_scatter | solution.py:991
  435.9 29.8 %collective-permute-start.40 = (bf16[128,2048]{1,0:T(8,128)(2,1)}, bf16[128,2048]{1,0:T(8,128)(2,1)}, u32[]{:S(2)}, u32[]{:S(2)}) collective-permute-start(bf16[128,2048]{1,0:T(8,128)(2,1)} %copy-done.26), channel_id=1, source_target_pairs={{1,2},{2,3},{5,6},{6,7},{9,10},{10,11},{13,14},{14,15},{17,18},{18... | collective-permute-start | bytes 1572872 | tf_op jit(solution)/shard_map/ppermute | solution.py:1044
  437.4 28.3 %collective-permute-start.41 = (bf16[128,2048]{1,0:T(8,128)(2,1)}, bf16[128,2048]{1,0:T(8,128)(2,1)}, u32[]{:S(2)}, u32[]{:S(2)}) collective-permute-start(bf16[128,2048]{1,0:T(8,128)(2,1)} %copy-done.27), channel_id=1, source_target_pairs={{1,0},{2,1},{5,4},{6,5},{9,8},{10,9},{13,12},{14,13},{17,16},{18,1... | collective-permute-start | bytes 1572872 | tf_op jit(solution)/shard_map/ppermute | solution.py:1045
  442.8 23.0 %collective-permute-start.38 = (bf16[128,2048]{1,0:T(8,128)(2,1)}, bf16[128,2048]{1,0:T(8,128)(2,1)}, u32[]{:S(2)}, u32[]{:S(2)}) collective-permute-start(bf16[128,2048]{1,0:T(8,128)(2,1)} %get-tuple-element.283), channel_id=1, source_target_pairs={{0,1},{4,5},{8,9},{12,13},{16,17},{20,21},{24,25},{28,29}} | collective-permute-start | bytes 1572872 | tf_op jit(solution)/shard_map/ppermute | solution.py:1021
  452.2 13.6 %collective-permute-start.39 = (bf16[128,2048]{1,0:T(8,128)(2,1)}, bf16[128,2048]{1,0:T(8,128)(2,1)}, u32[]{:S(2)}, u32[]{:S(2)}) collective-permute-start(bf16[128,2048]{1,0:T(8,128)(2,1)} %get-tuple-element.282), channel_id=1, source_target_pairs={{3,2},{7,6},{11,10},{15,14},{19,18},{23,22},{27,26},{31,30}} | collective-permute-start | bytes 1572872 | tf_op jit(solution)/shard_map/ppermute | solution.py:1022
  465.8 12.1 %collective-permute-start.45 = (bf16[512,2176]{1,0:T(8,128)(2,1)}, bf16[512,2176]{1,0:T(8,128)(2,1)S(1)}, u32[]{:S(2)}, u32[]{:S(2)}) collective-permute-start(bf16[512,2176]{1,0:T(8,128)(2,1)} %reduce-scatter.7.cloned.1.call-done.own_ref), channel_id=1, source_target_pairs={{0,4},{4,0},{1,5},{5,1},{2,6},{6,2},{3,7},{7,3},{8,12},{12,8},{9,1... | collective-permute-start | bytes 6684680 | tf_op jit(solution)/shard_map/ppermute | solution.py:968
  472.0 14.8 %collective-permute-start.43 = (bf16[128,2048]{1,0:T(8,128)(2,1)S(1)}, bf16[128,2048]{1,0:T(8,128)(2,1)}, u32[]{:S(2)}, u32[]{:S(2)}) collective-permute-start(bf16[128,2048]{1,0:T(8,128)(2,1)S(1)} %get-tuple-element.281), channel_id=1, source_target_pairs={{0,1},{1,2},{4,5},{5,6},{8,9},{9,10},{12,13},{13,14},{16,17},{17,1... | collective-permute-start | bytes 1572872 | tf_op jit(solution)/shard_map/ppermute | solution.py:1021
  474.4 12.4 %collective-permute-start.44 = (bf16[128,2048]{1,0:T(8,128)(2,1)S(1)}, bf16[128,2048]{1,0:T(8,128)(2,1)}, u32[]{:S(2)}, u32[]{:S(2)}) collective-permute-start(bf16[128,2048]{1,0:T(8,128)(2,1)S(1)} %get-tuple-element.280), channel_id=1, source_target_pairs={{2,1},{3,2},{6,5},{7,6},{10,9},{11,10},{14,13},{15,14},{18,17},{19... | collective-permute-start | bytes 1572872 | tf_op jit(solution)/shard_map/ppermute | solution.py:1022
  476.5 15.7 %collective-permute-start.47 = (bf16[128,2048]{1,0:T(8,128)(2,1)}, bf16[128,2048]{1,0:T(8,128)(2,1)S(1)}, u32[]{:S(2)}, u32[]{:S(2)}) collective-permute-start(bf16[128,2048]{1,0:T(8,128)(2,1)} %collective-permute-done.41.refs_5_), channel_id=1, source_target_pairs={{1,0},{5,4},{9,8},{13,12},{17,16},{21,20},{25,24},{29,28}} | collective-permute-start | bytes 1572872 | tf_op jit(solution)/shard_map/ppermute | solution.py:1045
  477.9 14.8 %collective-permute-start.48 = (f32[4352]{0:T(1024)S(1)}, f32[4352]{0:T(1024)S(1)}, u32[]{:S(2)}, u32[]{:S(2)}) collective-permute-start(f32[4352]{0:T(1024)S(1)} %add.274), channel_id=1, source_target_pairs={{0,1},{1,0},{2,3},{3,2},{4,5},{5,4},{6,7},{7,6},{8,9},{9,8},{10,11... | collective-permute-start | bytes 52232 | tf_op jit(solution)/shard_map/ppermute | solution.py:1225
  495.2 11.5 %collective-permute-start.49 = (bf16[128,2048]{1,0:T(8,128)(2,1)}, bf16[128,2048]{1,0:T(8,128)(2,1)S(1)}, u32[]{:S(2)}, u32[]{:S(2)}) collective-permute-start(bf16[128,2048]{1,0:T(8,128)(2,1)} %get-tuple-element.279), channel_id=1, source_target_pairs={{0,1},{1,2},{2,3},{4,5},{5,6},{6,7},{8,9},{9,10},{10,11},{12,13},{... | collective-permute-start | bytes 1572872 | tf_op jit(solution)/shard_map/ppermute | solution.py:1021
  496.7 13.9 %collective-permute-start.50 = (bf16[128,2048]{1,0:T(8,128)(2,1)}, bf16[128,2048]{1,0:T(8,128)(2,1)S(1)}, u32[]{:S(2)}, u32[]{:S(2)}) collective-permute-start(bf16[128,2048]{1,0:T(8,128)(2,1)} %get-tuple-element.278), channel_id=1, source_target_pairs={{1,0},{2,1},{3,2},{5,4},{6,5},{7,6},{9,8},{10,9},{11,10},{13,12},{... | collective-permute-start | bytes 1572872 | tf_op jit(solution)/shard_map/ppermute | solution.py:1022
  498.0 14.8 %collective-permute-start.51 = (f32[4352]{0:T(1024)S(1)}, f32[4352]{0:T(1024)S(1)}, u32[]{:S(2)}, u32[]{:S(2)}) collective-permute-start(f32[4352]{0:T(1024)S(1)} %add.278), channel_id=1, source_target_pairs={{0,2},{1,3},{2,0},{3,1},{4,6},{5,7},{6,4},{7,5},{8,10},{9,11},{10,... | collective-permute-start | bytes 52232 | tf_op jit(solution)/shard_map/ppermute | solution.py:1225
  515.8 14.5 %collective-permute-start.52 = (bf16[128,2048]{1,0:T(8,128)(2,1)}, bf16[128,2048]{1,0:T(8,128)(2,1)S(1)}, u32[]{:S(2)}, u32[]{:S(2)}) collective-permute-start(bf16[128,2048]{1,0:T(8,128)(2,1)} %fusion.15.refs_0_), channel_id=1, source_target_pairs={{0,1},{1,2},{2,3},{4,5},{5,6},{6,7},{8,9},{9,10},{10,11},{12,13},{... | collective-permute-start | bytes 1572872 | tf_op jit(solution)/shard_map/ppermute | solution.py:1044
  518.9 12.3 %collective-permute-start.53 = (bf16[128,2048]{1,0:T(8,128)(2,1)}, bf16[128,2048]{1,0:T(8,128)(2,1)S(1)}, u32[]{:S(2)}, u32[]{:S(2)}) collective-permute-start(bf16[128,2048]{1,0:T(8,128)(2,1)} %fusion.15.refs_0_), channel_id=1, source_target_pairs={{1,0},{2,1},{3,2},{5,4},{6,5},{7,6},{9,8},{10,9},{11,10},{13,12},{... | collective-permute-start | bytes 1572872 | tf_op jit(solution)/shard_map/ppermute | solution.py:1045
  531.9 13.9 %collective-permute-start.57 = (bf16[128,2048]{1,0:T(8,128)(2,1)S(1)}, bf16[128,2048]{1,0:T(8,128)(2,1)S(1)}, u32[]{:S(2)}, u32[]{:S(2)}) collective-permute-start(bf16[128,2048]{1,0:T(8,128)(2,1)S(1)} %collective-permute-done.53.refs_4_), channel_id=1, source_target_pairs={{1,0},{2,1},{5,4},{6,5},{9,8},{10,9},{13,12},{14,13},{17,16},{18,1... | collective-permute-start | bytes 1572872 | tf_op jit(solution)/shard_map/ppermute | solution.py:1045
  550.3 15.4 %collective-permute-start.60 = (bf16[128,2048]{1,0:T(8,128)(2,1)S(1)}, bf16[128,2048]{1,0:T(8,128)(2,1)S(1)}, u32[]{:S(2)}, u32[]{:S(2)}) collective-permute-start(bf16[128,2048]{1,0:T(8,128)(2,1)S(1)} %collective-permute-done.57.refs_5_), channel_id=1, source_target_pairs={{1,0},{5,4},{9,8},{13,12},{17,16},{21,20},{25,24},{29,28}} | collective-permute-start | bytes 1572872 | tf_op jit(solution)/shard_map/ppermute | solution.py:1045
  (63 other events, 550.3 us)
Sparse Core Ops, SparseCore 0:
  45.2 63.2 all-gather.2
  110.9 96.3 all-gather.4
  266.8 42.7 reduce-scatter.4
  312.9 90.1 reduce-scatter.6
  436.0 36.7 reduce-scatter.10
  475.6 75.1 reduce-scatter.8

commit v3 on v2

--- a/solution.py
+++ b/solution.py
@@ -67,6 +67,7 @@
 
 
 PER = 2
+FORWARD_PER = 4
 
 
 def inverses_of(systems, rows, cols):
@@ -101,7 +102,7 @@
 
 
 def forward_kernel(heads, key_dim, val_dim, order_ref, *refs):
-    pre_refs, refs = refs[:PER], refs[PER:]
+    pre_refs, refs = refs[:FORWARD_PER], refs[FORWARD_PER:]
     (
         taps_ref, params_ref, mixed_ref, states_ref, inverse_ref, new_ref, active_ref, sigma_ref,
         state, window,
@@ -109,14 +110,14 @@
     step = pl.program_id(0)
     wide = heads * key_dim
     width = window.shape[1]
-    span = PER * CHUNK
+    span = FORWARD_PER * CHUNK
 
     @pl.when(step == 0)
     def _():
         state[...] = jnp.zeros_like(state)
         window[0:8, :] = jnp.zeros((8, width), F32)
 
-    for c in range(PER):
+    for c in range(FORWARD_PER):
         window[8 + c * CHUNK : 8 + (c + 1) * CHUNK, :] = (
             pre_refs[c][:, :width].astype(BF16).astype(F32)
         )
@@ -130,8 +131,8 @@
     causal = rows >= cols
     strict = rows > cols
     triangle = causal.astype(F32)
-    rates = [rates_of(pre_refs[c][:, width:], params_ref, heads, triangle) for c in range(PER)]
-    chains = [(c, h) for c in range(PER) for h in range(heads)]
+    rates = [rates_of(pre_refs[c][:, width:], params_ref, heads, triangle) for c in range(FORWARD_PER)]
+    chains = [(c, h) for c in range(FORWARD_PER) for h in range(heads)]
 
     def piece(at, c, h, size):
         return active[c * CHUNK : (c + 1) * CHUNK, at + h * size : at + (h + 1) * size]
@@ -164,8 +165,8 @@
     ]
     for i, (c, h) in enumerate(chains):
         inverse_ref[(c * heads + h) * CHUNK : (c * heads + h + 1) * CHUNK, :] = inverse[i]
-    for c in range(PER):
-        place = pl.multiple_of(order_ref[step * PER + c] * CHUNK, CHUNK)
+    for c in range(FORWARD_PER):
+        place = pl.multiple_of(order_ref[step * FORWARD_PER + c] * CHUNK, CHUNK)
         for h in range(heads):
             i = c * heads + h
             begin = state[h * key_dim : (h + 1) * key_dim, :]
@@ -393,27 +394,27 @@
 def mixer_forward(order, pre, taps, params, heads, key_dim, val_dim):
     chunks = pre.shape[0] // CHUNK
     width = taps.shape[1]
-    here = lambda c: lambda n, order: (order[n * PER + c], 0)
+    here = lambda c: lambda n, order: (order[n * FORWARD_PER + c], 0)
     plain = lambda n, order: (n, 0)
     fixed = lambda n, order: (0, 0)
     return pl.pallas_call(
         functools.partial(forward_kernel, heads, key_dim, val_dim),
         grid_spec=pltpu.PrefetchScalarGridSpec(
             num_scalar_prefetch=1,
-            grid=(chunks // PER,),
-            in_specs=[pl.BlockSpec((CHUNK, pre.shape[1]), here(c)) for c in range(PER)]
+            grid=(chunks // FORWARD_PER,),
+            in_specs=[pl.BlockSpec((CHUNK, pre.shape[1]), here(c)) for c in range(FORWARD_PER)]
             + [pl.BlockSpec(taps.shape, fixed), pl.BlockSpec(params.shape, fixed)],
             out_specs=[
                 pl.BlockSpec((pre.shape[0], heads * val_dim), fixed),
-                pl.BlockSpec((PER * heads * key_dim, val_dim), plain),
-                pl.BlockSpec((PER * heads * CHUNK, CHUNK), plain),
-                pl.BlockSpec((PER * CHUNK, heads * val_dim), plain),
-                pl.BlockSpec((PER * CHUNK, width), plain),
-                pl.BlockSpec((PER * CHUNK, width), plain),
+                pl.BlockSpec((FORWARD_PER * heads * key_dim, val_dim), plain),
+                pl.BlockSpec((FORWARD_PER * heads * CHUNK, CHUNK), plain),
+                pl.BlockSpec((FORWARD_PER * CHUNK, heads * val_dim), plain),
+                pl.BlockSpec((FORWARD_PER * CHUNK, width), plain),
+                pl.BlockSpec((FORWARD_PER * CHUNK, width), plain),
             ],
             scratch_shapes=[
                 pltpu.VMEM((heads * key_dim, val_dim), F32),
-                pltpu.VMEM((PER * CHUNK + 8, width), F32),
+                pltpu.VMEM((FORWARD_PER * CHUNK + 8, width), F32),
             ],
         ),
         out_shape=[
@@ -424,10 +425,10 @@
             jax.ShapeDtypeStruct((pre.shape[0], width), F32),
             jax.ShapeDtypeStruct((pre.shape[0], width), F32),
         ],
-        compiler_params=pltpu.CompilerParams(vmem_limit_bytes=48 * 2**20),
+        compiler_params=pltpu.CompilerParams(vmem_limit_bytes=62 * 2**20),
         cost_estimate=small_cost(),
         name="mixer_forward",
-    )(order, *[pre] * PER, taps, params)
+    )(order, *[pre] * FORWARD_PER, taps, params)
 
 
 def mixer_backward(

time: 596 us -> 594 us (level)
    unnamed x89 -> x75, local copies, waits for them, and re-layouts: 14.7 us -> 10.6 us
  transfers between devices with their start and end apart: 69 -> 69, of which waited for: 27 -> 28; matrix products, arithmetic and copies ran while one was open for 8% -> 9% of each run, Pallas kernels for 27% -> 27%
where the time goes in v3:
time: 594 us; the launch traced here: 587 us
  waiting for transfers between devices  199 us (34%)
  Pallas kernels  182 us (31%)
  starting transfers between devices  120 us (20%)
  other arithmetic  36 us (6%)
  local copies, waits for them, and re-layouts  26.2 us (4%)
  between operations  16.3 us (3%)
  matrix products  7.12 us (1%)
    ppermute x6, waiting for transfers between devices, line_gather(): lax.ppermute(lefts[-1], axis, [(i, i - 1) for i in range(1, size - step +...  55.8 us
    pallas_call x2, Pallas kernels, feed_forward(): pl.pallas_call(feed_kernel, grid_spec=pltpu.PrefetchScalarGridSpec(num_sc...  36 us
    pallas_call x1, Pallas kernels, mixer_backward(): pl.pallas_call(functools.partial(backward_kernel, heads, key_dim, val_dim...  32.2 us
    ppermute x7, waiting for transfers between devices, across(): return lax.ppermute(value, 'fsdp', [(i, i ^ flip) for i in range(4)])  30.8 us
    ppermute x6, starting transfers between devices, line_sum_hops(): lax.ppermute(send_r.astype(BF16), axis, [(i, i + 1) for i in range(step)])  28.4 us
    ppermute x6, waiting for transfers between devices, line_sum_hops(): lax.ppermute(send_r.astype(BF16), axis, [(i, i + 1) for i in range(step)])  27.5 us
    ppermute x6, waiting for transfers between devices, line_hop(): lax.ppermute(left, axis, [(i, i - 1) for i in range(1, size - step + 1)])  26.8 us
    reduce_scatter x1, waiting for transfers between devices, on_device(): lax.psum_scatter(d_hidden_core, 'tensor', scatter_dimension=0, tiled=True)  24.5 us
  transfers between devices with their start and end apart: 69, of which 28 were waited for; matrix products, arithmetic and copies ran while one was open for 9% of the time, Pallas kernels for 27%

profile of v3, /device:TPU:1, one launch (start us, length us, event | category | flops | bytes accessed | tf_op | source)
XLA Modules:
  0.0 586.6 jit_solution(2908392517516191919)
XLA Ops:
  21.5 5.0 pack_rest.1
  27.4 5.6 arrange.1
  33.0 11.1 %collective-permute-done = bf16[512,1152]{1,0:T(8,128)(2,1)S(1)} collective-permute-done((bf16[512,1152]{1,0:T(8,128)(2,1)}, bf16[512,1152]{1,0:T(8,128)(2,1)S(1)}, u32[]{:S(2)}, u32[]{:S(2)}) %collective-permute-start) | collective-permute-done | bytes 1179680 | tf_op jit(solution)/shard_map/ppermute | solution.py:965
  55.5 16.3 %collective-permute-done.5 = bf16[256,1152]{1,0:T(8,128)(2,1)S(1)} collective-permute-done((bf16[256,1152]{1,0:T(8,128)(2,1)S(1)}, bf16[256,1152]{1,0:T(8,128)(2,1)S(1)}, u32[]{:S(2)}, u32[]{:S(2)}) %collective-permute-start.5) | collective-permute-done | bytes 589856 | tf_op jit(solution)/shard_map/ppermute | solution.py:965
  76.7 7.1 %fusion.46.refs_0_.refs_1_.refs_2_.refs_3_ = f32[1024,1152]{1,0:T(8,128)} fusion(bf16[1024,2048]{1,0:T(8,128)(2,1)S(1)} %pad_maximum_fusion.normed_ref, bf16[2048,1152]{1,0:T(8,128)(2,1)S(1)} %constant_dynamic-update-slice_fusion.weights_ref), kind=kOutput, calls=%fused_computation.134 | convolution fusion | flops 4831838208 | bytes 13631488 | tf_op jit(solution)/shard_map/dot_general | solution.py:1059
  87.7 18.3 %mixer_forward.1 = (f32[1024,512]{1,0:T(8,128)}, bf16[2048,256]{1,0:T(8,128)(2,1)}, bf16[2048,128]{1,0:T(8,128)(2,1)}, bf16[1024,512]{1,0:T(8,128)(2,1)}, f32[1024,1024]{1,0:T(8,128)}, /*index=5*/f32[1024,1024]{1,0:T(8,128)}) custom-call(s32[8]{0:T(128)} %fusion.32.order_ref, f32[1024,1152]{1,0:T(8,128)} %fusion.46.refs_0_.refs_1_.refs_2_.refs_3_, ...), custom_call_target="tpu_custom_call" | custom-call | flops 1 | bytes 1 | tf_op jit(solution)/shard_map/mixer_forward/pallas_call | solution.py:400
  108.4 10.9 %head_outputs.1 = (f32[1024,512]{1,0:T(8,128)}, bf16[1024,512]{1,0:T(8,128)(2,1)}, bf16[512,2048]{1,0:T(8,128)(2,1)}, bf16[512,2048]{1,0:T(8,128)(2,1)}) custom-call(bf16[1024,2048]{1,0:T(8,128)(2,1)} %copy-done, f32[1024,512]{1,0:T(8,128)} %get-tuple-element.148.mixed_ref.refs_9_.refs_10_, bf16[4,2,512,512]{3,2,1,0:T(8,128)(2,1)} %bitcast.82, ...), custom_call_target="tpu_custom_call" | custom-call | flops 1 | bytes 1 | tf_op jit(solution)/shard_map/head_outputs/pallas_call | solution.py:675
  120.0 4.0 collective-permute-done.9
  130.4 10.2 %collective-permute-done.10 = bf16[128,2048]{1,0:T(8,128)(2,1)S(1)} collective-permute-done((bf16[128,2048]{1,0:T(8,128)(2,1)S(1)}, bf16[128,2048]{1,0:T(8,128)(2,1)S(1)}, u32[]{:S(2)}, u32[]{:S(2)}) %collective-permute-start.10) | collective-permute-done | bytes 524320 | tf_op jit(solution)/shard_map/ppermute | solution.py:1022
  140.9 4.2 collective-permute-start.11
  145.8 9.4 %collective-permute-done.11 = bf16[128,2048]{1,0:T(8,128)(2,1)S(1)} collective-permute-done((bf16[128,2048]{1,0:T(8,128)(2,1)S(1)}, bf16[128,2048]{1,0:T(8,128)(2,1)S(1)}, u32[]{:S(2)}, u32[]{:S(2)}) %collective-permute-start.11) | collective-permute-done | bytes 524320 | tf_op jit(solution)/shard_map/ppermute | solution.py:1022
  156.4 7.8 %collective-permute-start.12 = (bf16[128,2048]{1,0:T(8,128)(2,1)}, bf16[128,2048]{1,0:T(8,128)(2,1)S(1)}, u32[]{:S(2)}, u32[]{:S(2)}) collective-permute-start(bf16[128,2048]{1,0:T(8,128)(2,1)} %get-tuple-element.287), channel_id=1, source_target_pairs={{0,1},{1,2},{2,3},{4,5},{5,6},{6,7},{8,9},{9,10},{10,11},{12,13},{... | collective-permute-start | bytes 1572872 | tf_op jit(solution)/shard_map/ppermute | solution.py:1022
  165.5 8.0 %collective-permute-done.12 = bf16[128,2048]{1,0:T(8,128)(2,1)S(1)} collective-permute-done((bf16[128,2048]{1,0:T(8,128)(2,1)}, bf16[128,2048]{1,0:T(8,128)(2,1)S(1)}, u32[]{:S(2)}, u32[]{:S(2)}) %collective-permute-start.12) | collective-permute-done | bytes 524320 | tf_op jit(solution)/shard_map/ppermute | solution.py:1022
  180.4 4.0 collective-permute-start.16
  184.4 6.7 %collective-permute-done.17 = bf16[128,2048]{1,0:T(8,128)(2,1)S(1)} collective-permute-done((bf16[128,2048]{1,0:T(8,128)(2,1)S(1)}, bf16[128,2048]{1,0:T(8,128)(2,1)S(1)}, u32[]{:S(2)}, u32[]{:S(2)}) %collective-permute-start.17) | collective-permute-done | bytes 524320 | tf_op jit(solution)/shard_map/ppermute | solution.py:1038
  193.1 9.2 %collective-permute-done.18 = bf16[128,2048]{1,0:T(8,128)(2,1)S(1)} collective-permute-done((bf16[128,2048]{1,0:T(8,128)(2,1)S(1)}, bf16[128,2048]{1,0:T(8,128)(2,1)S(1)}, u32[]{:S(2)}, u32[]{:S(2)}) %collective-permute-start.18) | collective-permute-done | bytes 524320 | tf_op jit(solution)/shard_map/ppermute | solution.py:1038
  204.6 8.0 %collective-permute-done.19 = bf16[128,2048]{1,0:T(8,128)(2,1)S(1)} collective-permute-done((bf16[128,2048]{1,0:T(8,128)(2,1)S(1)}, bf16[128,2048]{1,0:T(8,128)(2,1)S(1)}, u32[]{:S(2)}, u32[]{:S(2)}) %collective-permute-start.19) | collective-permute-done | bytes 524320 | tf_op jit(solution)/shard_map/ppermute | solution.py:1038
  213.1 6.0 %collective-permute-start.22 = (bf16[512,2048]{1,0:T(8,128)(2,1)S(1)}, bf16[512,2048]{1,0:T(8,128)(2,1)}, u32[]{:S(2)}, u32[]{:S(2)}) collective-permute-start(bf16[512,2048]{1,0:T(8,128)(2,1)S(1)} %pad_maximum_fusion.1.hidden_ref.h_own), channel_id=1, source_target_pairs={{0,4},{4,0},{1,5},{5,1},{2,6},{6,2},{3,7},{7,3},{8,12},{12,8},{9,1... | collective-permute-start | bytes 6291464 | tf_op jit(solution)/shard_map/ppermute | solution.py:969
  219.0 3.9 collective-permute-done.22.hidden_ref.h_other
  223.0 18.0 %feed_forward.3 = (bf16[3,512,704]{2,1,0:T(8,128)(2,1)}, bf16[512,2048]{1,0:T(8,128)(2,1)}, bf16[512,2048]{1,0:T(8,128)(2,1)}) custom-call(s32[4]{0:T(128)} %copy-done.31, bf16[512,2048]{1,0:T(8,128)(2,1)} %collective-permute-done.22.hidden_ref.h_other, bf16[512,2048]{1,0:T(8,128)(2,1)} %copy-done.6, bf16[4,3,512,704]{3,2,1,0:T(8,128)(2,1)} %bitcast.80), custom_call_target="tpu_custom_call" | custom-call | flops 1 | bytes 1 | tf_op jit(solution)/shard_map/feed_forward/pallas_call | solution.py:738
  241.3 18.0 %feed_forward.2 = (bf16[3,512,704]{2,1,0:T(8,128)(2,1)}, bf16[512,2048]{1,0:T(8,128)(2,1)}, bf16[512,2048]{1,0:T(8,128)(2,1)}) custom-call(s32[4]{0:T(128)} %copy-done.31, bf16[512,2048]{1,0:T(8,128)(2,1)} %copy-done.4, bf16[512,2048]{1,0:T(8,128)(2,1)} %get-tuple-element.144.branch_ref.b_own, bf16[4,3,512,704]{3,2,1,0:T(8,128)(2,1)} %bitcast.81), custom_call_target="tpu_custom_call" | custom-call | flops 1 | bytes 1 | tf_op jit(solution)/shard_map/feed_forward/pallas_call | solution.py:738
  259.3 3.8 add_convert_fusion.2
  263.6 15.4 %feed_grads.1 = bf16[2048,2176]{1,0:T(8,128)(2,1)} custom-call(bf16[512,2048]{1,0:T(8,128)(2,1)} %copy-done.4, bf16[512,2048]{1,0:T(8,128)(2,1)} %collective-permute-done.22.hidden_ref.h_other, bf16[512,2048]{1,0:T(8,128)(2,1)} %get-tuple-element.144.branch_ref.b_own, bf16[512,2048]{1,0:T(8,128)(2,1)} %copy-done.6, ...), custom_call_target="tpu_custom_call" | custom-call | flops 1 | bytes 1 | tf_op jit(solution)/shard_map/feed_grads/pallas_call | solution.py:778
  279.0 3.7 add_convert_fusion.1
  282.7 24.5 %reduce-scatter.5.cloned.1.call-done = bf16[128,2048]{1,0:T(8,128)(2,1)} async-done(((bf16[512,2048]{1,0:T(8,128)(2,1)}), bf16[128,2048]{1,0:T(8,128)(2,1)}) %reduce-scatter.5.cloned.1.call-update) | async-done | bytes 524304 | tf_op jit(solution)/shard_map/reduce_scatter | solution.py:1175
  311.3 4.0 collective-permute-start.25
  315.3 9.3 %collective-permute-done.26 = bf16[128,2048]{1,0:T(8,128)(2,1)S(1)} collective-permute-done((bf16[128,2048]{1,0:T(8,128)(2,1)S(1)}, bf16[128,2048]{1,0:T(8,128)(2,1)S(1)}, u32[]{:S(2)}, u32[]{:S(2)}) %collective-permute-start.26) | collective-permute-done | bytes 524320 | tf_op jit(solution)/shard_map/ppermute | solution.py:1038
  326.6 11.8 %collective-permute-done.27 = bf16[128,2048]{1,0:T(8,128)(2,1)S(1)} collective-permute-done((bf16[128,2048]{1,0:T(8,128)(2,1)S(1)}, bf16[128,2048]{1,0:T(8,128)(2,1)S(1)}, u32[]{:S(2)}, u32[]{:S(2)}) %collective-permute-start.27) | collective-permute-done | bytes 524320 | tf_op jit(solution)/shard_map/ppermute | solution.py:1038
  340.5 10.8 %collective-permute-done.28 = bf16[128,2048]{1,0:T(8,128)(2,1)S(1)} collective-permute-done((bf16[128,2048]{1,0:T(8,128)(2,1)S(1)}, bf16[128,2048]{1,0:T(8,128)(2,1)S(1)}, u32[]{:S(2)}, u32[]{:S(2)}) %collective-permute-start.28) | collective-permute-done | bytes 524320 | tf_op jit(solution)/shard_map/ppermute | solution.py:1038
  356.4 4.5 collective-permute-start.31
  362.6 32.2 %mixer_backward.1 = (bf16[1024,1664]{1,0:T(8,128)(2,1)}, f32[8,1024]{1,0:T(8,128)}, f32[8,128]{1,0:T(8,128)}, f32[8,256]{1,0:T(8,128)}) custom-call(s32[8]{0:T(128)} %fusion.32.order_ref, f32[1024,1152]{1,0:T(8,128)} %fusion.46.refs_0_.refs_1_.refs_2_.refs_3_, f32[1024,1152]{1,0:T(8,128)} %fusion.46.refs_0_.refs_1_.refs_2_.refs_3_, ...), custom_call_target="tpu_custom_call" | custom-call | flops 1 | bytes 1 | tf_op jit(solution)/shard_map/mixer_backward/pallas_call | solution.py:450
  394.8 8.4 %collective-permute-done.32 = bf16[128,2048]{1,0:T(8,128)(2,1)} collective-permute-done((bf16[128,2048]{1,0:T(8,128)(2,1)}, bf16[128,2048]{1,0:T(8,128)(2,1)}, u32[]{:S(2)}, u32[]{:S(2)}) %collective-permute-start.32) | collective-permute-done | bytes 524320 | tf_op jit(solution)/shard_map/ppermute | solution.py:999
  404.8 4.7 collective-permute-start.35
  411.1 13.6 %d_normed_rows.1 = (bf16[512,2048]{1,0:T(8,128)(2,1)}, bf16[512,2048]{1,0:T(8,128)(2,1)}, f32[8,2048]{1,0:T(8,128)}) custom-call(bf16[1024,1664]{1,0:T(8,128)(2,1)} %get-tuple-element.190.mix_ref, bf16[1024,2048]{1,0:T(8,128)(2,1)} %copy-done, bf16[2048,1152]{1,0:T(8,128)(2,1)} %copy-done.3, bf16[4,2,512,512]{3,2,1,0:T(8,128)(2,1)} %bitcast.84), custom_call_target="tpu_custom_call" | custom-call | flops 1 | bytes 1 | tf_op jit(solution)/shard_map/d_normed_rows/pallas_call | solution.py:820
  427.5 6.1 %out_grads.1 = bf16[2048,512]{1,0:T(8,128)(2,1)} custom-call(bf16[512,2048]{1,0:T(8,128)(2,1)} %copy-done.1, bf16[512,2048]{1,0:T(8,128)(2,1)} %copy-done.2, bf16[1024,512]{1,0:T(8,128)(2,1)} %get-tuple-element.186.heads_ref), custom_call_target="tpu_custom_call" | custom-call | flops 1 | bytes 1 | tf_op jit(solution)/shard_map/out_grads/pallas_call | solution.py:876
  440.5 9.4 %collective-permute-start.38 = (bf16[128,2048]{1,0:T(8,128)(2,1)}, bf16[128,2048]{1,0:T(8,128)(2,1)}, u32[]{:S(2)}, u32[]{:S(2)}) collective-permute-start(bf16[128,2048]{1,0:T(8,128)(2,1)} %get-tuple-element.283), channel_id=1, source_target_pairs={{0,1},{4,5},{8,9},{12,13},{16,17},{20,21},{24,25},{28,29}} | collective-permute-start | bytes 1572872 | tf_op jit(solution)/shard_map/ppermute | solution.py:1022
  451.4 12.1 %mix_grads.1 = bf16[2048,1664]{1,0:T(8,128)(2,1)} custom-call(bf16[1024,2048]{1,0:T(8,128)(2,1)} %copy-done, bf16[1024,1664]{1,0:T(8,128)(2,1)} %get-tuple-element.190.mix_ref), custom_call_target="tpu_custom_call" | custom-call | flops 1 | bytes 1 | tf_op jit(solution)/shard_map/mix_grads/pallas_call | solution.py:851
  478.1 6.4 %finish.3 = (f32[512,1408]{1,0:T(8,128)}, f32[512,1408]{1,0:T(8,128)}, f32[1408,512]{1,0:T(8,128)}) custom-call(s32[1]{0:T(128)} %bitcast.2.core_ref, bf16[512,2176]{1,0:T(8,128)(2,1)} %reduce-scatter.7.cloned.1.call-done.own_ref, bf16[512,2176]{1,0:T(8,128)(2,1)} %copy-done.14), custom_call_target="tpu_custom_call" | custom-call | flops 1 | bytes 1 | tf_op jit(solution)/shard_map/finish/pallas_call | solution.py:942
  484.5 5.4 collective-permute-done.47.refs_6_
  495.6 4.2 collective-permute-start.51
  499.8 4.5 place.2
  504.4 3.8 collective-permute-done.50
  524.0 4.0 finish.4
  534.9 8.7 %collective-permute-done.57.refs_5_ = bf16[128,2048]{1,0:T(8,128)(2,1)S(1)} collective-permute-done((bf16[128,2048]{1,0:T(8,128)(2,1)S(1)}, bf16[128,2048]{1,0:T(8,128)(2,1)S(1)}, u32[]{:S(2)}, u32[]{:S(2)}) %collective-permute-start.57) | collective-permute-done | bytes 524320 | tf_op jit(solution)/shard_map/ppermute | solution.py:1046
  543.6 3.6 collective-permute-start.62
  551.5 11.9 %collective-permute-done.60.refs_6_ = bf16[128,2048]{1,0:T(8,128)(2,1)S(1)} collective-permute-done((bf16[128,2048]{1,0:T(8,128)(2,1)S(1)}, bf16[128,2048]{1,0:T(8,128)(2,1)S(1)}, u32[]{:S(2)}, u32[]{:S(2)}) %collective-permute-start.60) | collective-permute-done | bytes 524320 | tf_op jit(solution)/shard_map/ppermute | solution.py:1046
  564.2 4.2 place.3
  574.4 5.0 finish.5
  (299 shorter events, 142.6 us)
Async XLA Ops:
  7.2 101.3 %all-gather.3.cloned.1.call-start = ((), (), s32[]{:S(2)}) async-start(), calls=%async_computation.4 | async-start | bytes 5242880 | tf_op jit(solution)/shard_map/all_gather | solution.py:1154
  14.3 12.2 %collective-permute-start.2 = (bf16[2112]{0:T(1024)(128)(2,1)S(1)}, bf16[2112]{0:T(1024)(128)(2,1)S(1)}, u32[]{:S(2)}, u32[]{:S(2)}) collective-permute-start(bf16[2112]{0:T(1024)(128)(2,1)S(1)} %concatenate.37), channel_id=1, source_target_pairs={{0,8},{8,0},{16,24},{24,16},{1,9},{9,1},{17,25},{25,17},{2,10},{10... | collective-permute-start | bytes 12680 | tf_op jit(solution)/shard_map/ppermute | solution.py:965
  17.6 26.6 %collective-permute-start = (bf16[512,1152]{1,0:T(8,128)(2,1)}, bf16[512,1152]{1,0:T(8,128)(2,1)S(1)}, u32[]{:S(2)}, u32[]{:S(2)}) collective-permute-start(bf16[512,1152]{1,0:T(8,128)(2,1)} %pack_mix.1), channel_id=1, source_target_pairs={{0,8},{8,0},{16,24},{24,16},{1,9},{9,1},{17,25},{25,17},{2,10},{10... | collective-permute-start | bytes 3538952 | tf_op jit(solution)/shard_map/ppermute | solution.py:965
  19.0 26.0 %collective-permute-start.1 = (bf16[512,1152]{1,0:T(8,128)(2,1)}, bf16[512,1152]{1,0:T(8,128)(2,1)S(1)}, u32[]{:S(2)}, u32[]{:S(2)}) collective-permute-start(bf16[512,1152]{1,0:T(8,128)(2,1)} %pack_mix.1), channel_id=1, source_target_pairs={{0,16},{8,24},{16,0},{24,8},{1,17},{9,25},{17,1},{25,9},{2,18},{10... | collective-permute-start | bytes 3538952 | tf_op jit(solution)/shard_map/ppermute | solution.py:965
  45.0 177.9 %all-gather.5.cloned.1.call-start = ((), (), s32[]{:S(2)}) async-start(), calls=%async_computation.5 | async-start | bytes 11796480 | tf_op jit(solution)/shard_map/all_gather | solution.py:1158
  47.8 26.4 %collective-permute-start.8 = (bf16[512,2048]{1,0:T(8,128)(2,1)}, bf16[512,2048]{1,0:T(8,128)(2,1)S(1)}, u32[]{:S(2)}, u32[]{:S(2)}) collective-permute-start(bf16[512,2048]{1,0:T(8,128)(2,1)} %get-tuple-element.144.branch_ref.b_own), channel_id=1, source_target_pairs={{0,4},{4,0},{1,5},{5,1},{2,6},{6,2},{3,7},{7,3},{8,12},{12,8},{9,1... | collective-permute-start | bytes 6291464 | tf_op jit(solution)/shard_map/ppermute | solution.py:969
  50.2 21.6 %collective-permute-start.5 = (bf16[256,1152]{1,0:T(8,128)(2,1)S(1)}, bf16[256,1152]{1,0:T(8,128)(2,1)S(1)}, u32[]{:S(2)}, u32[]{:S(2)}) collective-permute-start(bf16[256,1152]{1,0:T(8,128)(2,1)S(1)} %slice.151), channel_id=1, source_target_pairs={{0,16},{8,24},{16,0},{24,8},{1,17},{9,25},{17,1},{25,9},{2,18},{10... | collective-permute-start | bytes 1769480 | tf_op jit(solution)/shard_map/ppermute | solution.py:965
  51.6 22.7 %collective-permute-start.6 = (bf16[256,1152]{1,0:T(8,128)(2,1)S(1)}, bf16[256,1152]{1,0:T(8,128)(2,1)S(1)}, u32[]{:S(2)}, u32[]{:S(2)}) collective-permute-start(bf16[256,1152]{1,0:T(8,128)(2,1)S(1)} %slice.152), channel_id=1, source_target_pairs={{0,8},{8,0},{16,24},{24,16},{1,9},{9,1},{17,25},{25,17},{2,10},{10... | collective-permute-start | bytes 1769480 | tf_op jit(solution)/shard_map/ppermute | solution.py:965
  83.9 223.3 %reduce-scatter.5.cloned.1.call-start = ((), (), s32[]{:S(2)}) async-start(), calls=%async_computation.6 | async-start | bytes 2621440 | tf_op jit(solution)/shard_map/reduce_scatter | solution.py:1175
  126.5 14.0 %collective-permute-start.10 = (bf16[128,2048]{1,0:T(8,128)(2,1)S(1)}, bf16[128,2048]{1,0:T(8,128)(2,1)S(1)}, u32[]{:S(2)}, u32[]{:S(2)}) collective-permute-start(bf16[128,2048]{1,0:T(8,128)(2,1)S(1)} %get-tuple-element.291), channel_id=1, source_target_pairs={{0,1},{4,5},{8,9},{12,13},{16,17},{20,21},{24,25},{28,29}} | collective-permute-start | bytes 1572872 | tf_op jit(solution)/shard_map/ppermute | solution.py:1022
  140.9 14.3 %collective-permute-start.11 = (bf16[128,2048]{1,0:T(8,128)(2,1)S(1)}, bf16[128,2048]{1,0:T(8,128)(2,1)S(1)}, u32[]{:S(2)}, u32[]{:S(2)}) collective-permute-start(bf16[128,2048]{1,0:T(8,128)(2,1)S(1)} %get-tuple-element.289), channel_id=1, source_target_pairs={{0,1},{1,2},{4,5},{5,6},{8,9},{9,10},{12,13},{13,14},{16,17},{17,1... | collective-permute-start | bytes 1572872 | tf_op jit(solution)/shard_map/ppermute | solution.py:1022
  156.4 17.1 %collective-permute-start.12 = (bf16[128,2048]{1,0:T(8,128)(2,1)}, bf16[128,2048]{1,0:T(8,128)(2,1)S(1)}, u32[]{:S(2)}, u32[]{:S(2)}) collective-permute-start(bf16[128,2048]{1,0:T(8,128)(2,1)} %get-tuple-element.287), channel_id=1, source_target_pairs={{0,1},{1,2},{2,3},{4,5},{5,6},{6,7},{8,9},{9,10},{10,11},{12,13},{... | collective-permute-start | bytes 1572872 | tf_op jit(solution)/shard_map/ppermute | solution.py:1022
  164.1 12.9 %collective-permute-start.15 = (bf16[128,2048]{1,0:T(8,128)(2,1)S(1)}, bf16[128,2048]{1,0:T(8,128)(2,1)}, u32[]{:S(2)}, u32[]{:S(2)}) collective-permute-start(bf16[128,2048]{1,0:T(8,128)(2,1)S(1)} %get-tuple-element.288), channel_id=1, source_target_pairs={{1,0},{2,1},{3,2},{5,4},{6,5},{7,6},{9,8},{10,9},{11,10},{13,12},{... | collective-permute-start | bytes 1572872 | tf_op jit(solution)/shard_map/ppermute | solution.py:1023
  179.1 12.0 %collective-permute-start.17 = (bf16[128,2048]{1,0:T(8,128)(2,1)S(1)}, bf16[128,2048]{1,0:T(8,128)(2,1)S(1)}, u32[]{:S(2)}, u32[]{:S(2)}) collective-permute-start(bf16[128,2048]{1,0:T(8,128)(2,1)S(1)} %multiply_convert_fusion.1), channel_id=1, source_target_pairs={{1,0},{2,1},{3,2},{5,4},{6,5},{7,6},{9,8},{10,9},{11,10},{13,12},{... | collective-permute-start | bytes 1572872 | tf_op jit(solution)/shard_map/ppermute | solution.py:1038
  180.4 12.0 %collective-permute-start.16 = (bf16[128,2048]{1,0:T(8,128)(2,1)S(1)}, bf16[128,2048]{1,0:T(8,128)(2,1)S(1)}, u32[]{:S(2)}, u32[]{:S(2)}) collective-permute-start(bf16[128,2048]{1,0:T(8,128)(2,1)S(1)} %multiply_convert_fusion.1), channel_id=1, source_target_pairs={{0,1},{1,2},{2,3},{4,5},{5,6},{6,7},{8,9},{9,10},{10,11},{12,13},{... | collective-permute-start | bytes 1572872 | tf_op jit(solution)/shard_map/ppermute | solution.py:1036
  191.1 11.2 %collective-permute-start.18 = (bf16[128,2048]{1,0:T(8,128)(2,1)S(1)}, bf16[128,2048]{1,0:T(8,128)(2,1)S(1)}, u32[]{:S(2)}, u32[]{:S(2)}) collective-permute-start(bf16[128,2048]{1,0:T(8,128)(2,1)S(1)} %collective-permute-done.17), channel_id=1, source_target_pairs={{1,0},{2,1},{5,4},{6,5},{9,8},{10,9},{13,12},{14,13},{17,16},{18,1... | collective-permute-start | bytes 1572872 | tf_op jit(solution)/shard_map/ppermute | solution.py:1038
  240.9 18.4 %collective-permute-start.23 = (bf16[512,2048]{1,0:T(8,128)(2,1)}, bf16[512,2048]{1,0:T(8,128)(2,1)S(1)}, u32[]{:S(2)}, u32[]{:S(2)}) collective-permute-start(bf16[512,2048]{1,0:T(8,128)(2,1)} %get-tuple-element.156), channel_id=1, source_target_pairs={{0,4},{4,0},{1,5},{5,1},{2,6},{6,2},{3,7},{7,3},{8,12},{12,8},{9,1... | collective-permute-start | bytes 6291464 | tf_op jit(solution)/shard_map/ppermute | solution.py:969
  263.1 141.7 %reduce-scatter.7.cloned.1.call-start = ((), (), s32[]{:S(2)}) async-start(), calls=%async_computation.7 | async-start | bytes 11141120 | tf_op jit(solution)/shard_map/reduce_scatter | solution.py:992
  263.4 15.6 %collective-permute-start.24 = (bf16[512,2048]{1,0:T(8,128)(2,1)}, bf16[512,2048]{1,0:T(8,128)(2,1)}, u32[]{:S(2)}, u32[]{:S(2)}) collective-permute-start(bf16[512,2048]{1,0:T(8,128)(2,1)} %get-tuple-element.163), channel_id=1, source_target_pairs={{0,4},{4,0},{1,5},{5,1},{2,6},{6,2},{3,7},{7,3},{8,12},{12,8},{9,1... | collective-permute-start | bytes 6291464 | tf_op jit(solution)/shard_map/ppermute | solution.py:969
  307.2 210.7 %reduce-scatter.11.cloned.1.call-start = ((), (), s32[]{:S(2)}) async-start(), calls=%async_computation.9 | async-start | bytes 2621440 | tf_op jit(solution)/shard_map/reduce_scatter | solution.py:992
  310.0 14.6 %collective-permute-start.26 = (bf16[128,2048]{1,0:T(8,128)(2,1)S(1)}, bf16[128,2048]{1,0:T(8,128)(2,1)S(1)}, u32[]{:S(2)}, u32[]{:S(2)}) collective-permute-start(bf16[128,2048]{1,0:T(8,128)(2,1)S(1)} %multiply_convert_fusion), channel_id=1, source_target_pairs={{1,0},{2,1},{3,2},{5,4},{6,5},{7,6},{9,8},{10,9},{11,10},{13,12},{... | collective-permute-start | bytes 1572872 | tf_op jit(solution)/shard_map/ppermute | solution.py:1038
  311.3 14.6 %collective-permute-start.25 = (bf16[128,2048]{1,0:T(8,128)(2,1)S(1)}, bf16[128,2048]{1,0:T(8,128)(2,1)S(1)}, u32[]{:S(2)}, u32[]{:S(2)}) collective-permute-start(bf16[128,2048]{1,0:T(8,128)(2,1)S(1)} %multiply_convert_fusion), channel_id=1, source_target_pairs={{0,1},{1,2},{2,3},{4,5},{5,6},{6,7},{8,9},{9,10},{10,11},{12,13},{... | collective-permute-start | bytes 1572872 | tf_op jit(solution)/shard_map/ppermute | solution.py:1036
  324.6 13.8 %collective-permute-start.27 = (bf16[128,2048]{1,0:T(8,128)(2,1)S(1)}, bf16[128,2048]{1,0:T(8,128)(2,1)S(1)}, u32[]{:S(2)}, u32[]{:S(2)}) collective-permute-start(bf16[128,2048]{1,0:T(8,128)(2,1)S(1)} %collective-permute-done.26), channel_id=1, source_target_pairs={{1,0},{2,1},{5,4},{6,5},{9,8},{10,9},{13,12},{14,13},{17,16},{18,1... | collective-permute-start | bytes 1572872 | tf_op jit(solution)/shard_map/ppermute | solution.py:1038
  325.9 13.8 %collective-permute-start.29 = (bf16[128,2048]{1,0:T(8,128)(2,1)S(1)}, bf16[128,2048]{1,0:T(8,128)(2,1)S(1)}, u32[]{:S(2)}, u32[]{:S(2)}) collective-permute-start(bf16[128,2048]{1,0:T(8,128)(2,1)S(1)} %collective-permute-done.25), channel_id=1, source_target_pairs={{1,2},{2,3},{5,6},{6,7},{9,10},{10,11},{13,14},{14,15},{17,18},{18... | collective-permute-start | bytes 1572872 | tf_op jit(solution)/shard_map/ppermute | solution.py:1036
  338.4 13.0 %collective-permute-start.28 = (bf16[128,2048]{1,0:T(8,128)(2,1)S(1)}, bf16[128,2048]{1,0:T(8,128)(2,1)S(1)}, u32[]{:S(2)}, u32[]{:S(2)}) collective-permute-start(bf16[128,2048]{1,0:T(8,128)(2,1)S(1)} %collective-permute-done.27), channel_id=1, source_target_pairs={{1,0},{5,4},{9,8},{13,12},{17,16},{21,20},{25,24},{29,28}} | collective-permute-start | bytes 1572872 | tf_op jit(solution)/shard_map/ppermute | solution.py:1038
  339.7 11.8 %collective-permute-start.30 = (bf16[128,2048]{1,0:T(8,128)(2,1)S(1)}, bf16[128,2048]{1,0:T(8,128)(2,1)S(1)}, u32[]{:S(2)}, u32[]{:S(2)}) collective-permute-start(bf16[128,2048]{1,0:T(8,128)(2,1)S(1)} %collective-permute-done.29), channel_id=1, source_target_pairs={{2,3},{6,7},{10,11},{14,15},{18,19},{22,23},{26,27},{30,31}} | collective-permute-start | bytes 1572872 | tf_op jit(solution)/shard_map/ppermute | solution.py:1036
  356.4 38.4 %collective-permute-start.31 = (bf16[128,2048]{1,0:T(8,128)(2,1)}, bf16[128,2048]{1,0:T(8,128)(2,1)S(1)}, u32[]{:S(2)}, u32[]{:S(2)}) collective-permute-start(bf16[128,2048]{1,0:T(8,128)(2,1)} %get-tuple-element.286), channel_id=1, source_target_pairs={{0,3},{1,0},{2,1},{3,2},{4,7},{5,4},{6,5},{7,6},{8,11},{9,8},{10,9... | collective-permute-start | bytes 1572872 | tf_op jit(solution)/shard_map/ppermute | solution.py:999
  360.9 42.2 %collective-permute-start.32 = (bf16[128,2048]{1,0:T(8,128)(2,1)}, bf16[128,2048]{1,0:T(8,128)(2,1)}, u32[]{:S(2)}, u32[]{:S(2)}) collective-permute-start(bf16[128,2048]{1,0:T(8,128)(2,1)} %get-tuple-element.285), channel_id=1, source_target_pairs={{0,2},{1,3},{2,0},{3,1},{4,6},{5,7},{6,4},{7,5},{8,10},{9,11},{10,... | collective-permute-start | bytes 1572872 | tf_op jit(solution)/shard_map/ppermute | solution.py:999
  360.9 42.2 %collective-permute-start.33 = (bf16[128,2048]{1,0:T(8,128)(2,1)}, bf16[128,2048]{1,0:T(8,128)(2,1)}, u32[]{:S(2)}, u32[]{:S(2)}) collective-permute-start(bf16[128,2048]{1,0:T(8,128)(2,1)} %get-tuple-element.284), channel_id=1, source_target_pairs={{0,1},{1,2},{2,3},{3,0},{4,5},{5,6},{6,7},{7,4},{8,9},{9,10},{10,1... | collective-permute-start | bytes 1572872 | tf_op jit(solution)/shard_map/ppermute | solution.py:999
  404.8 19.9 %collective-permute-start.35 = (bf16[128,2048]{1,0:T(8,128)(2,1)S(1)}, bf16[128,2048]{1,0:T(8,128)(2,1)S(1)}, u32[]{:S(2)}, u32[]{:S(2)}) collective-permute-start(bf16[128,2048]{1,0:T(8,128)(2,1)S(1)} %add_convert_fusion.6.refs_0_), channel_id=1, source_target_pairs={{0,1},{1,2},{2,3},{4,5},{5,6},{6,7},{8,9},{9,10},{10,11},{12,13},{... | collective-permute-start | bytes 1572872 | tf_op jit(solution)/shard_map/ppermute | solution.py:1045
  409.6 15.2 %collective-permute-start.36 = (bf16[128,2048]{1,0:T(8,128)(2,1)S(1)}, bf16[128,2048]{1,0:T(8,128)(2,1)S(1)}, u32[]{:S(2)}, u32[]{:S(2)}) collective-permute-start(bf16[128,2048]{1,0:T(8,128)(2,1)S(1)} %add_convert_fusion.6.refs_0_), channel_id=1, source_target_pairs={{1,0},{2,1},{3,2},{5,4},{6,5},{7,6},{9,8},{10,9},{11,10},{13,12},{... | collective-permute-start | bytes 1572872 | tf_op jit(solution)/shard_map/ppermute | solution.py:1046
  433.6 134.8 %reduce-scatter.9.cloned.1.call-start = ((), (), s32[]{:S(2)}) async-start(), calls=%async_computation.8 | async-start | bytes 8519680 | tf_op jit(solution)/shard_map/reduce_scatter | solution.py:992
  433.6 29.8 %collective-permute-start.40 = (bf16[128,2048]{1,0:T(8,128)(2,1)}, bf16[128,2048]{1,0:T(8,128)(2,1)}, u32[]{:S(2)}, u32[]{:S(2)}) collective-permute-start(bf16[128,2048]{1,0:T(8,128)(2,1)} %copy-done.19), channel_id=1, source_target_pairs={{1,2},{2,3},{5,6},{6,7},{9,10},{10,11},{13,14},{14,15},{17,18},{18... | collective-permute-start | bytes 1572872 | tf_op jit(solution)/shard_map/ppermute | solution.py:1045
  435.1 28.3 %collective-permute-start.41 = (bf16[128,2048]{1,0:T(8,128)(2,1)}, bf16[128,2048]{1,0:T(8,128)(2,1)}, u32[]{:S(2)}, u32[]{:S(2)}) collective-permute-start(bf16[128,2048]{1,0:T(8,128)(2,1)} %copy-done.20), channel_id=1, source_target_pairs={{1,0},{2,1},{5,4},{6,5},{9,8},{10,9},{13,12},{14,13},{17,16},{18,1... | collective-permute-start | bytes 1572872 | tf_op jit(solution)/shard_map/ppermute | solution.py:1046
  440.5 23.0 %collective-permute-start.38 = (bf16[128,2048]{1,0:T(8,128)(2,1)}, bf16[128,2048]{1,0:T(8,128)(2,1)}, u32[]{:S(2)}, u32[]{:S(2)}) collective-permute-start(bf16[128,2048]{1,0:T(8,128)(2,1)} %get-tuple-element.283), channel_id=1, source_target_pairs={{0,1},{4,5},{8,9},{12,13},{16,17},{20,21},{24,25},{28,29}} | collective-permute-start | bytes 1572872 | tf_op jit(solution)/shard_map/ppermute | solution.py:1022
  449.9 13.6 %collective-permute-start.39 = (bf16[128,2048]{1,0:T(8,128)(2,1)}, bf16[128,2048]{1,0:T(8,128)(2,1)}, u32[]{:S(2)}, u32[]{:S(2)}) collective-permute-start(bf16[128,2048]{1,0:T(8,128)(2,1)} %get-tuple-element.282), channel_id=1, source_target_pairs={{3,2},{7,6},{11,10},{15,14},{19,18},{23,22},{27,26},{31,30}} | collective-permute-start | bytes 1572872 | tf_op jit(solution)/shard_map/ppermute | solution.py:1023
  463.5 12.1 %collective-permute-start.45 = (bf16[512,2176]{1,0:T(8,128)(2,1)}, bf16[512,2176]{1,0:T(8,128)(2,1)S(1)}, u32[]{:S(2)}, u32[]{:S(2)}) collective-permute-start(bf16[512,2176]{1,0:T(8,128)(2,1)} %reduce-scatter.7.cloned.1.call-done.own_ref), channel_id=1, source_target_pairs={{0,4},{4,0},{1,5},{5,1},{2,6},{6,2},{3,7},{7,3},{8,12},{12,8},{9,1... | collective-permute-start | bytes 6684680 | tf_op jit(solution)/shard_map/ppermute | solution.py:969
  469.7 14.8 %collective-permute-start.43 = (bf16[128,2048]{1,0:T(8,128)(2,1)S(1)}, bf16[128,2048]{1,0:T(8,128)(2,1)}, u32[]{:S(2)}, u32[]{:S(2)}) collective-permute-start(bf16[128,2048]{1,0:T(8,128)(2,1)S(1)} %get-tuple-element.281), channel_id=1, source_target_pairs={{0,1},{1,2},{4,5},{5,6},{8,9},{9,10},{12,13},{13,14},{16,17},{17,1... | collective-permute-start | bytes 1572872 | tf_op jit(solution)/shard_map/ppermute | solution.py:1022
  472.1 12.4 %collective-permute-start.44 = (bf16[128,2048]{1,0:T(8,128)(2,1)S(1)}, bf16[128,2048]{1,0:T(8,128)(2,1)}, u32[]{:S(2)}, u32[]{:S(2)}) collective-permute-start(bf16[128,2048]{1,0:T(8,128)(2,1)S(1)} %get-tuple-element.280), channel_id=1, source_target_pairs={{2,1},{3,2},{6,5},{7,6},{10,9},{11,10},{14,13},{15,14},{18,17},{19... | collective-permute-start | bytes 1572872 | tf_op jit(solution)/shard_map/ppermute | solution.py:1023
  474.2 15.6 %collective-permute-start.47 = (bf16[128,2048]{1,0:T(8,128)(2,1)}, bf16[128,2048]{1,0:T(8,128)(2,1)S(1)}, u32[]{:S(2)}, u32[]{:S(2)}) collective-permute-start(bf16[128,2048]{1,0:T(8,128)(2,1)} %collective-permute-done.41.refs_5_), channel_id=1, source_target_pairs={{1,0},{5,4},{9,8},{13,12},{17,16},{21,20},{25,24},{29,28}} | collective-permute-start | bytes 1572872 | tf_op jit(solution)/shard_map/ppermute | solution.py:1046
  475.6 14.7 %collective-permute-start.48 = (f32[4352]{0:T(1024)S(1)}, f32[4352]{0:T(1024)S(1)}, u32[]{:S(2)}, u32[]{:S(2)}) collective-permute-start(f32[4352]{0:T(1024)S(1)} %add.274), channel_id=1, source_target_pairs={{0,1},{1,0},{2,3},{3,2},{4,5},{5,4},{6,7},{7,6},{8,9},{9,8},{10,11... | collective-permute-start | bytes 52232 | tf_op jit(solution)/shard_map/ppermute | solution.py:1226
  492.9 11.5 %collective-permute-start.49 = (bf16[128,2048]{1,0:T(8,128)(2,1)}, bf16[128,2048]{1,0:T(8,128)(2,1)S(1)}, u32[]{:S(2)}, u32[]{:S(2)}) collective-permute-start(bf16[128,2048]{1,0:T(8,128)(2,1)} %get-tuple-element.279), channel_id=1, source_target_pairs={{0,1},{1,2},{2,3},{4,5},{5,6},{6,7},{8,9},{9,10},{10,11},{12,13},{... | collective-permute-start | bytes 1572872 | tf_op jit(solution)/shard_map/ppermute | solution.py:1022
  494.3 13.9 %collective-permute-start.50 = (bf16[128,2048]{1,0:T(8,128)(2,1)}, bf16[128,2048]{1,0:T(8,128)(2,1)S(1)}, u32[]{:S(2)}, u32[]{:S(2)}) collective-permute-start(bf16[128,2048]{1,0:T(8,128)(2,1)} %get-tuple-element.278), channel_id=1, source_target_pairs={{1,0},{2,1},{3,2},{5,4},{6,5},{7,6},{9,8},{10,9},{11,10},{13,12},{... | collective-permute-start | bytes 1572872 | tf_op jit(solution)/shard_map/ppermute | solution.py:1023
  495.6 14.8 %collective-permute-start.51 = (f32[4352]{0:T(1024)S(1)}, f32[4352]{0:T(1024)S(1)}, u32[]{:S(2)}, u32[]{:S(2)}) collective-permute-start(f32[4352]{0:T(1024)S(1)} %add.278), channel_id=1, source_target_pairs={{0,2},{1,3},{2,0},{3,1},{4,6},{5,7},{6,4},{7,5},{8,10},{9,11},{10,... | collective-permute-start | bytes 52232 | tf_op jit(solution)/shard_map/ppermute | solution.py:1226
  513.5 14.6 %collective-permute-start.52 = (bf16[128,2048]{1,0:T(8,128)(2,1)}, bf16[128,2048]{1,0:T(8,128)(2,1)S(1)}, u32[]{:S(2)}, u32[]{:S(2)}) collective-permute-start(bf16[128,2048]{1,0:T(8,128)(2,1)} %fusion.15.refs_0_), channel_id=1, source_target_pairs={{0,1},{1,2},{2,3},{4,5},{5,6},{6,7},{8,9},{9,10},{10,11},{12,13},{... | collective-permute-start | bytes 1572872 | tf_op jit(solution)/shard_map/ppermute | solution.py:1045
  516.6 12.3 %collective-permute-start.53 = (bf16[128,2048]{1,0:T(8,128)(2,1)}, bf16[128,2048]{1,0:T(8,128)(2,1)S(1)}, u32[]{:S(2)}, u32[]{:S(2)}) collective-permute-start(bf16[128,2048]{1,0:T(8,128)(2,1)} %fusion.15.refs_0_), channel_id=1, source_target_pairs={{1,0},{2,1},{3,2},{5,4},{6,5},{7,6},{9,8},{10,9},{11,10},{13,12},{... | collective-permute-start | bytes 1572872 | tf_op jit(solution)/shard_map/ppermute | solution.py:1046
  529.6 14.0 %collective-permute-start.57 = (bf16[128,2048]{1,0:T(8,128)(2,1)S(1)}, bf16[128,2048]{1,0:T(8,128)(2,1)S(1)}, u32[]{:S(2)}, u32[]{:S(2)}) collective-permute-start(bf16[128,2048]{1,0:T(8,128)(2,1)S(1)} %collective-permute-done.53.refs_4_), channel_id=1, source_target_pairs={{1,0},{2,1},{5,4},{6,5},{9,8},{10,9},{13,12},{14,13},{17,16},{18,1... | collective-permute-start | bytes 1572872 | tf_op jit(solution)/shard_map/ppermute | solution.py:1046
  548.0 15.4 %collective-permute-start.60 = (bf16[128,2048]{1,0:T(8,128)(2,1)S(1)}, bf16[128,2048]{1,0:T(8,128)(2,1)S(1)}, u32[]{:S(2)}, u32[]{:S(2)}) collective-permute-start(bf16[128,2048]{1,0:T(8,128)(2,1)S(1)} %collective-permute-done.57.refs_5_), channel_id=1, source_target_pairs={{1,0},{5,4},{9,8},{13,12},{17,16},{21,20},{25,24},{29,28}} | collective-permute-start | bytes 1572872 | tf_op jit(solution)/shard_map/ppermute | solution.py:1046
  (56 other events, 483.0 us)
Sparse Core Ops, SparseCore 0:
  45.2 63.2 all-gather.2
  110.9 96.3 all-gather.4
  263.3 43.8 reduce-scatter.4
  310.5 90.1 reduce-scatter.6
  433.7 36.6 reduce-scatter.10
  473.3 75.1 reduce-scatter.8
